TPU v7x, 512 devices: a whole 4x8x8 slice. The times are simulated.
512 devices in a mesh: kring: 32 (over y, z_hi, core), kblk: 16 (over z_lo, x).
Axes of the slice: x: 4, y: 8, z: 8 (z_hi: 2, z_lo: 4; z = z_hi * 4 + z_lo), core: 2. Of those that a mesh axis runs over, the one named last changes fastest.
Arguments:
- elem_x: bfloat16 [32, 16, 128, 1024], P('kring', 'kblk'), may hold values from -6 to 6
- elem_d: bfloat16 [32, 16, 128, 512], P('kring', 'kblk'), may hold values from -6 to 6
- rows_x: bfloat16 [32, 16, 128, 1024], P('kring', 'kblk'), may hold values from -0.1875 to 0.1875
- rows_d: bfloat16 [32, 16, 128, 512], P('kring', 'kblk'), may hold values from -0.25 to 0.25
- coulomb: float32 [1024], replicated, may hold values from 0.2 to 2
- screened: float32 [512], replicated, may hold values from 0.1 to 1
- cutoff: int32 [32, 16, 32], P('kring', 'kblk'), may hold values from 256 to 1024
- owners: int32 [32, 16, 32, 1], P('kring', 'kblk'), may hold values from 0 to 15; in each aligned block of 32 rows (0 to 31, 32 to 63, ..., all dimensions but the last counted through in order) at most 4 rows name the same one
Outputs:
- assembled: bfloat16 [32, 16, 16, 4, 128, 128], P('kring', 'kblk')
Inputs may be any that keep to these rules, and one draw needn't show every extreme that they name: `owners`: among the 32 entries of one (i, j), no owner appears more than 4 times, and some owner appears exactly 4 times.
All inputs are finite; a program needn't handle non-finite values.
Results may differ from a plain program's by a relative error of at most 0.0049.
Values may be sent and summed in bfloat16 or wider, within the bound.
No kernel may reach another device: no remote copies, remote signals or barrier semaphores. Data moves between devices by JAX's collectives and lax.ppermute only.
A program may use at most 64 MiB of HBM per device.

v0:
```python
import jax
import jax.numpy as jnp
from jax import lax
from jax.sharding import PartitionSpec as P

CAP = 4


def from_behind(x, axis, by):
    peers = lax.axis_size(axis)
    return lax.ppermute(x, axis, [(i, (i + by) % peers) for i in range(peers)])


def body(elem_x, elem_d, rows_x, rows_d, coulomb, screened, cutoff, owners):
    cycle_len = lax.axis_size("kring")
    cycle_pos = lax.axis_index("kring")
    blk_len = lax.axis_size("kblk")
    tile_rows = elem_x.shape[2]
    g_count = elem_x.shape[3]
    scaled_x = (elem_x[0, 0].astype(jnp.float32) * coulomb).astype(jnp.bfloat16)
    scaled_d = (elem_d[0, 0].astype(jnp.float32) * screened).astype(jnp.bfloat16)
    cut_row = cutoff[0, 0]
    g_index = jnp.arange(g_count, dtype=jnp.int32)
    contract = (((1,), (1,)), ((), ()))

    def make_tile(part_x, part_d, partner):
        limit_g = cut_row[partner]
        dir_part = lax.dot_general(scaled_d, part_d, contract, preferred_element_type=jnp.float32)
        masked = jnp.where((g_index < limit_g)[None, :], part_x, jnp.zeros_like(part_x))
        exch_part = lax.dot_general(scaled_x, masked, contract, preferred_element_type=jnp.float32)
        return (2.0 * exch_part - dir_part).astype(jnp.bfloat16)

    empty_set = jnp.zeros((cycle_len, tile_rows, tile_rows), jnp.bfloat16)

    def store(tile_set, tile_new, partner):
        return lax.dynamic_update_slice_in_dim(tile_set, tile_new[None], partner, 0)

    def cycle_step(step, carry):
        tile_set, cur_x, cur_d = carry
        partner = (cycle_pos - step) % cycle_len
        tile_set = store(tile_set, make_tile(cur_x[0, 0], cur_d[0, 0], partner), partner)
        cur_x, cur_d = from_behind((cur_x, cur_d), "kring", 1)
        return (tile_set, cur_x, cur_d)

    tile_set, cur_x, cur_d = lax.fori_loop(
        0, cycle_len - 1, cycle_step, (empty_set, rows_x, rows_d)
    )
    partner = (cycle_pos + 1) % cycle_len
    tile_set = store(tile_set, make_tile(cur_x[0, 0], cur_d[0, 0], partner), partner)
    dest = owners[0, 0, :, 0]
    onehot = (dest[:, None] == jnp.arange(blk_len, dtype=jnp.int32)[None, :]).astype(jnp.int32)
    before = jnp.cumsum(onehot, axis=0) - onehot
    slot_of = jnp.sum(before * onehot, axis=1)
    outbox = jnp.zeros((blk_len, CAP, tile_rows, tile_rows), jnp.bfloat16)
    outbox = outbox.at[dest, slot_of].set(tile_set)
    received = lax.all_to_all(outbox, "kblk", split_axis=0, concat_axis=0, tiled=True)
    return received[None, None]


def solution(mesh):
    in_specs = (
        P("kring", "kblk", None, None),
        P("kring", "kblk", None, None),
        P("kring", "kblk", None, None),
        P("kring", "kblk", None, None),
        P(),
        P(),
        P("kring", "kblk", None),
        P("kring", "kblk", None, None),
    )
    out_specs = P("kring", "kblk", None, None, None, None)
    return jax.shard_map(body, mesh=mesh, in_specs=in_specs, out_specs=out_specs, check_vma=False)
```

profile of v0, /device:TPU:1, one launch (start us, length us, event | category | flops | bytes accessed | tf_op | source)
XLA Modules:
  0.0 606.6 jit_solution(17696126308410073138)
XLA Ops:
  6.5 529.9 %while.20 = (s32[]{:T(128)}, bf16[32,128,128]{2,1,0:T(8,128)(2,1)S(1)}, bf16[1,1,128,1024]{3,2,1,0:T(8,128)(2,1)S(1)}, bf16[1,1,128,512]{3,2,1,0:T(8,128)(2,1)S(...) while((s32[]{:T(128)}, ...), condition=%wide.region_3.4_spmd.clone, body=%wide.region_2.3_spmd.clone.sunk | while | flops 50512912 | bytes 3443060 | solution.py:45
  6.5 12.2 %collective-permute-start.1 = (bf16[1,1,128,512]{3,2,1,0:T(8,128)(2,1)S(1)}, bf16[1,1,128,512]{3,2,1,0:T(8,128)(2,1)S(1)}, u32[]{:S(2)}, u32[]{:S(2)}) collective-permute-start(bf16[1,1,128,512]{3,2,1,0:T(8,128)(2,1)S(1)} %copy.24), channel_id=1, source_target_pairs={{0,16},{16,32},{32,48},{48,64},{64,80},{80,96},{96,112},{112,128},... | collective-permute-start | bytes 393224 | tf_op jit(solution)/shard_map/while/body/eval_jaxpr/ppermute | solution.py:11
  27.9 8.4 %collective-permute-start.1 = (bf16[1,1,128,512]{3,2,1,0:T(8,128)(2,1)S(1)}, bf16[1,1,128,512]{3,2,1,0:T(8,128)(2,1)S(1)}, u32[]{:S(2)}, u32[]{:S(2)}) collective-permute-start(bf16[1,1,128,512]{3,2,1,0:T(8,128)(2,1)S(1)} %copy.24), channel_id=1, source_target_pairs={{0,16},{16,32},{32,48},{48,64},{64,80},{80,96},{96,112},{112,128},... | collective-permute-start | bytes 393224 | tf_op jit(solution)/shard_map/while/body/eval_jaxpr/ppermute | solution.py:11
  45.3 8.4 %collective-permute-start.1 = (bf16[1,1,128,512]{3,2,1,0:T(8,128)(2,1)S(1)}, bf16[1,1,128,512]{3,2,1,0:T(8,128)(2,1)S(1)}, u32[]{:S(2)}, u32[]{:S(2)}) collective-permute-start(bf16[1,1,128,512]{3,2,1,0:T(8,128)(2,1)S(1)} %copy.24), channel_id=1, source_target_pairs={{0,16},{16,32},{32,48},{48,64},{64,80},{80,96},{96,112},{112,128},... | collective-permute-start | bytes 393224 | tf_op jit(solution)/shard_map/while/body/eval_jaxpr/ppermute | solution.py:11
  62.2 8.6 %collective-permute-start.1 = (bf16[1,1,128,512]{3,2,1,0:T(8,128)(2,1)S(1)}, bf16[1,1,128,512]{3,2,1,0:T(8,128)(2,1)S(1)}, u32[]{:S(2)}, u32[]{:S(2)}) collective-permute-start(bf16[1,1,128,512]{3,2,1,0:T(8,128)(2,1)S(1)} %copy.24), channel_id=1, source_target_pairs={{0,16},{16,32},{32,48},{48,64},{64,80},{80,96},{96,112},{112,128},... | collective-permute-start | bytes 393224 | tf_op jit(solution)/shard_map/while/body/eval_jaxpr/ppermute | solution.py:11
  79.6 8.5 %collective-permute-start.1 = (bf16[1,1,128,512]{3,2,1,0:T(8,128)(2,1)S(1)}, bf16[1,1,128,512]{3,2,1,0:T(8,128)(2,1)S(1)}, u32[]{:S(2)}, u32[]{:S(2)}) collective-permute-start(bf16[1,1,128,512]{3,2,1,0:T(8,128)(2,1)S(1)} %copy.24), channel_id=1, source_target_pairs={{0,16},{16,32},{32,48},{48,64},{64,80},{80,96},{96,112},{112,128},... | collective-permute-start | bytes 393224 | tf_op jit(solution)/shard_map/while/body/eval_jaxpr/ppermute | solution.py:11
  97.6 8.3 %collective-permute-start.1 = (bf16[1,1,128,512]{3,2,1,0:T(8,128)(2,1)S(1)}, bf16[1,1,128,512]{3,2,1,0:T(8,128)(2,1)S(1)}, u32[]{:S(2)}, u32[]{:S(2)}) collective-permute-start(bf16[1,1,128,512]{3,2,1,0:T(8,128)(2,1)S(1)} %copy.24), channel_id=1, source_target_pairs={{0,16},{16,32},{32,48},{48,64},{64,80},{80,96},{96,112},{112,128},... | collective-permute-start | bytes 393224 | tf_op jit(solution)/shard_map/while/body/eval_jaxpr/ppermute | solution.py:11
  114.8 8.8 %collective-permute-start.1 = (bf16[1,1,128,512]{3,2,1,0:T(8,128)(2,1)S(1)}, bf16[1,1,128,512]{3,2,1,0:T(8,128)(2,1)S(1)}, u32[]{:S(2)}, u32[]{:S(2)}) collective-permute-start(bf16[1,1,128,512]{3,2,1,0:T(8,128)(2,1)S(1)} %copy.24), channel_id=1, source_target_pairs={{0,16},{16,32},{32,48},{48,64},{64,80},{80,96},{96,112},{112,128},... | collective-permute-start | bytes 393224 | tf_op jit(solution)/shard_map/while/body/eval_jaxpr/ppermute | solution.py:11
  131.9 8.4 %collective-permute-start.1 = (bf16[1,1,128,512]{3,2,1,0:T(8,128)(2,1)S(1)}, bf16[1,1,128,512]{3,2,1,0:T(8,128)(2,1)S(1)}, u32[]{:S(2)}, u32[]{:S(2)}) collective-permute-start(bf16[1,1,128,512]{3,2,1,0:T(8,128)(2,1)S(1)} %copy.24), channel_id=1, source_target_pairs={{0,16},{16,32},{32,48},{48,64},{64,80},{80,96},{96,112},{112,128},... | collective-permute-start | bytes 393224 | tf_op jit(solution)/shard_map/while/body/eval_jaxpr/ppermute | solution.py:11
  147.8 8.4 %collective-permute-start.1 = (bf16[1,1,128,512]{3,2,1,0:T(8,128)(2,1)S(1)}, bf16[1,1,128,512]{3,2,1,0:T(8,128)(2,1)S(1)}, u32[]{:S(2)}, u32[]{:S(2)}) collective-permute-start(bf16[1,1,128,512]{3,2,1,0:T(8,128)(2,1)S(1)} %copy.24), channel_id=1, source_target_pairs={{0,16},{16,32},{32,48},{48,64},{64,80},{80,96},{96,112},{112,128},... | collective-permute-start | bytes 393224 | tf_op jit(solution)/shard_map/while/body/eval_jaxpr/ppermute | solution.py:11
  161.5 8.4 %collective-permute-start.1 = (bf16[1,1,128,512]{3,2,1,0:T(8,128)(2,1)S(1)}, bf16[1,1,128,512]{3,2,1,0:T(8,128)(2,1)S(1)}, u32[]{:S(2)}, u32[]{:S(2)}) collective-permute-start(bf16[1,1,128,512]{3,2,1,0:T(8,128)(2,1)S(1)} %copy.24), channel_id=1, source_target_pairs={{0,16},{16,32},{32,48},{48,64},{64,80},{80,96},{96,112},{112,128},... | collective-permute-start | bytes 393224 | tf_op jit(solution)/shard_map/while/body/eval_jaxpr/ppermute | solution.py:11
  246.8 8.3 %collective-permute-start.1 = (bf16[1,1,128,512]{3,2,1,0:T(8,128)(2,1)S(1)}, bf16[1,1,128,512]{3,2,1,0:T(8,128)(2,1)S(1)}, u32[]{:S(2)}, u32[]{:S(2)}) collective-permute-start(bf16[1,1,128,512]{3,2,1,0:T(8,128)(2,1)S(1)} %copy.24), channel_id=1, source_target_pairs={{0,16},{16,32},{32,48},{48,64},{64,80},{80,96},{96,112},{112,128},... | collective-permute-start | bytes 393224 | tf_op jit(solution)/shard_map/while/body/eval_jaxpr/ppermute | solution.py:11
  263.9 8.3 %collective-permute-start.1 = (bf16[1,1,128,512]{3,2,1,0:T(8,128)(2,1)S(1)}, bf16[1,1,128,512]{3,2,1,0:T(8,128)(2,1)S(1)}, u32[]{:S(2)}, u32[]{:S(2)}) collective-permute-start(bf16[1,1,128,512]{3,2,1,0:T(8,128)(2,1)S(1)} %copy.24), channel_id=1, source_target_pairs={{0,16},{16,32},{32,48},{48,64},{64,80},{80,96},{96,112},{112,128},... | collective-permute-start | bytes 393224 | tf_op jit(solution)/shard_map/while/body/eval_jaxpr/ppermute | solution.py:11
  279.8 8.3 %collective-permute-start.1 = (bf16[1,1,128,512]{3,2,1,0:T(8,128)(2,1)S(1)}, bf16[1,1,128,512]{3,2,1,0:T(8,128)(2,1)S(1)}, u32[]{:S(2)}, u32[]{:S(2)}) collective-permute-start(bf16[1,1,128,512]{3,2,1,0:T(8,128)(2,1)S(1)} %copy.24), channel_id=1, source_target_pairs={{0,16},{16,32},{32,48},{48,64},{64,80},{80,96},{96,112},{112,128},... | collective-permute-start | bytes 393224 | tf_op jit(solution)/shard_map/while/body/eval_jaxpr/ppermute | solution.py:11
  330.2 8.3 %collective-permute-start.1 = (bf16[1,1,128,512]{3,2,1,0:T(8,128)(2,1)S(1)}, bf16[1,1,128,512]{3,2,1,0:T(8,128)(2,1)S(1)}, u32[]{:S(2)}, u32[]{:S(2)}) collective-permute-start(bf16[1,1,128,512]{3,2,1,0:T(8,128)(2,1)S(1)} %copy.24), channel_id=1, source_target_pairs={{0,16},{16,32},{32,48},{48,64},{64,80},{80,96},{96,112},{112,128},... | collective-permute-start | bytes 393224 | tf_op jit(solution)/shard_map/while/body/eval_jaxpr/ppermute | solution.py:11
  346.4 8.8 %collective-permute-start.1 = (bf16[1,1,128,512]{3,2,1,0:T(8,128)(2,1)S(1)}, bf16[1,1,128,512]{3,2,1,0:T(8,128)(2,1)S(1)}, u32[]{:S(2)}, u32[]{:S(2)}) collective-permute-start(bf16[1,1,128,512]{3,2,1,0:T(8,128)(2,1)S(1)} %copy.24), channel_id=1, source_target_pairs={{0,16},{16,32},{32,48},{48,64},{64,80},{80,96},{96,112},{112,128},... | collective-permute-start | bytes 393224 | tf_op jit(solution)/shard_map/while/body/eval_jaxpr/ppermute | solution.py:11
  363.2 8.5 %collective-permute-start.1 = (bf16[1,1,128,512]{3,2,1,0:T(8,128)(2,1)S(1)}, bf16[1,1,128,512]{3,2,1,0:T(8,128)(2,1)S(1)}, u32[]{:S(2)}, u32[]{:S(2)}) collective-permute-start(bf16[1,1,128,512]{3,2,1,0:T(8,128)(2,1)S(1)} %copy.24), channel_id=1, source_target_pairs={{0,16},{16,32},{32,48},{48,64},{64,80},{80,96},{96,112},{112,128},... | collective-permute-start | bytes 393224 | tf_op jit(solution)/shard_map/while/body/eval_jaxpr/ppermute | solution.py:11
  380.5 8.7 %collective-permute-start.1 = (bf16[1,1,128,512]{3,2,1,0:T(8,128)(2,1)S(1)}, bf16[1,1,128,512]{3,2,1,0:T(8,128)(2,1)S(1)}, u32[]{:S(2)}, u32[]{:S(2)}) collective-permute-start(bf16[1,1,128,512]{3,2,1,0:T(8,128)(2,1)S(1)} %copy.24), channel_id=1, source_target_pairs={{0,16},{16,32},{32,48},{48,64},{64,80},{80,96},{96,112},{112,128},... | collective-permute-start | bytes 393224 | tf_op jit(solution)/shard_map/while/body/eval_jaxpr/ppermute | solution.py:11
  396.6 9.2 %collective-permute-start.1 = (bf16[1,1,128,512]{3,2,1,0:T(8,128)(2,1)S(1)}, bf16[1,1,128,512]{3,2,1,0:T(8,128)(2,1)S(1)}, u32[]{:S(2)}, u32[]{:S(2)}) collective-permute-start(bf16[1,1,128,512]{3,2,1,0:T(8,128)(2,1)S(1)} %copy.24), channel_id=1, source_target_pairs={{0,16},{16,32},{32,48},{48,64},{64,80},{80,96},{96,112},{112,128},... | collective-permute-start | bytes 393224 | tf_op jit(solution)/shard_map/while/body/eval_jaxpr/ppermute | solution.py:11
  414.2 8.9 %collective-permute-start.1 = (bf16[1,1,128,512]{3,2,1,0:T(8,128)(2,1)S(1)}, bf16[1,1,128,512]{3,2,1,0:T(8,128)(2,1)S(1)}, u32[]{:S(2)}, u32[]{:S(2)}) collective-permute-start(bf16[1,1,128,512]{3,2,1,0:T(8,128)(2,1)S(1)} %copy.24), channel_id=1, source_target_pairs={{0,16},{16,32},{32,48},{48,64},{64,80},{80,96},{96,112},{112,128},... | collective-permute-start | bytes 393224 | tf_op jit(solution)/shard_map/while/body/eval_jaxpr/ppermute | solution.py:11
  431.2 8.8 %collective-permute-start.1 = (bf16[1,1,128,512]{3,2,1,0:T(8,128)(2,1)S(1)}, bf16[1,1,128,512]{3,2,1,0:T(8,128)(2,1)S(1)}, u32[]{:S(2)}, u32[]{:S(2)}) collective-permute-start(bf16[1,1,128,512]{3,2,1,0:T(8,128)(2,1)S(1)} %copy.24), channel_id=1, source_target_pairs={{0,16},{16,32},{32,48},{48,64},{64,80},{80,96},{96,112},{112,128},... | collective-permute-start | bytes 393224 | tf_op jit(solution)/shard_map/while/body/eval_jaxpr/ppermute | solution.py:11
  448.6 8.6 %collective-permute-start.1 = (bf16[1,1,128,512]{3,2,1,0:T(8,128)(2,1)S(1)}, bf16[1,1,128,512]{3,2,1,0:T(8,128)(2,1)S(1)}, u32[]{:S(2)}, u32[]{:S(2)}) collective-permute-start(bf16[1,1,128,512]{3,2,1,0:T(8,128)(2,1)S(1)} %copy.24), channel_id=1, source_target_pairs={{0,16},{16,32},{32,48},{48,64},{64,80},{80,96},{96,112},{112,128},... | collective-permute-start | bytes 393224 | tf_op jit(solution)/shard_map/while/body/eval_jaxpr/ppermute | solution.py:11
  466.1 8.3 %collective-permute-start.1 = (bf16[1,1,128,512]{3,2,1,0:T(8,128)(2,1)S(1)}, bf16[1,1,128,512]{3,2,1,0:T(8,128)(2,1)S(1)}, u32[]{:S(2)}, u32[]{:S(2)}) collective-permute-start(bf16[1,1,128,512]{3,2,1,0:T(8,128)(2,1)S(1)} %copy.24), channel_id=1, source_target_pairs={{0,16},{16,32},{32,48},{48,64},{64,80},{80,96},{96,112},{112,128},... | collective-permute-start | bytes 393224 | tf_op jit(solution)/shard_map/while/body/eval_jaxpr/ppermute | solution.py:11
  539.5 65.8 %all_to_all.5 = bf16[16,4,128,128]{3,2,1,0:T(8,128)(2,1)S(1)} all-to-all(bf16[16,4,128,128]{3,2,1,0:T(8,128)(2,1)S(1)} %scatter_fusion), channel_id=1, replica_groups=mesh['kring'=32,'kblk'=16] {'kblk'}, dimensions={0} | all-to-all | bytes 4194304 | tf_op jit(solution)/shard_map/all_to_all | solution.py:56
  (378 shorter events, 346.5 us)
Async XLA Ops:
  6.5 15.9 %collective-permute-start.1 = (bf16[1,1,128,512]{3,2,1,0:T(8,128)(2,1)S(1)}, bf16[1,1,128,512]{3,2,1,0:T(8,128)(2,1)S(1)}, u32[]{:S(2)}, u32[]{:S(2)}) collective-permute-start(bf16[1,1,128,512]{3,2,1,0:T(8,128)(2,1)S(1)} %copy.24), channel_id=1, source_target_pairs={{0,16},{16,32},{32,48},{48,64},{64,80},{80,96},{96,112},{112,128},... | collective-permute-start | bytes 393224 | tf_op jit(solution)/shard_map/while/body/eval_jaxpr/ppermute | solution.py:11
  114.8 14.2 %collective-permute-start.1 = (bf16[1,1,128,512]{3,2,1,0:T(8,128)(2,1)S(1)}, bf16[1,1,128,512]{3,2,1,0:T(8,128)(2,1)S(1)}, u32[]{:S(2)}, u32[]{:S(2)}) collective-permute-start(bf16[1,1,128,512]{3,2,1,0:T(8,128)(2,1)S(1)} %copy.24), channel_id=1, source_target_pairs={{0,16},{16,32},{32,48},{48,64},{64,80},{80,96},{96,112},{112,128},... | collective-permute-start | bytes 393224 | tf_op jit(solution)/shard_map/while/body/eval_jaxpr/ppermute | solution.py:11
  161.5 15.3 %collective-permute-start.1 = (bf16[1,1,128,512]{3,2,1,0:T(8,128)(2,1)S(1)}, bf16[1,1,128,512]{3,2,1,0:T(8,128)(2,1)S(1)}, u32[]{:S(2)}, u32[]{:S(2)}) collective-permute-start(bf16[1,1,128,512]{3,2,1,0:T(8,128)(2,1)S(1)} %copy.24), channel_id=1, source_target_pairs={{0,16},{16,32},{32,48},{48,64},{64,80},{80,96},{96,112},{112,128},... | collective-permute-start | bytes 393224 | tf_op jit(solution)/shard_map/while/body/eval_jaxpr/ppermute | solution.py:11
  178.9 15.8 %collective-permute-start.1 = (bf16[1,1,128,512]{3,2,1,0:T(8,128)(2,1)S(1)}, bf16[1,1,128,512]{3,2,1,0:T(8,128)(2,1)S(1)}, u32[]{:S(2)}, u32[]{:S(2)}) collective-permute-start(bf16[1,1,128,512]{3,2,1,0:T(8,128)(2,1)S(1)} %copy.24), channel_id=1, source_target_pairs={{0,16},{16,32},{32,48},{48,64},{64,80},{80,96},{96,112},{112,128},... | collective-permute-start | bytes 393224 | tf_op jit(solution)/shard_map/while/body/eval_jaxpr/ppermute | solution.py:11
  196.9 14.5 %collective-permute-start.1 = (bf16[1,1,128,512]{3,2,1,0:T(8,128)(2,1)S(1)}, bf16[1,1,128,512]{3,2,1,0:T(8,128)(2,1)S(1)}, u32[]{:S(2)}, u32[]{:S(2)}) collective-permute-start(bf16[1,1,128,512]{3,2,1,0:T(8,128)(2,1)S(1)} %copy.24), channel_id=1, source_target_pairs={{0,16},{16,32},{32,48},{48,64},{64,80},{80,96},{96,112},{112,128},... | collective-permute-start | bytes 393224 | tf_op jit(solution)/shard_map/while/body/eval_jaxpr/ppermute | solution.py:11
  199.2 14.4 %collective-permute-start = (bf16[1,1,128,1024]{3,2,1,0:T(8,128)(2,1)S(1)}, bf16[1,1,128,1024]{3,2,1,0:T(8,128)(2,1)S(1)}, u32[]{:S(2)}, u32[]{:S(2)}) collective-permute-start(bf16[1,1,128,1024]{3,2,1,0:T(8,128)(2,1)S(1)} %copy.23), channel_id=1, source_target_pairs={{0,16},{16,32},{32,48},{48,64},{64,80},{80,96},{96,112},{112,128},... | collective-permute-start | bytes 786440 | tf_op jit(solution)/shard_map/while/body/eval_jaxpr/ppermute | solution.py:11
  213.6 13.5 %collective-permute-start.1 = (bf16[1,1,128,512]{3,2,1,0:T(8,128)(2,1)S(1)}, bf16[1,1,128,512]{3,2,1,0:T(8,128)(2,1)S(1)}, u32[]{:S(2)}, u32[]{:S(2)}) collective-permute-start(bf16[1,1,128,512]{3,2,1,0:T(8,128)(2,1)S(1)} %copy.24), channel_id=1, source_target_pairs={{0,16},{16,32},{32,48},{48,64},{64,80},{80,96},{96,112},{112,128},... | collective-permute-start | bytes 393224 | tf_op jit(solution)/shard_map/while/body/eval_jaxpr/ppermute | solution.py:11
  229.3 13.5 %collective-permute-start.1 = (bf16[1,1,128,512]{3,2,1,0:T(8,128)(2,1)S(1)}, bf16[1,1,128,512]{3,2,1,0:T(8,128)(2,1)S(1)}, u32[]{:S(2)}, u32[]{:S(2)}) collective-permute-start(bf16[1,1,128,512]{3,2,1,0:T(8,128)(2,1)S(1)} %copy.24), channel_id=1, source_target_pairs={{0,16},{16,32},{32,48},{48,64},{64,80},{80,96},{96,112},{112,128},... | collective-permute-start | bytes 393224 | tf_op jit(solution)/shard_map/while/body/eval_jaxpr/ppermute | solution.py:11
  246.8 14.4 %collective-permute-start.1 = (bf16[1,1,128,512]{3,2,1,0:T(8,128)(2,1)S(1)}, bf16[1,1,128,512]{3,2,1,0:T(8,128)(2,1)S(1)}, u32[]{:S(2)}, u32[]{:S(2)}) collective-permute-start(bf16[1,1,128,512]{3,2,1,0:T(8,128)(2,1)S(1)} %copy.24), channel_id=1, source_target_pairs={{0,16},{16,32},{32,48},{48,64},{64,80},{80,96},{96,112},{112,128},... | collective-permute-start | bytes 393224 | tf_op jit(solution)/shard_map/while/body/eval_jaxpr/ppermute | solution.py:11
  279.8 15.3 %collective-permute-start.1 = (bf16[1,1,128,512]{3,2,1,0:T(8,128)(2,1)S(1)}, bf16[1,1,128,512]{3,2,1,0:T(8,128)(2,1)S(1)}, u32[]{:S(2)}, u32[]{:S(2)}) collective-permute-start(bf16[1,1,128,512]{3,2,1,0:T(8,128)(2,1)S(1)} %copy.24), channel_id=1, source_target_pairs={{0,16},{16,32},{32,48},{48,64},{64,80},{80,96},{96,112},{112,128},... | collective-permute-start | bytes 393224 | tf_op jit(solution)/shard_map/while/body/eval_jaxpr/ppermute | solution.py:11
  296.5 15.3 %collective-permute-start.1 = (bf16[1,1,128,512]{3,2,1,0:T(8,128)(2,1)S(1)}, bf16[1,1,128,512]{3,2,1,0:T(8,128)(2,1)S(1)}, u32[]{:S(2)}, u32[]{:S(2)}) collective-permute-start(bf16[1,1,128,512]{3,2,1,0:T(8,128)(2,1)S(1)} %copy.24), channel_id=1, source_target_pairs={{0,16},{16,32},{32,48},{48,64},{64,80},{80,96},{96,112},{112,128},... | collective-permute-start | bytes 393224 | tf_op jit(solution)/shard_map/while/body/eval_jaxpr/ppermute | solution.py:11
  313.3 15.5 %collective-permute-start.1 = (bf16[1,1,128,512]{3,2,1,0:T(8,128)(2,1)S(1)}, bf16[1,1,128,512]{3,2,1,0:T(8,128)(2,1)S(1)}, u32[]{:S(2)}, u32[]{:S(2)}) collective-permute-start(bf16[1,1,128,512]{3,2,1,0:T(8,128)(2,1)S(1)} %copy.24), channel_id=1, source_target_pairs={{0,16},{16,32},{32,48},{48,64},{64,80},{80,96},{96,112},{112,128},... | collective-permute-start | bytes 393224 | tf_op jit(solution)/shard_map/while/body/eval_jaxpr/ppermute | solution.py:11
  330.2 14.7 %collective-permute-start.1 = (bf16[1,1,128,512]{3,2,1,0:T(8,128)(2,1)S(1)}, bf16[1,1,128,512]{3,2,1,0:T(8,128)(2,1)S(1)}, u32[]{:S(2)}, u32[]{:S(2)}) collective-permute-start(bf16[1,1,128,512]{3,2,1,0:T(8,128)(2,1)S(1)} %copy.24), channel_id=1, source_target_pairs={{0,16},{16,32},{32,48},{48,64},{64,80},{80,96},{96,112},{112,128},... | collective-permute-start | bytes 393224 | tf_op jit(solution)/shard_map/while/body/eval_jaxpr/ppermute | solution.py:11
  346.4 15.3 %collective-permute-start.1 = (bf16[1,1,128,512]{3,2,1,0:T(8,128)(2,1)S(1)}, bf16[1,1,128,512]{3,2,1,0:T(8,128)(2,1)S(1)}, u32[]{:S(2)}, u32[]{:S(2)}) collective-permute-start(bf16[1,1,128,512]{3,2,1,0:T(8,128)(2,1)S(1)} %copy.24), channel_id=1, source_target_pairs={{0,16},{16,32},{32,48},{48,64},{64,80},{80,96},{96,112},{112,128},... | collective-permute-start | bytes 393224 | tf_op jit(solution)/shard_map/while/body/eval_jaxpr/ppermute | solution.py:11
  363.2 15.8 %collective-permute-start.1 = (bf16[1,1,128,512]{3,2,1,0:T(8,128)(2,1)S(1)}, bf16[1,1,128,512]{3,2,1,0:T(8,128)(2,1)S(1)}, u32[]{:S(2)}, u32[]{:S(2)}) collective-permute-start(bf16[1,1,128,512]{3,2,1,0:T(8,128)(2,1)S(1)} %copy.24), channel_id=1, source_target_pairs={{0,16},{16,32},{32,48},{48,64},{64,80},{80,96},{96,112},{112,128},... | collective-permute-start | bytes 393224 | tf_op jit(solution)/shard_map/while/body/eval_jaxpr/ppermute | solution.py:11
  380.5 14.6 %collective-permute-start.1 = (bf16[1,1,128,512]{3,2,1,0:T(8,128)(2,1)S(1)}, bf16[1,1,128,512]{3,2,1,0:T(8,128)(2,1)S(1)}, u32[]{:S(2)}, u32[]{:S(2)}) collective-permute-start(bf16[1,1,128,512]{3,2,1,0:T(8,128)(2,1)S(1)} %copy.24), channel_id=1, source_target_pairs={{0,16},{16,32},{32,48},{48,64},{64,80},{80,96},{96,112},{112,128},... | collective-permute-start | bytes 393224 | tf_op jit(solution)/shard_map/while/body/eval_jaxpr/ppermute | solution.py:11
  396.6 16.1 %collective-permute-start.1 = (bf16[1,1,128,512]{3,2,1,0:T(8,128)(2,1)S(1)}, bf16[1,1,128,512]{3,2,1,0:T(8,128)(2,1)S(1)}, u32[]{:S(2)}, u32[]{:S(2)}) collective-permute-start(bf16[1,1,128,512]{3,2,1,0:T(8,128)(2,1)S(1)} %copy.24), channel_id=1, source_target_pairs={{0,16},{16,32},{32,48},{48,64},{64,80},{80,96},{96,112},{112,128},... | collective-permute-start | bytes 393224 | tf_op jit(solution)/shard_map/while/body/eval_jaxpr/ppermute | solution.py:11
  414.2 15.5 %collective-permute-start.1 = (bf16[1,1,128,512]{3,2,1,0:T(8,128)(2,1)S(1)}, bf16[1,1,128,512]{3,2,1,0:T(8,128)(2,1)S(1)}, u32[]{:S(2)}, u32[]{:S(2)}) collective-permute-start(bf16[1,1,128,512]{3,2,1,0:T(8,128)(2,1)S(1)} %copy.24), channel_id=1, source_target_pairs={{0,16},{16,32},{32,48},{48,64},{64,80},{80,96},{96,112},{112,128},... | collective-permute-start | bytes 393224 | tf_op jit(solution)/shard_map/while/body/eval_jaxpr/ppermute | solution.py:11
  431.2 15.9 %collective-permute-start.1 = (bf16[1,1,128,512]{3,2,1,0:T(8,128)(2,1)S(1)}, bf16[1,1,128,512]{3,2,1,0:T(8,128)(2,1)S(1)}, u32[]{:S(2)}, u32[]{:S(2)}) collective-permute-start(bf16[1,1,128,512]{3,2,1,0:T(8,128)(2,1)S(1)} %copy.24), channel_id=1, source_target_pairs={{0,16},{16,32},{32,48},{48,64},{64,80},{80,96},{96,112},{112,128},... | collective-permute-start | bytes 393224 | tf_op jit(solution)/shard_map/while/body/eval_jaxpr/ppermute | solution.py:11
  448.6 15.9 %collective-permute-start.1 = (bf16[1,1,128,512]{3,2,1,0:T(8,128)(2,1)S(1)}, bf16[1,1,128,512]{3,2,1,0:T(8,128)(2,1)S(1)}, u32[]{:S(2)}, u32[]{:S(2)}) collective-permute-start(bf16[1,1,128,512]{3,2,1,0:T(8,128)(2,1)S(1)} %copy.24), channel_id=1, source_target_pairs={{0,16},{16,32},{32,48},{48,64},{64,80},{80,96},{96,112},{112,128},... | collective-permute-start | bytes 393224 | tf_op jit(solution)/shard_map/while/body/eval_jaxpr/ppermute | solution.py:11
  466.1 16.0 %collective-permute-start.1 = (bf16[1,1,128,512]{3,2,1,0:T(8,128)(2,1)S(1)}, bf16[1,1,128,512]{3,2,1,0:T(8,128)(2,1)S(1)}, u32[]{:S(2)}, u32[]{:S(2)}) collective-permute-start(bf16[1,1,128,512]{3,2,1,0:T(8,128)(2,1)S(1)} %copy.24), channel_id=1, source_target_pairs={{0,16},{16,32},{32,48},{48,64},{64,80},{80,96},{96,112},{112,128},... | collective-permute-start | bytes 393224 | tf_op jit(solution)/shard_map/while/body/eval_jaxpr/ppermute | solution.py:11
  483.5 16.0 %collective-permute-start.1 = (bf16[1,1,128,512]{3,2,1,0:T(8,128)(2,1)S(1)}, bf16[1,1,128,512]{3,2,1,0:T(8,128)(2,1)S(1)}, u32[]{:S(2)}, u32[]{:S(2)}) collective-permute-start(bf16[1,1,128,512]{3,2,1,0:T(8,128)(2,1)S(1)} %copy.24), channel_id=1, source_target_pairs={{0,16},{16,32},{32,48},{48,64},{64,80},{80,96},{96,112},{112,128},... | collective-permute-start | bytes 393224 | tf_op jit(solution)/shard_map/while/body/eval_jaxpr/ppermute | solution.py:11
  501.1 16.2 %collective-permute-start.1 = (bf16[1,1,128,512]{3,2,1,0:T(8,128)(2,1)S(1)}, bf16[1,1,128,512]{3,2,1,0:T(8,128)(2,1)S(1)}, u32[]{:S(2)}, u32[]{:S(2)}) collective-permute-start(bf16[1,1,128,512]{3,2,1,0:T(8,128)(2,1)S(1)} %copy.24), channel_id=1, source_target_pairs={{0,16},{16,32},{32,48},{48,64},{64,80},{80,96},{96,112},{112,128},... | collective-permute-start | bytes 393224 | tf_op jit(solution)/shard_map/while/body/eval_jaxpr/ppermute | solution.py:11
  518.7 16.2 %collective-permute-start.1 = (bf16[1,1,128,512]{3,2,1,0:T(8,128)(2,1)S(1)}, bf16[1,1,128,512]{3,2,1,0:T(8,128)(2,1)S(1)}, u32[]{:S(2)}, u32[]{:S(2)}) collective-permute-start(bf16[1,1,128,512]{3,2,1,0:T(8,128)(2,1)S(1)} %copy.24), channel_id=1, source_target_pairs={{0,16},{16,32},{32,48},{48,64},{64,80},{80,96},{96,112},{112,128},... | collective-permute-start | bytes 393224 | tf_op jit(solution)/shard_map/while/body/eval_jaxpr/ppermute | solution.py:11
  (45 other events, 2502.9 us)
where the time goes:
time: 613 us; the launch traced here: 607 us
  starting transfers between devices  368 us (60%)
  waiting for transfers between devices  104 us (17%)
  blocking collectives  65.8 us (11%)
  local copies, waits for them, and re-layouts  29.5 us (5%)
  other arithmetic  23.8 us (4%)
  matrix products  13.4 us (2%)
    ppermute x62, starting transfers between devices, from_behind(): return lax.ppermute(x, axis, [(i, (i + by) % peers) for i in range(peers)])  368 us
    ppermute x62, waiting for transfers between devices, from_behind(): return lax.ppermute(x, axis, [(i, (i + by) % peers) for i in range(peers)])  104 us
    all_to_all x1, blocking collectives, body(): lax.all_to_all(outbox, 'kblk', split_axis=0, concat_axis=0, tiled=True)  65.8 us
    dynamic_slice x32, local copies, waits for them, and re-layouts, make_tile(): limit_g = cut_row[partner]  20.5 us
    lt x32, other arithmetic, make_tile(): g_index < limit_g  19.5 us
  transfers between devices with their start and end apart: 62, of which 39 were waited for; matrix products, arithmetic and copies ran while one was open for 9% of the time, Pallas kernels for 0%

commit v1 on v0

v1 whole, which is shorter than its diff:
```python
import jax
import jax.numpy as jnp
from jax import lax
from jax.experimental import pallas as pl
from jax.experimental.pallas import tpu as pltpu
from jax.sharding import PartitionSpec as P

CAP = 4
RING = 8
PIECES = 2
LIST = 16


def place(i):
    return i // 4, (i // 2) % 2, i % 2


def index(y, z, c):
    return ((y % RING) * 2 + z) * 2 + c


def pairs(move):
    return [(i, index(*move(*place(i)))) for i in range(4 * RING)]


OTHER_CORE = pairs(lambda y, z, c: (y, z, 1 - c))
OTHER_HALF = pairs(lambda y, z, c: (y, 1 - z, c))
ONWARD = pairs(lambda y, z, c: (y + 1 - 2 * c, z, c))


def send(x, perm):
    return lax.ppermute(x, "kring", perm)


def tiles_kernel(cut_ref, elem_ref, *refs):
    *row_refs, out_ref, masked = refs
    g_count = 1024
    rows = out_ref.shape[1]
    lane = lax.broadcasted_iota(jnp.int32, (16, g_count), 1)
    at = 0
    for ref in row_refs:
        for k in range(ref.shape[0]):
            keep = (lane < cut_ref[at]).astype(jnp.float32).astype(jnp.bfloat16)
            part = ref[k, :, :g_count].reshape(rows // 16, 16, g_count) * keep[None]
            span = pl.ds(at * rows, rows)
            masked[span, :g_count] = part.reshape(rows, g_count)
            masked[span, g_count:] = ref[k, :, g_count:]
            at += 1
    total = jnp.dot(masked[...], elem_ref[...], preferred_element_type=jnp.float32)
    out_ref[...] = total.astype(jnp.bfloat16).reshape(out_ref.shape)


def make_tiles(cut, elem_t, blocks):
    rows, depth = blocks[0].shape[1:]
    width = elem_t.shape[1]
    vmem = pl.BlockSpec(memory_space=pltpu.VMEM)
    return pl.pallas_call(
        tiles_kernel,
        out_shape=jax.ShapeDtypeStruct((LIST, rows, width), jnp.bfloat16),
        in_specs=[pl.BlockSpec(memory_space=pltpu.SMEM)] + [vmem] * (1 + len(blocks)),
        out_specs=vmem,
        scratch_shapes=[pltpu.VMEM((LIST * rows, depth), jnp.bfloat16)],
        compiler_params=pltpu.CompilerParams(vmem_limit_bytes=40 << 20),
        cost_estimate=pl.CostEstimate(
            flops=2 * LIST * rows * depth * width, bytes_accessed=2 * LIST * rows * depth, transcendentals=0
        ),
    )(cut, elem_t, *blocks)


def outbox_kernel(pos_ref, mine_ref, other_ref, out_ref, held):
    held[:LIST] = mine_ref[...]
    held[LIST : 2 * LIST] = other_ref[...]
    held[2 * LIST] = jnp.zeros(held.shape[1:], held.dtype)
    for s in range(out_ref.shape[0]):
        out_ref[s] = held[pos_ref[s]]


def make_outbox(pos, mine, other):
    rows, width = mine.shape[1:]
    slots = pos.shape[0]
    vmem = pl.BlockSpec(memory_space=pltpu.VMEM)
    return pl.pallas_call(
        outbox_kernel,
        out_shape=jax.ShapeDtypeStruct((slots, rows, width), jnp.bfloat16),
        in_specs=[pl.BlockSpec(memory_space=pltpu.SMEM), vmem, vmem],
        out_specs=vmem,
        scratch_shapes=[pltpu.VMEM((2 * LIST + 1, rows, width), jnp.bfloat16)],
        compiler_params=pltpu.CompilerParams(vmem_limit_bytes=16 << 20),
    )(pos, mine, other)


def turn_kernel(*refs):
    *in_refs, out_ref = refs
    for s in range(out_ref.shape[0]):
        whole = jnp.concatenate([ref[s] for ref in in_refs], axis=0)
        out_ref[s] = whole.T


def turn(parts):
    slots, _, width = parts[0].shape
    rows = sum(p.shape[1] for p in parts)
    at_once = 8
    return pl.pallas_call(
        turn_kernel,
        grid=(slots // at_once,),
        out_shape=jax.ShapeDtypeStruct((slots, width, rows), jnp.bfloat16),
        in_specs=[pl.BlockSpec((at_once,) + p.shape[1:], lambda s: (s, 0, 0)) for p in parts],
        out_specs=pl.BlockSpec((at_once, width, rows), lambda s: (s, 0, 0)),
    )(*parts)


def body(elem_x, elem_d, rows_x, rows_d, coulomb, screened, cutoff, owners):
    blk_len = lax.axis_size("kblk")
    me = lax.axis_index("kring")
    my_y, my_z, my_c = place(me)
    rows = jnp.concatenate([rows_x[0, 0], rows_d[0, 0]], axis=1)
    tile_rows = rows.shape[0]
    step = tile_rows // PIECES

    near = send(rows, OTHER_CORE)
    far = [send(rows[k * step : (k + 1) * step], OTHER_HALF) for k in range(PIECES)]

    scaled_x = (elem_x[0, 0].astype(jnp.float32) * coulomb).astype(jnp.bfloat16)
    scaled_d = (elem_d[0, 0].astype(jnp.float32) * screened).astype(jnp.bfloat16)
    elem_t = jnp.concatenate([2 * scaled_x, -scaled_d], axis=1).T
    cut_row = cutoff[0, 0]
    elem_near = send(elem_t, OTHER_CORE)
    cut_near = send(cut_row, OTHER_CORE)

    partner = jnp.arange(4 * RING, dtype=jnp.int32)
    p_y, p_z, p_c = place(partner)

    def in_list(core):
        ahead = jnp.where(core == 0, my_y - p_y, p_y - my_y) % RING
        off = jnp.abs(p_c - core)
        has = jnp.where((ahead == 0) | (ahead == 4), off == 0, ahead < 4)
        spot = jnp.where(ahead == 0, 0, 2 * ahead - 1 + off) + 8 * jnp.abs(p_z - my_z)
        return has, spot

    has_mine, spot_mine = in_list(my_c)
    _, spot_other = in_list(1 - my_c)
    spot = jnp.where(has_mine, spot_mine, LIST + spot_other)
    fits = has_mine[None, :] & (spot_mine[None, :] == jnp.arange(LIST, dtype=jnp.int32)[:, None])
    cut_mine = jnp.sum(jnp.where(fits, cut_row[None, :], 0), axis=1)
    cut_other = jnp.sum(jnp.where(fits, cut_near[None, :], 0), axis=1)

    dest = owners[0, 0, :, 0]
    same = (dest[:, None] == dest[None, :]) & (partner[None, :] < partner[:, None])
    slot_of = jnp.sum(same.astype(jnp.int32), axis=1)
    slots = jnp.arange(blk_len * CAP, dtype=jnp.int32)
    hit = slots[:, None] == (dest * CAP + slot_of)[None, :]
    pos = 2 * LIST + jnp.sum(jnp.where(hit, (spot - 2 * LIST)[None, :], 0), axis=1)

    received = []
    for k in range(PIECES):
        span = slice(k * step, (k + 1) * step)
        blocks = []
        for first, second in ((rows[span], near[span]), (far[k], send(far[k], OTHER_CORE))):
            held = jnp.stack([first, second])
            blocks.append(held[:1])
            for _ in range(3):
                held = send(held, ONWARD)
                blocks.append(held)
            blocks.append(send(held[:1], ONWARD))
        other = send(make_tiles(cut_other, elem_near, blocks), OTHER_CORE)
        mine = make_tiles(cut_mine, elem_t, blocks)
        outbox = make_outbox(pos, mine, other).reshape(blk_len, CAP, step, tile_rows)
        got = lax.all_to_all(outbox, "kblk", split_axis=0, concat_axis=0, tiled=True)
        received.append(got.reshape(blk_len * CAP, step, tile_rows))
    return turn(received).reshape(1, 1, blk_len, CAP, tile_rows, tile_rows)


def solution(mesh):
    in_specs = (
        P("kring", "kblk", None, None),
        P("kring", "kblk", None, None),
        P("kring", "kblk", None, None),
        P("kring", "kblk", None, None),
        P(),
        P(),
        P("kring", "kblk", None),
        P("kring", "kblk", None, None),
    )
    out_specs = P("kring", "kblk", None, None, None, None)
    return jax.shard_map(body, mesh=mesh, in_specs=in_specs, out_specs=out_specs, check_vma=False)
```

time: 613 us -> 187 us (0.31)
  starting transfers between devices: 368 us -> 113 us
  waiting for transfers between devices: 104 us -> 19.1 us
  blocking collectives: 65.8 us -> 32.3 us
  local copies, waits for them, and re-layouts: 29.5 us -> 1.09 us
  other arithmetic: 23.8 us -> 4 us
  Pallas kernels: 0 us -> 15.4 us
  matrix products: 13.4 us -> 0 us
    ppermute x62 -> x25, starting transfers between devices: 368 us -> 107 us  [send(): return lax.ppermute(x, 'kring', perm)]
    ppermute x62 -> x25, waiting for transfers between devices: 104 us -> 19.1 us  [send(): return lax.ppermute(x, 'kring', perm)]
    all_to_all x1, blocking collectives: 65.8 us -> 32.3 us  [body(): lax.all_to_all(outbox, 'kblk', split_axis=0, concat_axis=0, tiled=True)]
    dynamic_slice x32 -> x0, local copies, waits for them, and re-layouts: 20.5 us -> none  [make_tile(): limit_g = cut_row[partner]]
    lt x32 -> x0, other arithmetic: 19.5 us -> none  [make_tile(): g_index < limit_g]
    pallas_call x0 -> x7, Pallas kernels: none -> 15.4 us  [the longest x4 7.01 us: make_tiles(): pl.pallas_call(tiles_kernel, out_shape=jax.ShapeDtypeStruct((LIST, rows,...]
    dot_general x64 -> x0, matrix products: 13.4 us -> none  [the longest x32 7.39 us: make_tile(): lax.dot_general(scaled_x, masked, contract, preferred_element_type=jnp.fl...]
  transfers between devices with their start and end apart: 62 -> 26, of which waited for: 39 -> 10; matrix products, arithmetic and copies ran while one was open for 9% -> 2% of each run, Pallas kernels for 0% -> 5%
where the time goes in v1:
time: 187 us; the launch traced here: 186 us
  starting transfers between devices  113 us (60%)
  blocking collectives  32.3 us (17%)
  waiting for transfers between devices  19.1 us (10%)
  Pallas kernels  15.4 us (8%)
  other arithmetic  4 us (2%)
    ppermute x25, starting transfers between devices, send(): return lax.ppermute(x, 'kring', perm)  107 us
    all_to_all x1, blocking collectives, body(): lax.all_to_all(outbox, 'kblk', split_axis=0, concat_axis=0, tiled=True)  32.3 us
    ppermute x25, waiting for transfers between devices, send(): return lax.ppermute(x, 'kring', perm)  19.1 us
    pallas_call x4, Pallas kernels, make_tiles(): pl.pallas_call(tiles_kernel, out_shape=jax.ShapeDtypeStruct((LIST, rows,...  7.01 us
    pallas_call x1, Pallas kernels, turn(): pl.pallas_call(turn_kernel, grid=(slots // at_once,), out_shape=jax.Shape...  6.13 us
    all_to_all x1, starting transfers between devices, body(): lax.all_to_all(outbox, 'kblk', split_axis=0, concat_axis=0, tiled=True)  5.79 us
  transfers between devices with their start and end apart: 26, of which 10 were waited for; matrix products, arithmetic and copies ran while one was open for 2% of the time, Pallas kernels for 5%

profile of v1, /device:TPU:1, one launch (start us, length us, event | category | flops | bytes accessed | tf_op | source)
XLA Modules:
  0.0 185.7 jit_solution(3019338982201095867)
XLA Ops:
  1.1 11.5 %collective-permute-start.18 = (bf16[64,1536]{1,0:T(8,128)(2,1)S(1)}, bf16[64,1536]{1,0:T(8,128)(2,1)S(1)}, u32[]{:S(2)}, u32[]{:S(2)}) collective-permute-start(bf16[64,1536]{1,0:T(8,128)(2,1)S(1)} %get-tuple-element.12), channel_id=1, source_target_pairs={{0,32},{16,48},{32,0},{48,16},{64,96},{80,112},{96,64},{112,80},{1... | collective-permute-start | bytes 589832 | tf_op jit(solution)/shard_map/ppermute | solution.py:32
  12.6 4.7 %collective-permute-done.18 = bf16[64,1536]{1,0:T(8,128)(2,1)S(1)} collective-permute-done((bf16[64,1536]{1,0:T(8,128)(2,1)S(1)}, bf16[64,1536]{1,0:T(8,128)(2,1)S(1)}, u32[]{:S(2)}, u32[]{:S(2)}) %collective-permute-start.18) | collective-permute-done | bytes 196640 | tf_op jit(solution)/shard_map/ppermute | solution.py:32
  17.3 4.2 %collective-permute-start.19 = (bf16[64,1536]{1,0:T(8,128)(2,1)S(1)}, bf16[64,1536]{1,0:T(8,128)(2,1)S(1)}, u32[]{:S(2)}, u32[]{:S(2)}) collective-permute-start(bf16[64,1536]{1,0:T(8,128)(2,1)S(1)} %collective-permute-done.18), channel_id=1, source_target_pairs={{0,16},{16,0},{32,48},{48,32},{64,80},{80,64},{96,112},{112,96},{1... | collective-permute-start | bytes 589832 | tf_op jit(solution)/shard_map/ppermute | solution.py:32
  24.6 4.0 %collective-permute-start.20 = (bf16[2,64,1536]{2,1,0:T(8,128)(2,1)S(1)}, bf16[2,64,1536]{2,1,0:T(8,128)(2,1)S(1)}, u32[]{:S(2)}, u32[]{:S(2)}) collective-permute-start(bf16[2,64,1536]{2,1,0:T(8,128)(2,1)S(1)} %pad_maximum_fusion.4), channel_id=1, source_target_pairs={{0,64},{16,464},{32,96},{48,496},{64,128},{80,16},{96,160},{112,48... | collective-permute-start | bytes 1179656 | tf_op jit(solution)/shard_map/ppermute | solution.py:32
  34.6 3.7 %collective-permute-start.21 = (bf16[2,64,1536]{2,1,0:T(8,128)(2,1)S(1)}, bf16[2,64,1536]{2,1,0:T(8,128)(2,1)S(1)}, u32[]{:S(2)}, u32[]{:S(2)}) collective-permute-start(bf16[2,64,1536]{2,1,0:T(8,128)(2,1)S(1)} %collective-permute-done.20.refs_6_), channel_id=1, source_target_pairs={{0,64},{16,464},{32,96},{48,496},{64,128},{80,16},{96,160},{112,48... | collective-permute-start | bytes 1179656 | tf_op jit(solution)/shard_map/ppermute | solution.py:32
  38.3 4.2 %collective-permute-start.15 = (bf16[2,64,1536]{2,1,0:T(8,128)(2,1)S(1)}, bf16[2,64,1536]{2,1,0:T(8,128)(2,1)}, u32[]{:S(2)}, u32[]{:S(2)}) collective-permute-start(bf16[2,64,1536]{2,1,0:T(8,128)(2,1)S(1)} %collective-permute-done.14.refs_1_), channel_id=1, source_target_pairs={{0,64},{16,464},{32,96},{48,496},{64,128},{80,16},{96,160},{112,48... | collective-permute-start | bytes 1179656 | tf_op jit(solution)/shard_map/ppermute | solution.py:32
  43.4 4.6 %collective-permute-start.22 = (bf16[2,64,1536]{2,1,0:T(8,128)(2,1)S(1)}, bf16[2,64,1536]{2,1,0:T(8,128)(2,1)S(1)}, u32[]{:S(2)}, u32[]{:S(2)}) collective-permute-start(bf16[2,64,1536]{2,1,0:T(8,128)(2,1)S(1)} %collective-permute-done.21.refs_7_), channel_id=1, source_target_pairs={{0,64},{16,464},{32,96},{48,496},{64,128},{80,16},{96,160},{112,48... | collective-permute-start | bytes 1179656 | tf_op jit(solution)/shard_map/ppermute | solution.py:32
  48.0 4.3 %collective-permute-start.16 = (bf16[2,64,1536]{2,1,0:T(8,128)(2,1)}, bf16[2,64,1536]{2,1,0:T(8,128)(2,1)S(1)}, u32[]{:S(2)}, u32[]{:S(2)}) collective-permute-start(bf16[2,64,1536]{2,1,0:T(8,128)(2,1)} %collective-permute-done.15.refs_2_), channel_id=1, source_target_pairs={{0,64},{16,464},{32,96},{48,496},{64,128},{80,16},{96,160},{112,48... | collective-permute-start | bytes 1179656 | tf_op jit(solution)/shard_map/ppermute | solution.py:32
  55.0 10.7 %collective-permute-start.5 = (bf16[64,1536]{1,0:T(8,128)(2,1)S(1)}, bf16[64,1536]{1,0:T(8,128)(2,1)S(1)}, u32[]{:S(2)}, u32[]{:S(2)}) collective-permute-start(bf16[64,1536]{1,0:T(8,128)(2,1)S(1)} %get-tuple-element.13), channel_id=1, source_target_pairs={{0,32},{16,48},{32,0},{48,16},{64,96},{80,112},{96,64},{112,80},{1... | collective-permute-start | bytes 589832 | tf_op jit(solution)/shard_map/ppermute | solution.py:32
  66.0 4.7 %collective-permute-start.23 = (bf16[1,64,1536]{2,1,0:T(8,128)(2,1)S(1)}, bf16[1,64,1536]{2,1,0:T(8,128)(2,1)S(1)}, u32[]{:S(2)}, u32[]{:S(2)}) collective-permute-start(bf16[1,64,1536]{2,1,0:T(8,128)(2,1)S(1)} %slice.43), channel_id=1, source_target_pairs={{0,64},{16,464},{32,96},{48,496},{64,128},{80,16},{96,160},{112,48... | collective-permute-start | bytes 589832 | tf_op jit(solution)/shard_map/ppermute | solution.py:32
  73.3 4.1 %collective-permute-done.17.refs_4_ = bf16[1,64,1536]{2,1,0:T(8,128)(2,1)S(1)} collective-permute-done((bf16[1,64,1536]{2,1,0:T(8,128)(2,1)S(1)}, bf16[1,64,1536]{2,1,0:T(8,128)(2,1)S(1)}, u32[]{:S(2)}, u32[]{:S(2)}) %collective-permute-start.17) | collective-permute-done | bytes 196640 | tf_op jit(solution)/shard_map/ppermute | solution.py:32
  79.4 3.4 %collective-permute-start.24 = (bf16[16,64,128]{2,1,0:T(8,128)(2,1)S(1)}, bf16[16,64,128]{2,1,0:T(8,128)(2,1)S(1)}, u32[]{:S(2)}, u32[]{:S(2)}) collective-permute-start(bf16[16,64,128]{2,1,0:T(8,128)(2,1)S(1)} %shard_map.86), channel_id=1, source_target_pairs={{0,16},{16,0},{32,48},{48,32},{64,80},{80,64},{96,112},{112,96},{1... | collective-permute-start | bytes 786440 | tf_op jit(solution)/shard_map/ppermute | solution.py:32
  88.5 5.8 %all-to-all-start.1 = ((bf16[16,4,64,128]{3,2,1,0:T(8,128)(2,1)}), bf16[16,4,64,128]{3,2,1,0:T(8,128)(2,1)S(1)}, u32[]{:S(2)}, u32[]{:S(2)}) async-start(bf16[16,4,64,128]{3,2,1,0:T(8,128)(2,1)} %bitcast.17), calls=%async_computation.1 | async-start | bytes 2097152 | tf_op jit(solution)/shard_map/all_to_all | solution.py:168
  97.6 3.0 %collective-permute-start.1 = (bf16[2,64,1536]{2,1,0:T(8,128)(2,1)S(1)}, bf16[2,64,1536]{2,1,0:T(8,128)(2,1)S(1)}, u32[]{:S(2)}, u32[]{:S(2)}) collective-permute-start(bf16[2,64,1536]{2,1,0:T(8,128)(2,1)S(1)} %pad_maximum_fusion.1), channel_id=1, source_target_pairs={{0,64},{16,464},{32,96},{48,496},{64,128},{80,16},{96,160},{112,48... | collective-permute-start | bytes 1179656 | tf_op jit(solution)/shard_map/ppermute | solution.py:32
  100.6 3.5 %collective-permute-done.7.refs_6_ = bf16[2,64,1536]{2,1,0:T(8,128)(2,1)S(1)} collective-permute-done((bf16[2,64,1536]{2,1,0:T(8,128)(2,1)S(1)}, bf16[2,64,1536]{2,1,0:T(8,128)(2,1)S(1)}, u32[]{:S(2)}, u32[]{:S(2)}) %collective-permute-start.7) | collective-permute-done | bytes 393248 | tf_op jit(solution)/shard_map/ppermute | solution.py:32
  104.1 3.5 %collective-permute-start.8 = (bf16[2,64,1536]{2,1,0:T(8,128)(2,1)S(1)}, bf16[2,64,1536]{2,1,0:T(8,128)(2,1)S(1)}, u32[]{:S(2)}, u32[]{:S(2)}) collective-permute-start(bf16[2,64,1536]{2,1,0:T(8,128)(2,1)S(1)} %collective-permute-done.7.refs_6_), channel_id=1, source_target_pairs={{0,64},{16,464},{32,96},{48,496},{64,128},{80,16},{96,160},{112,48... | collective-permute-start | bytes 1179656 | tf_op jit(solution)/shard_map/ppermute | solution.py:32
  108.3 3.5 %collective-permute-start.2 = (bf16[2,64,1536]{2,1,0:T(8,128)(2,1)S(1)}, bf16[2,64,1536]{2,1,0:T(8,128)(2,1)S(1)}, u32[]{:S(2)}, u32[]{:S(2)}) collective-permute-start(bf16[2,64,1536]{2,1,0:T(8,128)(2,1)S(1)} %collective-permute-done.1.refs_1_), channel_id=1, source_target_pairs={{0,64},{16,464},{32,96},{48,496},{64,128},{80,16},{96,160},{112,48... | collective-permute-start | bytes 1179656 | tf_op jit(solution)/shard_map/ppermute | solution.py:32
  113.4 3.8 %collective-permute-start.9 = (bf16[2,64,1536]{2,1,0:T(8,128)(2,1)S(1)}, bf16[2,64,1536]{2,1,0:T(8,128)(2,1)S(1)}, u32[]{:S(2)}, u32[]{:S(2)}) collective-permute-start(bf16[2,64,1536]{2,1,0:T(8,128)(2,1)S(1)} %collective-permute-done.8.refs_7_), channel_id=1, source_target_pairs={{0,64},{16,464},{32,96},{48,496},{64,128},{80,16},{96,160},{112,48... | collective-permute-start | bytes 1179656 | tf_op jit(solution)/shard_map/ppermute | solution.py:32
  117.6 4.0 %collective-permute-start.3 = (bf16[2,64,1536]{2,1,0:T(8,128)(2,1)S(1)}, bf16[2,64,1536]{2,1,0:T(8,128)(2,1)S(1)}, u32[]{:S(2)}, u32[]{:S(2)}) collective-permute-start(bf16[2,64,1536]{2,1,0:T(8,128)(2,1)S(1)} %collective-permute-done.2.refs_2_), channel_id=1, source_target_pairs={{0,64},{16,464},{32,96},{48,496},{64,128},{80,16},{96,160},{112,48... | collective-permute-start | bytes 1179656 | tf_op jit(solution)/shard_map/ppermute | solution.py:32
  122.0 5.0 %collective-permute-start.10 = (bf16[1,64,1536]{2,1,0:T(8,128)(2,1)S(1)}, bf16[1,64,1536]{2,1,0:T(8,128)(2,1)S(1)}, u32[]{:S(2)}, u32[]{:S(2)}) collective-permute-start(bf16[1,64,1536]{2,1,0:T(8,128)(2,1)S(1)} %slice.38), channel_id=1, source_target_pairs={{0,64},{16,464},{32,96},{48,496},{64,128},{80,16},{96,160},{112,48... | collective-permute-start | bytes 589832 | tf_op jit(solution)/shard_map/ppermute | solution.py:32
  127.0 4.4 %collective-permute-start.4 = (bf16[1,64,1536]{2,1,0:T(8,128)(2,1)S(1)}, bf16[1,64,1536]{2,1,0:T(8,128)(2,1)S(1)}, u32[]{:S(2)}, u32[]{:S(2)}) collective-permute-start(bf16[1,64,1536]{2,1,0:T(8,128)(2,1)S(1)} %slice.37), channel_id=1, source_target_pairs={{0,64},{16,464},{32,96},{48,496},{64,128},{80,16},{96,160},{112,48... | collective-permute-start | bytes 589832 | tf_op jit(solution)/shard_map/ppermute | solution.py:32
  135.5 9.5 %collective-permute-start.13 = (bf16[16,64,128]{2,1,0:T(8,128)(2,1)S(1)}, bf16[16,64,128]{2,1,0:T(8,128)(2,1)S(1)}, u32[]{:S(2)}, u32[]{:S(2)}) collective-permute-start(bf16[16,64,128]{2,1,0:T(8,128)(2,1)S(1)} %shard_map.83), channel_id=1, source_target_pairs={{0,16},{16,0},{32,48},{48,32},{64,80},{80,64},{96,112},{112,96},{1... | collective-permute-start | bytes 786440 | tf_op jit(solution)/shard_map/ppermute | solution.py:32
  147.3 32.3 %all_to_all.10 = bf16[16,4,64,128]{3,2,1,0:T(8,128)(2,1)} all-to-all(bf16[16,4,64,128]{3,2,1,0:T(8,128)(2,1)S(1)} %bitcast.28), channel_id=1, replica_groups=mesh['kring'=32,'kblk'=16] {'kblk'}, dimensions={0} | all-to-all | bytes 2097152 | tf_op jit(solution)/shard_map/all_to_all | solution.py:168
  179.6 6.1 %shard_map.88 = bf16[64,128,128]{2,1,0:T(8,128)(2,1)} custom-call(bf16[64,64,128]{2,1,0:T(8,128)(2,1)} %bitcast.42, bf16[64,64,128]{2,1,0:T(8,128)(2,1)} %bitcast.41), custom_call_target="tpu_custom_call" | custom-call | tf_op jit(solution)/shard_map/pallas_call | solution.py:103
  (74 shorter events, 36.6 us)
Async XLA Ops:
  1.1 16.2 %collective-permute-start.18 = (bf16[64,1536]{1,0:T(8,128)(2,1)S(1)}, bf16[64,1536]{1,0:T(8,128)(2,1)S(1)}, u32[]{:S(2)}, u32[]{:S(2)}) collective-permute-start(bf16[64,1536]{1,0:T(8,128)(2,1)S(1)} %get-tuple-element.12), channel_id=1, source_target_pairs={{0,32},{16,48},{32,0},{48,16},{64,96},{80,112},{96,64},{112,80},{1... | collective-permute-start | bytes 589832 | tf_op jit(solution)/shard_map/ppermute | solution.py:32
  17.3 7.2 %collective-permute-start.19 = (bf16[64,1536]{1,0:T(8,128)(2,1)S(1)}, bf16[64,1536]{1,0:T(8,128)(2,1)S(1)}, u32[]{:S(2)}, u32[]{:S(2)}) collective-permute-start(bf16[64,1536]{1,0:T(8,128)(2,1)S(1)} %collective-permute-done.18), channel_id=1, source_target_pairs={{0,16},{16,0},{32,48},{48,32},{64,80},{80,64},{96,112},{112,96},{1... | collective-permute-start | bytes 589832 | tf_op jit(solution)/shard_map/ppermute | solution.py:32
  24.6 10.0 %collective-permute-start.20 = (bf16[2,64,1536]{2,1,0:T(8,128)(2,1)S(1)}, bf16[2,64,1536]{2,1,0:T(8,128)(2,1)S(1)}, u32[]{:S(2)}, u32[]{:S(2)}) collective-permute-start(bf16[2,64,1536]{2,1,0:T(8,128)(2,1)S(1)} %pad_maximum_fusion.4), channel_id=1, source_target_pairs={{0,64},{16,464},{32,96},{48,496},{64,128},{80,16},{96,160},{112,48... | collective-permute-start | bytes 1179656 | tf_op jit(solution)/shard_map/ppermute | solution.py:32
  29.4 9.0 %collective-permute-start.14 = (bf16[2,64,1536]{2,1,0:T(8,128)(2,1)S(1)}, bf16[2,64,1536]{2,1,0:T(8,128)(2,1)S(1)}, u32[]{:S(2)}, u32[]{:S(2)}) collective-permute-start(bf16[2,64,1536]{2,1,0:T(8,128)(2,1)S(1)} %pad_maximum_fusion.3), channel_id=1, source_target_pairs={{0,64},{16,464},{32,96},{48,496},{64,128},{80,16},{96,160},{112,48... | collective-permute-start | bytes 1179656 | tf_op jit(solution)/shard_map/ppermute | solution.py:32
  32.3 40.4 %collective-permute-start.11 = (s32[32]{0:T(128)S(1)}, s32[32]{0:T(128)S(1)}, u32[]{:S(2)}, u32[]{:S(2)}) collective-permute-start(s32[32]{0:T(128)S(1)} %bitcast.48), channel_id=1, source_target_pairs={{0,16},{16,0},{32,48},{48,32},{64,80},{80,64},{96,112},{112,96},{1... | collective-permute-start | bytes 392 | tf_op jit(solution)/shard_map/ppermute | solution.py:32
  34.6 8.8 %collective-permute-start.21 = (bf16[2,64,1536]{2,1,0:T(8,128)(2,1)S(1)}, bf16[2,64,1536]{2,1,0:T(8,128)(2,1)S(1)}, u32[]{:S(2)}, u32[]{:S(2)}) collective-permute-start(bf16[2,64,1536]{2,1,0:T(8,128)(2,1)S(1)} %collective-permute-done.20.refs_6_), channel_id=1, source_target_pairs={{0,64},{16,464},{32,96},{48,496},{64,128},{80,16},{96,160},{112,48... | collective-permute-start | bytes 1179656 | tf_op jit(solution)/shard_map/ppermute | solution.py:32
  38.3 9.7 %collective-permute-start.15 = (bf16[2,64,1536]{2,1,0:T(8,128)(2,1)S(1)}, bf16[2,64,1536]{2,1,0:T(8,128)(2,1)}, u32[]{:S(2)}, u32[]{:S(2)}) collective-permute-start(bf16[2,64,1536]{2,1,0:T(8,128)(2,1)S(1)} %collective-permute-done.14.refs_1_), channel_id=1, source_target_pairs={{0,64},{16,464},{32,96},{48,496},{64,128},{80,16},{96,160},{112,48... | collective-permute-start | bytes 1179656 | tf_op jit(solution)/shard_map/ppermute | solution.py:32
  43.4 22.5 %collective-permute-start.22 = (bf16[2,64,1536]{2,1,0:T(8,128)(2,1)S(1)}, bf16[2,64,1536]{2,1,0:T(8,128)(2,1)S(1)}, u32[]{:S(2)}, u32[]{:S(2)}) collective-permute-start(bf16[2,64,1536]{2,1,0:T(8,128)(2,1)S(1)} %collective-permute-done.21.refs_7_), channel_id=1, source_target_pairs={{0,64},{16,464},{32,96},{48,496},{64,128},{80,16},{96,160},{112,48... | collective-permute-start | bytes 1179656 | tf_op jit(solution)/shard_map/ppermute | solution.py:32
  48.0 22.7 %collective-permute-start.16 = (bf16[2,64,1536]{2,1,0:T(8,128)(2,1)}, bf16[2,64,1536]{2,1,0:T(8,128)(2,1)S(1)}, u32[]{:S(2)}, u32[]{:S(2)}) collective-permute-start(bf16[2,64,1536]{2,1,0:T(8,128)(2,1)} %collective-permute-done.15.refs_2_), channel_id=1, source_target_pairs={{0,64},{16,464},{32,96},{48,496},{64,128},{80,16},{96,160},{112,48... | collective-permute-start | bytes 1179656 | tf_op jit(solution)/shard_map/ppermute | solution.py:32
  52.4 20.4 %collective-permute-start.12 = (bf16[1536,128]{1,0:T(8,128)(2,1)S(1)}, bf16[1536,128]{1,0:T(8,128)(2,1)S(1)}, u32[]{:S(2)}, u32[]{:S(2)}) collective-permute-start(bf16[1536,128]{1,0:T(8,128)(2,1)S(1)} %maximum_bitcast_fusion.elem_ref), channel_id=1, source_target_pairs={{0,16},{16,0},{32,48},{48,32},{64,80},{80,64},{96,112},{112,96},{1... | collective-permute-start | bytes 1179656 | tf_op jit(solution)/shard_map/ppermute | solution.py:32
  55.0 27.9 %collective-permute-start.5 = (bf16[64,1536]{1,0:T(8,128)(2,1)S(1)}, bf16[64,1536]{1,0:T(8,128)(2,1)S(1)}, u32[]{:S(2)}, u32[]{:S(2)}) collective-permute-start(bf16[64,1536]{1,0:T(8,128)(2,1)S(1)} %get-tuple-element.13), channel_id=1, source_target_pairs={{0,32},{16,48},{32,0},{48,16},{64,96},{80,112},{96,64},{112,80},{1... | collective-permute-start | bytes 589832 | tf_op jit(solution)/shard_map/ppermute | solution.py:32
  66.0 7.3 %collective-permute-start.23 = (bf16[1,64,1536]{2,1,0:T(8,128)(2,1)S(1)}, bf16[1,64,1536]{2,1,0:T(8,128)(2,1)S(1)}, u32[]{:S(2)}, u32[]{:S(2)}) collective-permute-start(bf16[1,64,1536]{2,1,0:T(8,128)(2,1)S(1)} %slice.43), channel_id=1, source_target_pairs={{0,64},{16,464},{32,96},{48,496},{64,128},{80,16},{96,160},{112,48... | collective-permute-start | bytes 589832 | tf_op jit(solution)/shard_map/ppermute | solution.py:32
  79.4 7.4 %collective-permute-start.24 = (bf16[16,64,128]{2,1,0:T(8,128)(2,1)S(1)}, bf16[16,64,128]{2,1,0:T(8,128)(2,1)S(1)}, u32[]{:S(2)}, u32[]{:S(2)}) collective-permute-start(bf16[16,64,128]{2,1,0:T(8,128)(2,1)S(1)} %shard_map.86), channel_id=1, source_target_pairs={{0,16},{16,0},{32,48},{48,32},{64,80},{80,64},{96,112},{112,96},{1... | collective-permute-start | bytes 786440 | tf_op jit(solution)/shard_map/ppermute | solution.py:32
  82.9 11.4 %collective-permute-start.6 = (bf16[64,1536]{1,0:T(8,128)(2,1)S(1)}, bf16[64,1536]{1,0:T(8,128)(2,1)}, u32[]{:S(2)}, u32[]{:S(2)}) collective-permute-start(bf16[64,1536]{1,0:T(8,128)(2,1)S(1)} %collective-permute-done.5), channel_id=1, source_target_pairs={{0,16},{16,0},{32,48},{48,32},{64,80},{80,64},{96,112},{112,96},{1... | collective-permute-start | bytes 589832 | tf_op jit(solution)/shard_map/ppermute | solution.py:32
  88.5 58.8 %all-to-all-start.1 = ((bf16[16,4,64,128]{3,2,1,0:T(8,128)(2,1)}), bf16[16,4,64,128]{3,2,1,0:T(8,128)(2,1)S(1)}, u32[]{:S(2)}, u32[]{:S(2)}) async-start(bf16[16,4,64,128]{3,2,1,0:T(8,128)(2,1)} %bitcast.17), calls=%async_computation.1 | async-start | bytes 2097152 | tf_op jit(solution)/shard_map/all_to_all | solution.py:168
  95.2 8.8 %collective-permute-start.7 = (bf16[2,64,1536]{2,1,0:T(8,128)(2,1)S(1)}, bf16[2,64,1536]{2,1,0:T(8,128)(2,1)S(1)}, u32[]{:S(2)}, u32[]{:S(2)}) collective-permute-start(bf16[2,64,1536]{2,1,0:T(8,128)(2,1)S(1)} %pad_maximum_fusion.2), channel_id=1, source_target_pairs={{0,64},{16,464},{32,96},{48,496},{64,128},{80,16},{96,160},{112,48... | collective-permute-start | bytes 1179656 | tf_op jit(solution)/shard_map/ppermute | solution.py:32
  97.6 10.7 %collective-permute-start.1 = (bf16[2,64,1536]{2,1,0:T(8,128)(2,1)S(1)}, bf16[2,64,1536]{2,1,0:T(8,128)(2,1)S(1)}, u32[]{:S(2)}, u32[]{:S(2)}) collective-permute-start(bf16[2,64,1536]{2,1,0:T(8,128)(2,1)S(1)} %pad_maximum_fusion.1), channel_id=1, source_target_pairs={{0,64},{16,464},{32,96},{48,496},{64,128},{80,16},{96,160},{112,48... | collective-permute-start | bytes 1179656 | tf_op jit(solution)/shard_map/ppermute | solution.py:32
  104.1 9.4 %collective-permute-start.8 = (bf16[2,64,1536]{2,1,0:T(8,128)(2,1)S(1)}, bf16[2,64,1536]{2,1,0:T(8,128)(2,1)S(1)}, u32[]{:S(2)}, u32[]{:S(2)}) collective-permute-start(bf16[2,64,1536]{2,1,0:T(8,128)(2,1)S(1)} %collective-permute-done.7.refs_6_), channel_id=1, source_target_pairs={{0,64},{16,464},{32,96},{48,496},{64,128},{80,16},{96,160},{112,48... | collective-permute-start | bytes 1179656 | tf_op jit(solution)/shard_map/ppermute | solution.py:32
  108.3 9.4 %collective-permute-start.2 = (bf16[2,64,1536]{2,1,0:T(8,128)(2,1)S(1)}, bf16[2,64,1536]{2,1,0:T(8,128)(2,1)S(1)}, u32[]{:S(2)}, u32[]{:S(2)}) collective-permute-start(bf16[2,64,1536]{2,1,0:T(8,128)(2,1)S(1)} %collective-permute-done.1.refs_1_), channel_id=1, source_target_pairs={{0,64},{16,464},{32,96},{48,496},{64,128},{80,16},{96,160},{112,48... | collective-permute-start | bytes 1179656 | tf_op jit(solution)/shard_map/ppermute | solution.py:32
  113.4 8.5 %collective-permute-start.9 = (bf16[2,64,1536]{2,1,0:T(8,128)(2,1)S(1)}, bf16[2,64,1536]{2,1,0:T(8,128)(2,1)S(1)}, u32[]{:S(2)}, u32[]{:S(2)}) collective-permute-start(bf16[2,64,1536]{2,1,0:T(8,128)(2,1)S(1)} %collective-permute-done.8.refs_7_), channel_id=1, source_target_pairs={{0,64},{16,464},{32,96},{48,496},{64,128},{80,16},{96,160},{112,48... | collective-permute-start | bytes 1179656 | tf_op jit(solution)/shard_map/ppermute | solution.py:32
  117.6 9.4 %collective-permute-start.3 = (bf16[2,64,1536]{2,1,0:T(8,128)(2,1)S(1)}, bf16[2,64,1536]{2,1,0:T(8,128)(2,1)S(1)}, u32[]{:S(2)}, u32[]{:S(2)}) collective-permute-start(bf16[2,64,1536]{2,1,0:T(8,128)(2,1)S(1)} %collective-permute-done.2.refs_2_), channel_id=1, source_target_pairs={{0,64},{16,464},{32,96},{48,496},{64,128},{80,16},{96,160},{112,48... | collective-permute-start | bytes 1179656 | tf_op jit(solution)/shard_map/ppermute | solution.py:32
  122.0 9.5 %collective-permute-start.10 = (bf16[1,64,1536]{2,1,0:T(8,128)(2,1)S(1)}, bf16[1,64,1536]{2,1,0:T(8,128)(2,1)S(1)}, u32[]{:S(2)}, u32[]{:S(2)}) collective-permute-start(bf16[1,64,1536]{2,1,0:T(8,128)(2,1)S(1)} %slice.38), channel_id=1, source_target_pairs={{0,64},{16,464},{32,96},{48,496},{64,128},{80,16},{96,160},{112,48... | collective-permute-start | bytes 589832 | tf_op jit(solution)/shard_map/ppermute | solution.py:32
  127.0 7.0 %collective-permute-start.4 = (bf16[1,64,1536]{2,1,0:T(8,128)(2,1)S(1)}, bf16[1,64,1536]{2,1,0:T(8,128)(2,1)S(1)}, u32[]{:S(2)}, u32[]{:S(2)}) collective-permute-start(bf16[1,64,1536]{2,1,0:T(8,128)(2,1)S(1)} %slice.37), channel_id=1, source_target_pairs={{0,64},{16,464},{32,96},{48,496},{64,128},{80,16},{96,160},{112,48... | collective-permute-start | bytes 589832 | tf_op jit(solution)/shard_map/ppermute | solution.py:32
  135.5 11.1 %collective-permute-start.13 = (bf16[16,64,128]{2,1,0:T(8,128)(2,1)S(1)}, bf16[16,64,128]{2,1,0:T(8,128)(2,1)S(1)}, u32[]{:S(2)}, u32[]{:S(2)}) collective-permute-start(bf16[16,64,128]{2,1,0:T(8,128)(2,1)S(1)} %shard_map.83), channel_id=1, source_target_pairs={{0,16},{16,0},{32,48},{48,32},{64,80},{80,64},{96,112},{112,96},{1... | collective-permute-start | bytes 786440 | tf_op jit(solution)/shard_map/ppermute | solution.py:32
  (10 other events, 281.0 us)

commit v2 on v0

v2 whole, which is shorter than its diff:
```python
import functools

import jax
import jax.numpy as jnp
from jax import lax
from jax.experimental import pallas as pl
from jax.experimental.pallas import tpu as pltpu
from jax.sharding import PartitionSpec as P

CAP = 4
RING = 8
TILE = 128
G_COUNT = 1024
OWN_CHAINS = 2
FAR_CHAINS = 2


def place(i):
    return i // 4, (i // 2) % 2, i % 2


def index(y, z, c):
    return ((y % RING) * 2 + z) * 2 + c


def pairs(move):
    return [(i, index(*move(*place(i)))) for i in range(4 * RING)]


OTHER_CORE = pairs(lambda y, z, c: (y, z, 1 - c))
OTHER_HALF = pairs(lambda y, z, c: (y, 1 - z, c))
ONWARD = pairs(lambda y, z, c: (y + 1 - 2 * c, z, c))


def send(x, perm):
    return lax.ppermute(x, "kring", perm)


def tiles_kernel(count, cut_ref, elem_ref, *refs):
    *block_refs, out_ref, masked, total = refs
    depth = masked.shape[1]
    lane = lax.broadcasted_iota(jnp.int32, (16, G_COUNT), 1)
    half = len(block_refs) // count
    for first in range(count):
        refs_here = block_refs[first::count]
        rows = refs_here[0].shape[1]
        at = 0
        for j, ref in enumerate(refs_here):
            for k in range(1 if j in (0, half - 1) else 2):
                keep = (lane < cut_ref[at]).astype(jnp.float32).astype(jnp.bfloat16)
                part = ref[k, :, :G_COUNT].reshape(rows // 16, 16, G_COUNT) * keep[None]
                span = pl.ds(at * TILE + first * rows, rows)
                masked[span, :G_COUNT] = part.reshape(rows, G_COUNT)
                masked[span, G_COUNT:] = ref[k, :, G_COUNT:]
                at += 1
    total[...] = jnp.dot(masked[...], elem_ref[:depth, :], preferred_element_type=jnp.float32)
    for k in range(RING):
        out_ref[k] = total[pl.ds(k * TILE, TILE), :].T.astype(jnp.bfloat16)


def make_tiles(cuts, elem, blocks, after=()):
    depth = blocks[0][0].shape[2]
    flat = [b for step in zip(*blocks) for b in step]
    vmem = pl.BlockSpec(memory_space=pltpu.VMEM)
    free = pl.BlockSpec(memory_space=pl.ANY)

    def kernel(*refs):
        tiles_kernel(len(blocks), *refs[: 2 + len(flat)], *refs[2 + len(flat) + len(after) :])

    return pl.pallas_call(
        kernel,
        out_shape=jax.ShapeDtypeStruct((RING, TILE, TILE), jnp.bfloat16),
        in_specs=[pl.BlockSpec(memory_space=pltpu.SMEM)] + [vmem] * (1 + len(flat)) + [free] * len(after),
        out_specs=vmem,
        scratch_shapes=[
            pltpu.VMEM((RING * TILE, depth), jnp.bfloat16),
            pltpu.VMEM((RING * TILE, TILE), jnp.float32),
        ],
        compiler_params=pltpu.CompilerParams(vmem_limit_bytes=24 << 20),
        cost_estimate=pl.CostEstimate(
            flops=2 * RING * TILE * depth * TILE, bytes_accessed=2 * RING * TILE * depth, transcendentals=0
        ),
    )(cuts, elem, *flat, *after)


def pair_kernel(pieces, a_ref, b_ref, *refs):
    out_refs = refs[-pieces:]
    rows = out_refs[0].shape[1]
    for k, ref in enumerate(out_refs):
        ref[0] = a_ref[pl.ds(k * rows, rows), :]
        ref[1] = b_ref[pl.ds(k * rows, rows), :]


def pair(a, b, pieces, after=()):
    vmem = pl.BlockSpec(memory_space=pltpu.VMEM)
    free = pl.BlockSpec(memory_space=pl.ANY)
    shape = jax.ShapeDtypeStruct((2, a.shape[0] // pieces, a.shape[1]), a.dtype)
    return pl.pallas_call(
        functools.partial(pair_kernel, pieces),
        out_shape=(shape,) * pieces,
        in_specs=[vmem, vmem] + [free] * len(after),
        out_specs=(vmem,) * pieces,
        compiler_params=pltpu.CompilerParams(vmem_limit_bytes=8 << 20),
    )(a, b, *after)


def outbox_kernel(pos_ref, *refs):
    in_refs, (out_ref, held) = refs[:4], refs[-2:]
    for k, ref in enumerate(in_refs):
        held[k * RING : (k + 1) * RING] = ref[...]
    held[4 * RING] = jnp.zeros(held.shape[1:], held.dtype)
    for s in range(out_ref.shape[0]):
        out_ref[s] = held[pos_ref[s]]


def make_outbox(pos, parts, after=()):
    rows, width = parts[0].shape[1:]
    slots = pos.shape[0]
    free = pl.BlockSpec(memory_space=pl.ANY)
    vmem = pl.BlockSpec(memory_space=pltpu.VMEM)
    return pl.pallas_call(
        outbox_kernel,
        out_shape=jax.ShapeDtypeStruct((slots, rows, width), jnp.bfloat16),
        in_specs=[pl.BlockSpec(memory_space=pltpu.SMEM)] + [vmem] * 4 + [free] * len(after),
        out_specs=vmem,
        scratch_shapes=[pltpu.VMEM((4 * RING + 1, rows, width), jnp.bfloat16)],
        compiler_params=pltpu.CompilerParams(vmem_limit_bytes=16 << 20),
    )(pos, *parts, *after)


def copy_kernel(x_ref, *refs):
    refs[-1][...] = x_ref[...]


def copy_after(x, after):
    vmem = pl.BlockSpec(memory_space=pltpu.VMEM)
    free = pl.BlockSpec(memory_space=pl.ANY)
    return pl.pallas_call(
        copy_kernel,
        out_shape=jax.ShapeDtypeStruct(x.shape, x.dtype),
        in_specs=[vmem] + [free] * len(after),
        out_specs=vmem,
        compiler_params=pltpu.CompilerParams(vmem_limit_bytes=8 << 20),
    )(x, *after)


def ring(held):
    blocks = [held]
    for _ in range(RING // 2 - 1):
        held = send(held, ONWARD)
        blocks.append(held)
    return blocks + [send(held[:1], ONWARD)]


def body(elem_x, elem_d, rows_x, rows_d, coulomb, screened, cutoff, owners):
    blk_len = lax.axis_size("kblk")
    me = lax.axis_index("kring")
    my_y, my_z, my_c = place(me)
    rows = jnp.concatenate([rows_x[0, 0], rows_d[0, 0]], axis=1)
    tile_rows, depth = rows.shape

    scaled_x = (elem_x[0, 0].astype(jnp.float32) * coulomb).astype(jnp.bfloat16)
    scaled_d = (elem_d[0, 0].astype(jnp.float32) * screened).astype(jnp.bfloat16)
    cut = cutoff[0, 0]
    cut_parts = jnp.stack([cut // 32, cut % 32]).astype(jnp.bfloat16)
    cut_parts = jnp.pad(cut_parts, ((0, 14), (0, tile_rows - cut.shape[0])))
    elem_t = jnp.concatenate([2 * scaled_x, -scaled_d], axis=1).T
    elem_t = jnp.concatenate([elem_t, cut_parts])
    near = send(elem_t, OTHER_CORE)

    far = send(rows, OTHER_HALF)
    near_rows = send(copy_after(rows, (elem_t,)), OTHER_CORE)
    own = [ring(held) for held in pair(rows, near_rows, OWN_CHAINS)]
    early = [chain[1] for chain in own]
    far = copy_after(far, early)
    far = [ring(held) for held in pair(far, send(far, OTHER_CORE), FAR_CHAINS)]


    partner = jnp.arange(4 * RING, dtype=jnp.int32)
    p_y, p_z, p_c = place(partner)

    def in_list(core):
        ahead = jnp.where(core == 0, my_y - p_y, p_y - my_y) % RING
        off = jnp.abs(p_c - core)
        has = jnp.where((ahead == 0) | (ahead == 4), off == 0, ahead < 4)
        return has, jnp.where(ahead == 0, 0, 2 * ahead - 1 + off)

    has_mine, spot_mine = in_list(my_c)
    _, spot_other = in_list(1 - my_c)
    listed = has_mine & (spot_mine == jnp.arange(RING, dtype=jnp.int32)[:, None])

    def cuts_of(elem, z):
        parts = elem[depth : depth + 2, : 4 * RING].astype(jnp.int32)
        row = parts[0] * 32 + parts[1]
        return jnp.sum(jnp.where(listed & (p_z == z), row[None, :], 0), axis=1)


    spot = jnp.where(has_mine, spot_mine, RING + spot_other) + 2 * RING * jnp.abs(p_z - my_z)
    dest = owners[0, 0, :, 0]
    same = (dest[:, None] == dest[None, :]) & (partner[None, :] < partner[:, None])
    slot_of = jnp.sum(same.astype(jnp.int32), axis=1)
    slots = jnp.arange(blk_len * CAP, dtype=jnp.int32)
    hit = slots[:, None] == (dest * CAP + slot_of)[None, :]
    pos = 4 * RING + jnp.sum(jnp.where(hit, (spot - 4 * RING)[None, :], 0), axis=1)

    parts = []
    for blocks, z in ((own, my_z), (far, 1 - my_z)):
        to_near = make_tiles(cuts_of(near, z), near, blocks)
        parts.append(make_tiles(cuts_of(elem_t, z), elem_t, blocks))
        parts.append(send(to_near, OTHER_CORE))
    outbox = make_outbox(pos, parts).reshape(blk_len, CAP, tile_rows, tile_rows)
    received = lax.all_to_all(outbox, "kblk", split_axis=0, concat_axis=0, tiled=True)
    return received[None, None]


def solution(mesh):
    in_specs = (
        P("kring", "kblk", None, None),
        P("kring", "kblk", None, None),
        P("kring", "kblk", None, None),
        P("kring", "kblk", None, None),
        P(),
        P(),
        P("kring", "kblk", None),
        P("kring", "kblk", None, None),
    )
    out_specs = P("kring", "kblk", None, None, None, None)
    return jax.shard_map(body, mesh=mesh, in_specs=in_specs, out_specs=out_specs, check_vma=False)
```

time: 613 us -> 165 us (0.27)
  starting transfers between devices: 368 us -> 82.5 us
  waiting for transfers between devices: 104 us -> 8.3 us
  local copies, waits for them, and re-layouts: 29.5 us -> 3.53 us
  other arithmetic: 23.8 us -> 3 us
  matrix products: 13.4 us -> 0 us
  Pallas kernels: 0 us -> 8.21 us
  blocking collectives: 65.8 us -> 57.7 us
    ppermute x62 -> x22, starting transfers between devices: 368 us -> 82.5 us  [send(): return lax.ppermute(x, 'kring', perm)]
    ppermute x62 -> x22, waiting for transfers between devices: 104 us -> 8.3 us  [send(): return lax.ppermute(x, 'kring', perm)]
    dynamic_slice x32 -> x0, local copies, waits for them, and re-layouts: 20.5 us -> none  [make_tile(): limit_g = cut_row[partner]]
    lt x32 -> x0, other arithmetic: 19.5 us -> none  [make_tile(): g_index < limit_g]
    dot_general x64 -> x0, matrix products: 13.4 us -> none  [the longest x32 7.39 us: make_tile(): lax.dot_general(scaled_x, masked, contract, preferred_element_type=jnp.fl...]
    pallas_call x0 -> x9, Pallas kernels: none -> 8.21 us  [the longest x4 7.3 us: make_tiles(): pl.pallas_call(kernel, out_shape=jax.ShapeDtypeStruct((RING, TILE, TILE),...]
    all_to_all x1, blocking collectives: 65.8 us -> 57.7 us  [body(): lax.all_to_all(outbox, 'kblk', split_axis=0, concat_axis=0, tiled=True)]
  transfers between devices with their start and end apart: 62 -> 22, of which waited for: 39 -> 2; matrix products, arithmetic and copies ran while one was open for 9% -> 0% of each run, Pallas kernels for 0% -> 4%
where the time goes in v2:
time: 165 us; the launch traced here: 164 us
  starting transfers between devices  82.5 us (50%)
  blocking collectives  57.7 us (35%)
  waiting for transfers between devices  8.3 us (5%)
  Pallas kernels  8.21 us (5%)
  local copies, waits for them, and re-layouts  3.53 us (2%)
  other arithmetic  3 us (2%)
    ppermute x22, starting transfers between devices, send(): return lax.ppermute(x, 'kring', perm)  82.5 us
    all_to_all x1, blocking collectives, body(): lax.all_to_all(outbox, 'kblk', split_axis=0, concat_axis=0, tiled=True)  57.7 us
    ppermute x22, waiting for transfers between devices, send(): return lax.ppermute(x, 'kring', perm)  8.3 us
    pallas_call x4, Pallas kernels, make_tiles(): pl.pallas_call(kernel, out_shape=jax.ShapeDtypeStruct((RING, TILE, TILE),...  7.3 us
    unnamed x9, local copies, waits for them, and re-layouts  3.47 us
  transfers between devices with their start and end apart: 22, of which 2 were waited for; matrix products, arithmetic and copies ran while one was open for 0% of the time, Pallas kernels for 4%

profile of v2, /device:TPU:1, one launch (start us, length us, event | category | flops | bytes accessed | tf_op | source)
XLA Modules:
  0.0 163.8 jit_solution(18291696321344161627)
XLA Ops:
  4.8 8.8 %collective-permute-start = (bf16[128,1536]{1,0:T(8,128)(2,1)S(1)}, bf16[128,1536]{1,0:T(8,128)(2,1)S(1)}, u32[]{:S(2)}, u32[]{:S(2)}) collective-permute-start(bf16[128,1536]{1,0:T(8,128)(2,1)S(1)} %shard_map.82), channel_id=1, source_target_pairs={{0,16},{16,0},{32,48},{48,32},{64,80},{80,64},{96,112},{112,96},{1... | collective-permute-start | bytes 1179656 | tf_op jit(solution)/shard_map/ppermute | solution.py:36
  13.6 5.3 %collective-permute-start.11 = (bf16[128,1536]{1,0:T(8,128)(2,1)S(1)}, bf16[128,1536]{1,0:T(8,128)(2,1)S(1)}, u32[]{:S(2)}, u32[]{:S(2)}) collective-permute-start(bf16[128,1536]{1,0:T(8,128)(2,1)S(1)} %pad_maximum_fusion.x_ref.a_ref), channel_id=1, source_target_pairs={{0,32},{16,48},{32,0},{48,16},{64,96},{80,112},{96,64},{112,80},{1... | collective-permute-start | bytes 1179656 | tf_op jit(solution)/shard_map/ppermute | solution.py:36
  18.9 5.1 %collective-permute-start.1 = (bf16[2,64,1536]{2,1,0:T(8,128)(2,1)S(1)}, bf16[2,64,1536]{2,1,0:T(8,128)(2,1)S(1)}, u32[]{:S(2)}, u32[]{:S(2)}) collective-permute-start(bf16[2,64,1536]{2,1,0:T(8,128)(2,1)S(1)} %get-tuple-element.9.refs_2_), channel_id=1, source_target_pairs={{0,64},{16,464},{32,96},{48,496},{64,128},{80,16},{96,160},{112,48... | collective-permute-start | bytes 1179656 | tf_op jit(solution)/shard_map/ppermute | solution.py:36
  24.0 3.0 %collective-permute-start.2 = (bf16[2,64,1536]{2,1,0:T(8,128)(2,1)S(1)}, bf16[2,64,1536]{2,1,0:T(8,128)(2,1)S(1)}, u32[]{:S(2)}, u32[]{:S(2)}) collective-permute-start(bf16[2,64,1536]{2,1,0:T(8,128)(2,1)S(1)} %get-tuple-element.10.refs_3_), channel_id=1, source_target_pairs={{0,64},{16,464},{32,96},{48,496},{64,128},{80,16},{96,160},{112,48... | collective-permute-start | bytes 1179656 | tf_op jit(solution)/shard_map/ppermute | solution.py:36
  27.0 6.9 %collective-permute-done.11.x_ref = bf16[128,1536]{1,0:T(8,128)(2,1)S(1)} collective-permute-done((bf16[128,1536]{1,0:T(8,128)(2,1)S(1)}, bf16[128,1536]{1,0:T(8,128)(2,1)S(1)}, u32[]{:S(2)}, u32[]{:S(2)}) %collective-permute-start.11) | collective-permute-done | bytes 393248 | tf_op jit(solution)/shard_map/ppermute | solution.py:36
  34.0 2.8 %collective-permute-start.12 = (bf16[128,1536]{1,0:T(8,128)(2,1)S(1)}, bf16[128,1536]{1,0:T(8,128)(2,1)S(1)}, u32[]{:S(2)}, u32[]{:S(2)}) collective-permute-start(bf16[128,1536]{1,0:T(8,128)(2,1)S(1)} %shard_map.86.a_ref), channel_id=1, source_target_pairs={{0,16},{16,0},{32,48},{48,32},{64,80},{80,64},{96,112},{112,96},{1... | collective-permute-start | bytes 1179656 | tf_op jit(solution)/shard_map/ppermute | solution.py:36
  38.2 3.5 %collective-permute-start.13 = (bf16[2,64,1536]{2,1,0:T(8,128)(2,1)S(1)}, bf16[2,64,1536]{2,1,0:T(8,128)(2,1)S(1)}, u32[]{:S(2)}, u32[]{:S(2)}) collective-permute-start(bf16[2,64,1536]{2,1,0:T(8,128)(2,1)S(1)} %get-tuple-element.11.refs_2_), channel_id=1, source_target_pairs={{0,64},{16,464},{32,96},{48,496},{64,128},{80,16},{96,160},{112,48... | collective-permute-start | bytes 1179656 | tf_op jit(solution)/shard_map/ppermute | solution.py:36
  41.7 2.8 %collective-permute-start.14 = (bf16[2,64,1536]{2,1,0:T(8,128)(2,1)S(1)}, bf16[2,64,1536]{2,1,0:T(8,128)(2,1)}, u32[]{:S(2)}, u32[]{:S(2)}) collective-permute-start(bf16[2,64,1536]{2,1,0:T(8,128)(2,1)S(1)} %get-tuple-element.12.refs_3_), channel_id=1, source_target_pairs={{0,64},{16,464},{32,96},{48,496},{64,128},{80,16},{96,160},{112,48... | collective-permute-start | bytes 1179656 | tf_op jit(solution)/shard_map/ppermute | solution.py:36
  44.5 1.9 %collective-permute-start.9 = (bf16[1552,128]{1,0:T(8,128)(2,1)S(1)}, bf16[1552,128]{1,0:T(8,128)(2,1)S(1)}, u32[]{:S(2)}, u32[]{:S(2)}) collective-permute-start(bf16[1552,128]{1,0:T(8,128)(2,1)S(1)} %fusion.2.refs_0_.refs_1_), channel_id=1, source_target_pairs={{0,16},{16,0},{32,48},{48,32},{64,80},{80,64},{96,112},{112,96},{1... | collective-permute-start | bytes 1191944 | tf_op jit(solution)/shard_map/ppermute | solution.py:36
  46.7 3.0 %collective-permute-start.3 = (bf16[2,64,1536]{2,1,0:T(8,128)(2,1)S(1)}, bf16[2,64,1536]{2,1,0:T(8,128)(2,1)S(1)}, u32[]{:S(2)}, u32[]{:S(2)}) collective-permute-start(bf16[2,64,1536]{2,1,0:T(8,128)(2,1)S(1)} %collective-permute-done.1.refs_4_.refs_0_), channel_id=1, source_target_pairs={{0,64},{16,464},{32,96},{48,496},{64,128},{80,16},{96,160},{112,48... | collective-permute-start | bytes 1179656 | tf_op jit(solution)/shard_map/ppermute | solution.py:36
  49.7 4.2 %collective-permute-start.4 = (bf16[2,64,1536]{2,1,0:T(8,128)(2,1)S(1)}, bf16[2,64,1536]{2,1,0:T(8,128)(2,1)S(1)}, u32[]{:S(2)}, u32[]{:S(2)}) collective-permute-start(bf16[2,64,1536]{2,1,0:T(8,128)(2,1)S(1)} %collective-permute-done.2.refs_5_.refs_1_), channel_id=1, source_target_pairs={{0,64},{16,464},{32,96},{48,496},{64,128},{80,16},{96,160},{112,48... | collective-permute-start | bytes 1179656 | tf_op jit(solution)/shard_map/ppermute | solution.py:36
  55.8 2.4 %collective-permute-start.16 = (bf16[2,64,1536]{2,1,0:T(8,128)(2,1)}, bf16[2,64,1536]{2,1,0:T(8,128)(2,1)S(1)}, u32[]{:S(2)}, u32[]{:S(2)}) collective-permute-start(bf16[2,64,1536]{2,1,0:T(8,128)(2,1)} %collective-permute-done.14.refs_5_), channel_id=1, source_target_pairs={{0,64},{16,464},{32,96},{48,496},{64,128},{80,16},{96,160},{112,48... | collective-permute-start | bytes 1179656 | tf_op jit(solution)/shard_map/ppermute | solution.py:36
  58.3 4.7 %collective-permute-start.5 = (bf16[2,64,1536]{2,1,0:T(8,128)(2,1)S(1)}, bf16[2,64,1536]{2,1,0:T(8,128)(2,1)S(1)}, u32[]{:S(2)}, u32[]{:S(2)}) collective-permute-start(bf16[2,64,1536]{2,1,0:T(8,128)(2,1)S(1)} %collective-permute-done.3.refs_6_), channel_id=1, source_target_pairs={{0,64},{16,464},{32,96},{48,496},{64,128},{80,16},{96,160},{112,48... | collective-permute-start | bytes 1179656 | tf_op jit(solution)/shard_map/ppermute | solution.py:36
  63.0 3.6 %collective-permute-start.6 = (bf16[2,64,1536]{2,1,0:T(8,128)(2,1)S(1)}, bf16[2,64,1536]{2,1,0:T(8,128)(2,1)S(1)}, u32[]{:S(2)}, u32[]{:S(2)}) collective-permute-start(bf16[2,64,1536]{2,1,0:T(8,128)(2,1)S(1)} %collective-permute-done.4.refs_7_), channel_id=1, source_target_pairs={{0,64},{16,464},{32,96},{48,496},{64,128},{80,16},{96,160},{112,48... | collective-permute-start | bytes 1179656 | tf_op jit(solution)/shard_map/ppermute | solution.py:36
  68.6 3.8 %collective-permute-start.18 = (bf16[2,64,1536]{2,1,0:T(8,128)(2,1)S(1)}, bf16[2,64,1536]{2,1,0:T(8,128)(2,1)S(1)}, u32[]{:S(2)}, u32[]{:S(2)}) collective-permute-start(bf16[2,64,1536]{2,1,0:T(8,128)(2,1)S(1)} %collective-permute-done.16.refs_7_), channel_id=1, source_target_pairs={{0,64},{16,464},{32,96},{48,496},{64,128},{80,16},{96,160},{112,48... | collective-permute-start | bytes 1179656 | tf_op jit(solution)/shard_map/ppermute | solution.py:36
  72.6 4.1 %collective-permute-start.7 = (bf16[1,64,1536]{2,1,0:T(8,128)(2,1)S(1)}, bf16[1,64,1536]{2,1,0:T(8,128)(2,1)S(1)}, u32[]{:S(2)}, u32[]{:S(2)}) collective-permute-start(bf16[1,64,1536]{2,1,0:T(8,128)(2,1)S(1)} %slice.43), channel_id=1, source_target_pairs={{0,64},{16,464},{32,96},{48,496},{64,128},{80,16},{96,160},{112,48... | collective-permute-start | bytes 589832 | tf_op jit(solution)/shard_map/ppermute | solution.py:36
  76.7 4.2 %collective-permute-start.8 = (bf16[1,64,1536]{2,1,0:T(8,128)(2,1)S(1)}, bf16[1,64,1536]{2,1,0:T(8,128)(2,1)S(1)}, u32[]{:S(2)}, u32[]{:S(2)}) collective-permute-start(bf16[1,64,1536]{2,1,0:T(8,128)(2,1)S(1)} %slice.44), channel_id=1, source_target_pairs={{0,64},{16,464},{32,96},{48,496},{64,128},{80,16},{96,160},{112,48... | collective-permute-start | bytes 589832 | tf_op jit(solution)/shard_map/ppermute | solution.py:36
  81.0 4.2 %collective-permute-start.19 = (bf16[1,64,1536]{2,1,0:T(8,128)(2,1)S(1)}, bf16[1,64,1536]{2,1,0:T(8,128)(2,1)S(1)}, u32[]{:S(2)}, u32[]{:S(2)}) collective-permute-start(bf16[1,64,1536]{2,1,0:T(8,128)(2,1)S(1)} %slice.46), channel_id=1, source_target_pairs={{0,64},{16,464},{32,96},{48,496},{64,128},{80,16},{96,160},{112,48... | collective-permute-start | bytes 589832 | tf_op jit(solution)/shard_map/ppermute | solution.py:36
  85.2 4.2 %collective-permute-start.20 = (bf16[1,64,1536]{2,1,0:T(8,128)(2,1)S(1)}, bf16[1,64,1536]{2,1,0:T(8,128)(2,1)S(1)}, u32[]{:S(2)}, u32[]{:S(2)}) collective-permute-start(bf16[1,64,1536]{2,1,0:T(8,128)(2,1)S(1)} %slice.47), channel_id=1, source_target_pairs={{0,64},{16,464},{32,96},{48,496},{64,128},{80,16},{96,160},{112,48... | collective-permute-start | bytes 589832 | tf_op jit(solution)/shard_map/ppermute | solution.py:36
  91.1 4.2 %collective-permute-start.10 = (bf16[8,128,128]{2,1,0:T(8,128)(2,1)S(1)}, bf16[8,128,128]{2,1,0:T(8,128)(2,1)S(1)}, u32[]{:S(2)}, u32[]{:S(2)}) collective-permute-start(bf16[8,128,128]{2,1,0:T(8,128)(2,1)S(1)} %shard_map.85), channel_id=1, source_target_pairs={{0,16},{16,0},{32,48},{48,32},{64,80},{80,64},{96,112},{112,96},{1... | collective-permute-start | bytes 786440 | tf_op jit(solution)/shard_map/ppermute | solution.py:36
  95.3 2.1 %shard_map.89 = bf16[8,128,128]{2,1,0:T(8,128)(2,1)S(1)} custom-call(s32[8]{0:T(128)S(1)} %get-tuple-element.13.refs_0_, bf16[1552,128]{1,0:T(8,128)(2,1)S(1)} %collective-permute-done.9.refs_1_, bf16[2,64,1536]{2,1,0:T(8,128)(2,1)S(1)} %get-tuple-element.11.refs_2_, bf16[2,64,1536]{2,1,0:T(8,128)(2,1)S(1)} %get-tuple-element.12.refs_3_, ...), custom_call_target="tpu_custom_call" | custom-call | flops 402653184 | bytes 3145728 | tf_op jit(solution)/shard_map/pallas_call | solution.py:70
  97.4 3.0 %collective-permute-start.21 = (bf16[8,128,128]{2,1,0:T(8,128)(2,1)S(1)}, bf16[8,128,128]{2,1,0:T(8,128)(2,1)S(1)}, u32[]{:S(2)}, u32[]{:S(2)}) collective-permute-start(bf16[8,128,128]{2,1,0:T(8,128)(2,1)S(1)} %shard_map.89), channel_id=1, source_target_pairs={{0,16},{16,0},{32,48},{48,32},{64,80},{80,64},{96,112},{112,96},{1... | collective-permute-start | bytes 786440 | tf_op jit(solution)/shard_map/ppermute | solution.py:36
  102.0 2.1 %shard_map.88.refs_2_ = bf16[8,128,128]{2,1,0:T(8,128)(2,1)S(1)} custom-call(s32[8]{0:T(128)S(1)} %get-tuple-element.14.refs_0_, bf16[1552,128]{1,0:T(8,128)(2,1)S(1)} %fusion.2.refs_0_.refs_1_, bf16[2,64,1536]{2,1,0:T(8,128)(2,1)S(1)} %get-tuple-element.11.refs_2_, bf16[2,64,1536]{2,1,0:T(8,128)(2,1)S(1)} %get-tuple-element.12.refs_3_, ...), custom_call_target="tpu_custom_call" | custom-call | flops 402653184 | bytes 3145728 | tf_op jit(solution)/shard_map/pallas_call | solution.py:70
  104.8 57.7 %all_to_all.5 = bf16[16,4,128,128]{3,2,1,0:T(8,128)(2,1)S(1)} all-to-all(bf16[16,4,128,128]{3,2,1,0:T(8,128)(2,1)S(1)} %bitcast.35), channel_id=1, replica_groups=mesh['kring'=32,'kblk'=16] {'kblk'}, dimensions={0} | all-to-all | bytes 4194304 | tf_op jit(solution)/shard_map/all_to_all | solution.py:212
  (60 shorter events, 15.8 us)
Async XLA Ops:
  0.0 4.7 %copy-start = (bf16[1,1,128,1024]{3,2,1,0:T(8,128)(2,1)S(1)}, bf16[1,1,128,1024]{3,2,1,0:T(8,128)(2,1)}, u32[]{:S(2)}) copy-start(bf16[1,1,128,1024]{3,2,1,0:T(8,128)(2,1)} %param.10) | copy-start | bytes 786436
  4.7 41.8 %copy-start.2 = (s32[1,1,32,1]{2,3,1,0:T(1,128)S(1)}, s32[1,1,32,1]{2,3,1,0:T(1,128)}, u32[]{:S(2)}) copy-start(s32[1,1,32,1]{2,3,1,0:T(1,128)} %param.15) | copy-start | bytes 388
  4.8 14.1 %collective-permute-start = (bf16[128,1536]{1,0:T(8,128)(2,1)S(1)}, bf16[128,1536]{1,0:T(8,128)(2,1)S(1)}, u32[]{:S(2)}, u32[]{:S(2)}) collective-permute-start(bf16[128,1536]{1,0:T(8,128)(2,1)S(1)} %shard_map.82), channel_id=1, source_target_pairs={{0,16},{16,0},{32,48},{48,32},{64,80},{80,64},{96,112},{112,96},{1... | collective-permute-start | bytes 1179656 | tf_op jit(solution)/shard_map/ppermute | solution.py:36
  13.6 20.4 %collective-permute-start.11 = (bf16[128,1536]{1,0:T(8,128)(2,1)S(1)}, bf16[128,1536]{1,0:T(8,128)(2,1)S(1)}, u32[]{:S(2)}, u32[]{:S(2)}) collective-permute-start(bf16[128,1536]{1,0:T(8,128)(2,1)S(1)} %pad_maximum_fusion.x_ref.a_ref), channel_id=1, source_target_pairs={{0,32},{16,48},{32,0},{48,16},{64,96},{80,112},{96,64},{112,80},{1... | collective-permute-start | bytes 1179656 | tf_op jit(solution)/shard_map/ppermute | solution.py:36
  18.9 15.0 %collective-permute-start.1 = (bf16[2,64,1536]{2,1,0:T(8,128)(2,1)S(1)}, bf16[2,64,1536]{2,1,0:T(8,128)(2,1)S(1)}, u32[]{:S(2)}, u32[]{:S(2)}) collective-permute-start(bf16[2,64,1536]{2,1,0:T(8,128)(2,1)S(1)} %get-tuple-element.9.refs_2_), channel_id=1, source_target_pairs={{0,64},{16,464},{32,96},{48,496},{64,128},{80,16},{96,160},{112,48... | collective-permute-start | bytes 1179656 | tf_op jit(solution)/shard_map/ppermute | solution.py:36
  24.0 9.9 %collective-permute-start.2 = (bf16[2,64,1536]{2,1,0:T(8,128)(2,1)S(1)}, bf16[2,64,1536]{2,1,0:T(8,128)(2,1)S(1)}, u32[]{:S(2)}, u32[]{:S(2)}) collective-permute-start(bf16[2,64,1536]{2,1,0:T(8,128)(2,1)S(1)} %get-tuple-element.10.refs_3_), channel_id=1, source_target_pairs={{0,64},{16,464},{32,96},{48,496},{64,128},{80,16},{96,160},{112,48... | collective-permute-start | bytes 1179656 | tf_op jit(solution)/shard_map/ppermute | solution.py:36
  34.0 4.2 %collective-permute-start.12 = (bf16[128,1536]{1,0:T(8,128)(2,1)S(1)}, bf16[128,1536]{1,0:T(8,128)(2,1)S(1)}, u32[]{:S(2)}, u32[]{:S(2)}) collective-permute-start(bf16[128,1536]{1,0:T(8,128)(2,1)S(1)} %shard_map.86.a_ref), channel_id=1, source_target_pairs={{0,16},{16,0},{32,48},{48,32},{64,80},{80,64},{96,112},{112,96},{1... | collective-permute-start | bytes 1179656 | tf_op jit(solution)/shard_map/ppermute | solution.py:36
  38.2 15.7 %collective-permute-start.13 = (bf16[2,64,1536]{2,1,0:T(8,128)(2,1)S(1)}, bf16[2,64,1536]{2,1,0:T(8,128)(2,1)S(1)}, u32[]{:S(2)}, u32[]{:S(2)}) collective-permute-start(bf16[2,64,1536]{2,1,0:T(8,128)(2,1)S(1)} %get-tuple-element.11.refs_2_), channel_id=1, source_target_pairs={{0,64},{16,464},{32,96},{48,496},{64,128},{80,16},{96,160},{112,48... | collective-permute-start | bytes 1179656 | tf_op jit(solution)/shard_map/ppermute | solution.py:36
  41.7 14.2 %collective-permute-start.14 = (bf16[2,64,1536]{2,1,0:T(8,128)(2,1)S(1)}, bf16[2,64,1536]{2,1,0:T(8,128)(2,1)}, u32[]{:S(2)}, u32[]{:S(2)}) collective-permute-start(bf16[2,64,1536]{2,1,0:T(8,128)(2,1)S(1)} %get-tuple-element.12.refs_3_), channel_id=1, source_target_pairs={{0,64},{16,464},{32,96},{48,496},{64,128},{80,16},{96,160},{112,48... | collective-permute-start | bytes 1179656 | tf_op jit(solution)/shard_map/ppermute | solution.py:36
  44.5 28.1 %collective-permute-start.9 = (bf16[1552,128]{1,0:T(8,128)(2,1)S(1)}, bf16[1552,128]{1,0:T(8,128)(2,1)S(1)}, u32[]{:S(2)}, u32[]{:S(2)}) collective-permute-start(bf16[1552,128]{1,0:T(8,128)(2,1)S(1)} %fusion.2.refs_0_.refs_1_), channel_id=1, source_target_pairs={{0,16},{16,0},{32,48},{48,32},{64,80},{80,64},{96,112},{112,96},{1... | collective-permute-start | bytes 1191944 | tf_op jit(solution)/shard_map/ppermute | solution.py:36
  46.7 11.6 %collective-permute-start.3 = (bf16[2,64,1536]{2,1,0:T(8,128)(2,1)S(1)}, bf16[2,64,1536]{2,1,0:T(8,128)(2,1)S(1)}, u32[]{:S(2)}, u32[]{:S(2)}) collective-permute-start(bf16[2,64,1536]{2,1,0:T(8,128)(2,1)S(1)} %collective-permute-done.1.refs_4_.refs_0_), channel_id=1, source_target_pairs={{0,64},{16,464},{32,96},{48,496},{64,128},{80,16},{96,160},{112,48... | collective-permute-start | bytes 1179656 | tf_op jit(solution)/shard_map/ppermute | solution.py:36
  49.7 13.3 %collective-permute-start.4 = (bf16[2,64,1536]{2,1,0:T(8,128)(2,1)S(1)}, bf16[2,64,1536]{2,1,0:T(8,128)(2,1)S(1)}, u32[]{:S(2)}, u32[]{:S(2)}) collective-permute-start(bf16[2,64,1536]{2,1,0:T(8,128)(2,1)S(1)} %collective-permute-done.2.refs_5_.refs_1_), channel_id=1, source_target_pairs={{0,64},{16,464},{32,96},{48,496},{64,128},{80,16},{96,160},{112,48... | collective-permute-start | bytes 1179656 | tf_op jit(solution)/shard_map/ppermute | solution.py:36
  53.9 12.8 %collective-permute-start.15 = (bf16[2,64,1536]{2,1,0:T(8,128)(2,1)S(1)}, bf16[2,64,1536]{2,1,0:T(8,128)(2,1)S(1)}, u32[]{:S(2)}, u32[]{:S(2)}) collective-permute-start(bf16[2,64,1536]{2,1,0:T(8,128)(2,1)S(1)} %collective-permute-done.13.refs_4_), channel_id=1, source_target_pairs={{0,64},{16,464},{32,96},{48,496},{64,128},{80,16},{96,160},{112,48... | collective-permute-start | bytes 1179656 | tf_op jit(solution)/shard_map/ppermute | solution.py:36
  55.8 12.8 %collective-permute-start.16 = (bf16[2,64,1536]{2,1,0:T(8,128)(2,1)}, bf16[2,64,1536]{2,1,0:T(8,128)(2,1)S(1)}, u32[]{:S(2)}, u32[]{:S(2)}) collective-permute-start(bf16[2,64,1536]{2,1,0:T(8,128)(2,1)} %collective-permute-done.14.refs_5_), channel_id=1, source_target_pairs={{0,64},{16,464},{32,96},{48,496},{64,128},{80,16},{96,160},{112,48... | collective-permute-start | bytes 1179656 | tf_op jit(solution)/shard_map/ppermute | solution.py:36
  58.3 14.3 %collective-permute-start.5 = (bf16[2,64,1536]{2,1,0:T(8,128)(2,1)S(1)}, bf16[2,64,1536]{2,1,0:T(8,128)(2,1)S(1)}, u32[]{:S(2)}, u32[]{:S(2)}) collective-permute-start(bf16[2,64,1536]{2,1,0:T(8,128)(2,1)S(1)} %collective-permute-done.3.refs_6_), channel_id=1, source_target_pairs={{0,64},{16,464},{32,96},{48,496},{64,128},{80,16},{96,160},{112,48... | collective-permute-start | bytes 1179656 | tf_op jit(solution)/shard_map/ppermute | solution.py:36
  63.0 13.7 %collective-permute-start.6 = (bf16[2,64,1536]{2,1,0:T(8,128)(2,1)S(1)}, bf16[2,64,1536]{2,1,0:T(8,128)(2,1)S(1)}, u32[]{:S(2)}, u32[]{:S(2)}) collective-permute-start(bf16[2,64,1536]{2,1,0:T(8,128)(2,1)S(1)} %collective-permute-done.4.refs_7_), channel_id=1, source_target_pairs={{0,64},{16,464},{32,96},{48,496},{64,128},{80,16},{96,160},{112,48... | collective-permute-start | bytes 1179656 | tf_op jit(solution)/shard_map/ppermute | solution.py:36
  66.7 14.2 %collective-permute-start.17 = (bf16[2,64,1536]{2,1,0:T(8,128)(2,1)S(1)}, bf16[2,64,1536]{2,1,0:T(8,128)(2,1)S(1)}, u32[]{:S(2)}, u32[]{:S(2)}) collective-permute-start(bf16[2,64,1536]{2,1,0:T(8,128)(2,1)S(1)} %collective-permute-done.15.refs_6_), channel_id=1, source_target_pairs={{0,64},{16,464},{32,96},{48,496},{64,128},{80,16},{96,160},{112,48... | collective-permute-start | bytes 1179656 | tf_op jit(solution)/shard_map/ppermute | solution.py:36
  68.6 16.5 %collective-permute-start.18 = (bf16[2,64,1536]{2,1,0:T(8,128)(2,1)S(1)}, bf16[2,64,1536]{2,1,0:T(8,128)(2,1)S(1)}, u32[]{:S(2)}, u32[]{:S(2)}) collective-permute-start(bf16[2,64,1536]{2,1,0:T(8,128)(2,1)S(1)} %collective-permute-done.16.refs_7_), channel_id=1, source_target_pairs={{0,64},{16,464},{32,96},{48,496},{64,128},{80,16},{96,160},{112,48... | collective-permute-start | bytes 1179656 | tf_op jit(solution)/shard_map/ppermute | solution.py:36
  72.6 16.9 %collective-permute-start.7 = (bf16[1,64,1536]{2,1,0:T(8,128)(2,1)S(1)}, bf16[1,64,1536]{2,1,0:T(8,128)(2,1)S(1)}, u32[]{:S(2)}, u32[]{:S(2)}) collective-permute-start(bf16[1,64,1536]{2,1,0:T(8,128)(2,1)S(1)} %slice.43), channel_id=1, source_target_pairs={{0,64},{16,464},{32,96},{48,496},{64,128},{80,16},{96,160},{112,48... | collective-permute-start | bytes 589832 | tf_op jit(solution)/shard_map/ppermute | solution.py:36
  76.7 12.8 %collective-permute-start.8 = (bf16[1,64,1536]{2,1,0:T(8,128)(2,1)S(1)}, bf16[1,64,1536]{2,1,0:T(8,128)(2,1)S(1)}, u32[]{:S(2)}, u32[]{:S(2)}) collective-permute-start(bf16[1,64,1536]{2,1,0:T(8,128)(2,1)S(1)} %slice.44), channel_id=1, source_target_pairs={{0,64},{16,464},{32,96},{48,496},{64,128},{80,16},{96,160},{112,48... | collective-permute-start | bytes 589832 | tf_op jit(solution)/shard_map/ppermute | solution.py:36
  81.0 14.4 %collective-permute-start.19 = (bf16[1,64,1536]{2,1,0:T(8,128)(2,1)S(1)}, bf16[1,64,1536]{2,1,0:T(8,128)(2,1)S(1)}, u32[]{:S(2)}, u32[]{:S(2)}) collective-permute-start(bf16[1,64,1536]{2,1,0:T(8,128)(2,1)S(1)} %slice.46), channel_id=1, source_target_pairs={{0,64},{16,464},{32,96},{48,496},{64,128},{80,16},{96,160},{112,48... | collective-permute-start | bytes 589832 | tf_op jit(solution)/shard_map/ppermute | solution.py:36
  85.2 10.1 %collective-permute-start.20 = (bf16[1,64,1536]{2,1,0:T(8,128)(2,1)S(1)}, bf16[1,64,1536]{2,1,0:T(8,128)(2,1)S(1)}, u32[]{:S(2)}, u32[]{:S(2)}) collective-permute-start(bf16[1,64,1536]{2,1,0:T(8,128)(2,1)S(1)} %slice.47), channel_id=1, source_target_pairs={{0,64},{16,464},{32,96},{48,496},{64,128},{80,16},{96,160},{112,48... | collective-permute-start | bytes 589832 | tf_op jit(solution)/shard_map/ppermute | solution.py:36
  91.1 12.9 %collective-permute-start.10 = (bf16[8,128,128]{2,1,0:T(8,128)(2,1)S(1)}, bf16[8,128,128]{2,1,0:T(8,128)(2,1)S(1)}, u32[]{:S(2)}, u32[]{:S(2)}) collective-permute-start(bf16[8,128,128]{2,1,0:T(8,128)(2,1)S(1)} %shard_map.85), channel_id=1, source_target_pairs={{0,16},{16,0},{32,48},{48,32},{64,80},{80,64},{96,112},{112,96},{1... | collective-permute-start | bytes 786440 | tf_op jit(solution)/shard_map/ppermute | solution.py:36
  97.4 6.6 %collective-permute-start.21 = (bf16[8,128,128]{2,1,0:T(8,128)(2,1)S(1)}, bf16[8,128,128]{2,1,0:T(8,128)(2,1)S(1)}, u32[]{:S(2)}, u32[]{:S(2)}) collective-permute-start(bf16[8,128,128]{2,1,0:T(8,128)(2,1)S(1)} %shard_map.89), channel_id=1, source_target_pairs={{0,16},{16,0},{32,48},{48,32},{64,80},{80,64},{96,112},{112,96},{1... | collective-permute-start | bytes 786440 | tf_op jit(solution)/shard_map/ppermute | solution.py:36
  (1 other events, 4.7 us)

commit v3 on v2

v3 whole, which is shorter than its diff:
```python
import functools

import jax
import jax.numpy as jnp
from jax import lax
from jax.experimental import pallas as pl
from jax.experimental.pallas import tpu as pltpu
from jax.sharding import PartitionSpec as P

CAP = 4
RING = 8
TILE = 128
G_COUNT = 1024
CHAINS = 2
STEPS = ((0, 1, 2, 3, 4),)


def place(i):
    return i // 4, (i // 2) % 2, i % 2


def index(y, z, c):
    return ((y % RING) * 2 + z) * 2 + c


def pairs(move):
    return [(i, index(*move(*place(i)))) for i in range(4 * RING)]


OTHER_CORE = pairs(lambda y, z, c: (y, z, 1 - c))
OTHER_HALF = pairs(lambda y, z, c: (y, 1 - z, c))
OTHER_BOTH = pairs(lambda y, z, c: (y, 1 - z, 1 - c))
ONWARD = pairs(lambda y, z, c: (y + 1 - 2 * c, z, c))


def send(x, perm):
    return lax.ppermute(x, "kring", perm)


def tiles_kernel(parts, cut_ref, elem_a, elem_b, *refs):
    *block_refs, out_a, out_b, masked, total = refs
    depth = masked.shape[2]
    lane = lax.broadcasted_iota(jnp.int32, (16, G_COUNT), 1)
    for e, (elem_ref, out_ref) in enumerate(((elem_a, out_a), (elem_b, out_b))):
        for at, (spot, sources, k) in enumerate(parts):
            keep = (lane < cut_ref[e, spot]).astype(jnp.float32).astype(jnp.bfloat16)
            for n, source in enumerate(sources):
                ref = block_refs[source]
                rows = ref.shape[1]
                part = ref[k, :, :G_COUNT].reshape(rows // 16, 16, G_COUNT) * keep[None]
                span = pl.ds(at * TILE + n * rows, rows)
                masked[e, span, :G_COUNT] = part.reshape(rows, G_COUNT)
                masked[e, span, G_COUNT:] = ref[k, :, G_COUNT:]
        total[e] = jnp.dot(masked[e], elem_ref[:depth, :], preferred_element_type=jnp.float32)
        for at in range(len(parts)):
            out_ref[at] = total[e, pl.ds(at * TILE, TILE), :].T.astype(jnp.bfloat16)


def make_tiles(cuts, elem_a, elem_b, chains, steps, after=()):
    depth = chains[0][0].shape[2]
    flat, parts = [], []
    for step in steps:
        sources = list(range(len(flat), len(flat) + len(chains)))
        flat += [chain[step] for chain in chains]
        for k in range(1 if step in (0, RING // 2) else 2):
            parts.append((max(0, 2 * step - 1) + k, sources, k))
    vmem = pl.BlockSpec(memory_space=pltpu.VMEM)
    free = pl.BlockSpec(memory_space=pl.ANY)
    count = len(parts)
    shape = jax.ShapeDtypeStruct((count, TILE, TILE), jnp.bfloat16)

    def kernel(*refs):
        tiles_kernel(parts, *refs[: 3 + len(flat)], *refs[3 + len(flat) + len(after) :])

    return pl.pallas_call(
        kernel,
        out_shape=(shape, shape),
        in_specs=[pl.BlockSpec(memory_space=pltpu.SMEM)] + [vmem] * (2 + len(flat)) + [free] * len(after),
        out_specs=(vmem, vmem),
        scratch_shapes=[
            pltpu.VMEM((2, count * TILE, depth), jnp.bfloat16),
            pltpu.VMEM((2, count * TILE, TILE), jnp.float32),
        ],
        compiler_params=pltpu.CompilerParams(vmem_limit_bytes=24 << 20),
        cost_estimate=pl.CostEstimate(
            flops=4 * count * TILE * depth * TILE, bytes_accessed=2 * count * TILE * depth, transcendentals=0
        ),
    )(cuts, elem_a, elem_b, *flat, *after)


def pair_kernel(pieces, a_ref, b_ref, *refs):
    out_refs = refs[-pieces:]
    rows = out_refs[0].shape[1]
    for k, ref in enumerate(out_refs):
        ref[0] = a_ref[pl.ds(k * rows, rows), :]
        ref[1] = b_ref[pl.ds(k * rows, rows), :]


def pair(a, b, pieces, after=()):
    vmem = pl.BlockSpec(memory_space=pltpu.VMEM)
    free = pl.BlockSpec(memory_space=pl.ANY)
    shape = jax.ShapeDtypeStruct((2, a.shape[0] // pieces, a.shape[1]), a.dtype)
    return pl.pallas_call(
        functools.partial(pair_kernel, pieces),
        out_shape=(shape,) * pieces,
        in_specs=[vmem, vmem] + [free] * len(after),
        out_specs=(vmem,) * pieces,
        compiler_params=pltpu.CompilerParams(vmem_limit_bytes=8 << 20),
    )(a, b, *after)


def outbox_kernel(pos_ref, *refs):
    *in_refs, out_ref, held = refs
    at = 0
    for ref in in_refs:
        held[at : at + ref.shape[0]] = ref[...]
        at += ref.shape[0]
    held[at] = jnp.zeros(held.shape[1:], held.dtype)
    for s in range(out_ref.shape[0]):
        out_ref[s] = held[pos_ref[s]]


def make_outbox(pos, parts):
    rows, width = parts[0].shape[1:]
    slots = pos.shape[0]
    vmem = pl.BlockSpec(memory_space=pltpu.VMEM)
    return pl.pallas_call(
        outbox_kernel,
        out_shape=jax.ShapeDtypeStruct((slots, rows, width), jnp.bfloat16),
        in_specs=[pl.BlockSpec(memory_space=pltpu.SMEM)] + [vmem] * len(parts),
        out_specs=vmem,
        scratch_shapes=[pltpu.VMEM((4 * RING + 1, rows, width), jnp.bfloat16)],
        compiler_params=pltpu.CompilerParams(vmem_limit_bytes=16 << 20),
    )(pos, *parts)


def copy_kernel(x_ref, *refs):
    refs[-1][...] = x_ref[...]


def copy_after(x, after):
    vmem = pl.BlockSpec(memory_space=pltpu.VMEM)
    free = pl.BlockSpec(memory_space=pl.ANY)
    return pl.pallas_call(
        copy_kernel,
        out_shape=jax.ShapeDtypeStruct(x.shape, x.dtype),
        in_specs=[vmem] + [free] * len(after),
        out_specs=vmem,
        compiler_params=pltpu.CompilerParams(vmem_limit_bytes=8 << 20),
    )(x, *after)


def ring(held):
    blocks = [held]
    for _ in range(RING // 2 - 1):
        held = send(held, ONWARD)
        blocks.append(held)
    return blocks + [send(held[:1], ONWARD)]


def body(elem_x, elem_d, rows_x, rows_d, coulomb, screened, cutoff, owners):
    blk_len = lax.axis_size("kblk")
    me = lax.axis_index("kring")
    my_y, my_z, my_c = place(me)
    rows = jnp.concatenate([rows_x[0, 0], rows_d[0, 0]], axis=1)
    tile_rows, depth = rows.shape

    chains = [ring(held) for held in pair(rows, send(rows, OTHER_CORE), CHAINS)]

    scaled_x = (elem_x[0, 0].astype(jnp.float32) * coulomb).astype(jnp.bfloat16)
    scaled_d = (elem_d[0, 0].astype(jnp.float32) * screened).astype(jnp.bfloat16)
    cut = cutoff[0, 0]
    cut_parts = jnp.stack([cut // 32, cut % 32]).astype(jnp.bfloat16)
    cut_parts = jnp.pad(cut_parts, ((0, 14), (0, tile_rows - cut.shape[0])))
    elem_t = jnp.concatenate([2 * scaled_x, -scaled_d], axis=1).T
    elem_t = jnp.concatenate([elem_t, cut_parts])
    far = send(elem_t, OTHER_HALF)
    far = copy_after(far, (chains[0][3],))
    far_near = send(far, OTHER_CORE)
    near = send(elem_t, OTHER_CORE)

    partner = jnp.arange(4 * RING, dtype=jnp.int32)
    p_y, p_z, p_c = place(partner)

    def in_list(core):
        ahead = jnp.where(core == 0, my_y - p_y, p_y - my_y) % RING
        off = jnp.abs(p_c - core)
        has = jnp.where((ahead == 0) | (ahead == 4), off == 0, ahead < 4)
        return has, jnp.where(ahead == 0, 0, 2 * ahead - 1 + off)

    has_mine, spot_mine = in_list(my_c)
    _, spot_other = in_list(1 - my_c)
    listed = has_mine & (p_z == my_z) & (spot_mine == jnp.arange(RING, dtype=jnp.int32)[:, None])

    def cuts_of(*elems):
        parts = jnp.stack([e[depth : depth + 2, : 4 * RING] for e in elems]).astype(jnp.int32)
        row = parts[:, 0] * 32 + parts[:, 1]
        return jnp.sum(jnp.where(listed[None], row[:, None, :], 0), axis=2)

    cuts_far, cuts_near = cuts_of(far, far_near), cuts_of(elem_t, near)

    spot = jnp.where(has_mine, spot_mine, RING + spot_other) + 2 * RING * jnp.abs(p_z - my_z)
    dest = owners[0, 0, :, 0]
    same = (dest[:, None] == dest[None, :]) & (partner[None, :] < partner[:, None])
    slot_of = jnp.sum(same.astype(jnp.int32), axis=1)
    slots = jnp.arange(blk_len * CAP, dtype=jnp.int32)
    hit = slots[:, None] == (dest * CAP + slot_of)[None, :]
    pos = 4 * RING + jnp.sum(jnp.where(hit, (spot - 4 * RING)[None, :], 0), axis=1)

    from_far, from_far_near, after = [], [], ()
    for steps in STEPS:
        to_far, to_far_near = make_tiles(cuts_far, far, far_near, chains, steps, after)
        from_far.append(send(to_far, OTHER_HALF))
        from_far_near.append(send(to_far_near, OTHER_BOTH))
        after = from_far[-1:]
    mine, to_near = make_tiles(cuts_near, elem_t, near, chains, range(RING // 2 + 1), (to_far,))
    parts = [mine, send(to_near, OTHER_CORE)] + from_far + from_far_near
    outbox = make_outbox(pos, parts).reshape(blk_len, CAP, tile_rows, tile_rows)
    received = lax.all_to_all(outbox, "kblk", split_axis=0, concat_axis=0, tiled=True)
    return received[None, None]


def solution(mesh):
    in_specs = (
        P("kring", "kblk", None, None),
        P("kring", "kblk", None, None),
        P("kring", "kblk", None, None),
        P("kring", "kblk", None, None),
        P(),
        P(),
        P("kring", "kblk", None),
        P("kring", "kblk", None, None),
    )
    out_specs = P("kring", "kblk", None, None, None, None)
    return jax.shard_map(body, mesh=mesh, in_specs=in_specs, out_specs=out_specs, check_vma=False)
```

time: 165 us -> 154 us (0.933)
  starting transfers between devices: 82.5 us -> 65.9 us
  waiting for transfers between devices: 8.3 us -> 14.8 us
  Pallas kernels: 8.21 us -> 5.71 us
    ppermute x22 -> x15, starting transfers between devices: 82.5 us -> 65.9 us  [send(): return lax.ppermute(x, 'kring', perm)]
    ppermute x22 -> x15, waiting for transfers between devices: 8.3 us -> 14.8 us  [send(): return lax.ppermute(x, 'kring', perm)]
    pallas_call x4 -> x2, Pallas kernels: 7.3 us -> 4.88 us  [make_tiles(): pl.pallas_call(kernel, out_shape=(shape, shape), in_specs=[pl.BlockSpec(m...]
    unnamed x9 -> x7, local copies, waits for them, and re-layouts: 3.47 us -> 3.47 us
  transfers between devices with their start and end apart: 22 -> 15, of which waited for: 2 -> 6; matrix products, arithmetic and copies ran while one was open for 0% -> 3% of each run, Pallas kernels for 4% -> 2%
where the time goes in v3:
time: 154 us; the launch traced here: 152 us
  starting transfers between devices  65.9 us (43%)
  blocking collectives  58.6 us (38%)
  waiting for transfers between devices  14.8 us (10%)
  Pallas kernels  5.71 us (4%)
  local copies, waits for them, and re-layouts  3.51 us (2%)
  other arithmetic  3.36 us (2%)
    ppermute x15, starting transfers between devices, send(): return lax.ppermute(x, 'kring', perm)  65.9 us
    all_to_all x1, blocking collectives, body(): lax.all_to_all(outbox, 'kblk', split_axis=0, concat_axis=0, tiled=True)  58.6 us
    ppermute x15, waiting for transfers between devices, send(): return lax.ppermute(x, 'kring', perm)  14.8 us
    pallas_call x2, Pallas kernels, make_tiles(): pl.pallas_call(kernel, out_shape=(shape, shape), in_specs=[pl.BlockSpec(m...  4.88 us
    unnamed x7, local copies, waits for them, and re-layouts  3.47 us
  transfers between devices with their start and end apart: 15, of which 6 were waited for; matrix products, arithmetic and copies ran while one was open for 3% of the time, Pallas kernels for 2%

profile of v3, /device:TPU:1, one launch (start us, length us, event | category | flops | bytes accessed | tf_op | source)
XLA Modules:
  0.0 152.3 jit_solution(6811108360706735127)
XLA Ops:
  1.1 8.8 %collective-permute-start.1 = (bf16[128,1536]{1,0:T(8,128)(2,1)S(1)}, bf16[128,1536]{1,0:T(8,128)(2,1)S(1)}, u32[]{:S(2)}, u32[]{:S(2)}) collective-permute-start(bf16[128,1536]{1,0:T(8,128)(2,1)S(1)} %pad_maximum_fusion.1.a_ref), channel_id=1, source_target_pairs={{0,16},{16,0},{32,48},{48,32},{64,80},{80,64},{96,112},{112,96},{1... | collective-permute-start | bytes 1179656 | tf_op jit(solution)/shard_map/ppermute | solution.py:37
  10.9 1.1 copy.11
  13.9 1.9 %collective-permute-start.2 = (bf16[2,64,1536]{2,1,0:T(8,128)(2,1)S(1)}, bf16[2,64,1536]{2,1,0:T(8,128)(2,1)S(1)}, u32[]{:S(2)}, u32[]{:S(2)}) collective-permute-start(bf16[2,64,1536]{2,1,0:T(8,128)(2,1)S(1)} %get-tuple-element.11.refs_3_), channel_id=1, source_target_pairs={{0,64},{16,464},{32,96},{48,496},{64,128},{80,16},{96,160},{112,48... | collective-permute-start | bytes 1179656 | tf_op jit(solution)/shard_map/ppermute | solution.py:37
  15.9 8.4 %collective-permute-start.10 = (bf16[1552,128]{1,0:T(8,128)(2,1)S(1)}, bf16[1552,128]{1,0:T(8,128)(2,1)S(1)}, u32[]{:S(2)}, u32[]{:S(2)}) collective-permute-start(bf16[1552,128]{1,0:T(8,128)(2,1)S(1)} %pad_maximum_fusion.refs_1_), channel_id=1, source_target_pairs={{0,32},{16,48},{32,0},{48,16},{64,96},{80,112},{96,64},{112,80},{1... | collective-permute-start | bytes 1191944 | tf_op jit(solution)/shard_map/ppermute | solution.py:37
  24.3 1.9 %collective-permute-start = (bf16[1552,128]{1,0:T(8,128)(2,1)S(1)}, bf16[1552,128]{1,0:T(8,128)(2,1)S(1)}, u32[]{:S(2)}, u32[]{:S(2)}) collective-permute-start(bf16[1552,128]{1,0:T(8,128)(2,1)S(1)} %pad_maximum_fusion.refs_1_), channel_id=1, source_target_pairs={{0,16},{16,0},{32,48},{48,32},{64,80},{80,64},{96,112},{112,96},{1... | collective-permute-start | bytes 1191944 | tf_op jit(solution)/shard_map/ppermute | solution.py:37
  26.3 3.0 %collective-permute-start.3 = (bf16[2,64,1536]{2,1,0:T(8,128)(2,1)S(1)}, bf16[2,64,1536]{2,1,0:T(8,128)(2,1)S(1)}, u32[]{:S(2)}, u32[]{:S(2)}) collective-permute-start(bf16[2,64,1536]{2,1,0:T(8,128)(2,1)S(1)} %get-tuple-element.12.refs_4_), channel_id=1, source_target_pairs={{0,64},{16,464},{32,96},{48,496},{64,128},{80,16},{96,160},{112,48... | collective-permute-start | bytes 1179656 | tf_op jit(solution)/shard_map/ppermute | solution.py:37
  29.5 3.0 %collective-permute-start.4 = (bf16[2,64,1536]{2,1,0:T(8,128)(2,1)S(1)}, bf16[2,64,1536]{2,1,0:T(8,128)(2,1)S(1)}, u32[]{:S(2)}, u32[]{:S(2)}) collective-permute-start(bf16[2,64,1536]{2,1,0:T(8,128)(2,1)S(1)} %collective-permute-done.2.refs_5_), channel_id=1, source_target_pairs={{0,64},{16,464},{32,96},{48,496},{64,128},{80,16},{96,160},{112,48... | collective-permute-start | bytes 1179656 | tf_op jit(solution)/shard_map/ppermute | solution.py:37
  32.5 2.6 %collective-permute-done.3.refs_6_ = bf16[2,64,1536]{2,1,0:T(8,128)(2,1)S(1)} collective-permute-done((bf16[2,64,1536]{2,1,0:T(8,128)(2,1)S(1)}, bf16[2,64,1536]{2,1,0:T(8,128)(2,1)S(1)}, u32[]{:S(2)}, u32[]{:S(2)}) %collective-permute-start.3) | collective-permute-done | bytes 393248 | tf_op jit(solution)/shard_map/ppermute | solution.py:37
  35.1 3.9 %collective-permute-start.5 = (bf16[2,64,1536]{2,1,0:T(8,128)(2,1)S(1)}, bf16[2,64,1536]{2,1,0:T(8,128)(2,1)S(1)}, u32[]{:S(2)}, u32[]{:S(2)}) collective-permute-start(bf16[2,64,1536]{2,1,0:T(8,128)(2,1)S(1)} %collective-permute-done.3.refs_6_), channel_id=1, source_target_pairs={{0,64},{16,464},{32,96},{48,496},{64,128},{80,16},{96,160},{112,48... | collective-permute-start | bytes 1179656 | tf_op jit(solution)/shard_map/ppermute | solution.py:37
  39.3 3.9 %collective-permute-start.6 = (bf16[2,64,1536]{2,1,0:T(8,128)(2,1)S(1)}, bf16[2,64,1536]{2,1,0:T(8,128)(2,1)S(1)}, u32[]{:S(2)}, u32[]{:S(2)}) collective-permute-start(bf16[2,64,1536]{2,1,0:T(8,128)(2,1)S(1)} %collective-permute-done.4.refs_7_), channel_id=1, source_target_pairs={{0,64},{16,464},{32,96},{48,496},{64,128},{80,16},{96,160},{112,48... | collective-permute-start | bytes 1179656 | tf_op jit(solution)/shard_map/ppermute | solution.py:37
  43.7 5.0 %collective-permute-start.7 = (bf16[2,64,1536]{2,1,0:T(8,128)(2,1)S(1)}, bf16[2,64,1536]{2,1,0:T(8,128)(2,1)S(1)}, u32[]{:S(2)}, u32[]{:S(2)}) collective-permute-start(bf16[2,64,1536]{2,1,0:T(8,128)(2,1)S(1)} %collective-permute-done.5.refs_8_), channel_id=1, source_target_pairs={{0,64},{16,464},{32,96},{48,496},{64,128},{80,16},{96,160},{112,48... | collective-permute-start | bytes 1179656 | tf_op jit(solution)/shard_map/ppermute | solution.py:37
  48.8 5.9 %collective-permute-start.11 = (bf16[1552,128]{1,0:T(8,128)(2,1)S(1)}, bf16[1552,128]{1,0:T(8,128)(2,1)S(1)}, u32[]{:S(2)}, u32[]{:S(2)}) collective-permute-start(bf16[1552,128]{1,0:T(8,128)(2,1)S(1)} %shard_map.83.refs_1_), channel_id=1, source_target_pairs={{0,16},{16,0},{32,48},{48,32},{64,80},{80,64},{96,112},{112,96},{1... | collective-permute-start | bytes 1191944 | tf_op jit(solution)/shard_map/ppermute | solution.py:37
  54.8 2.6 %collective-permute-start.8 = (bf16[1,64,1536]{2,1,0:T(8,128)(2,1)S(1)}, bf16[1,64,1536]{2,1,0:T(8,128)(2,1)S(1)}, u32[]{:S(2)}, u32[]{:S(2)}) collective-permute-start(bf16[1,64,1536]{2,1,0:T(8,128)(2,1)S(1)} %slice.40), channel_id=1, source_target_pairs={{0,64},{16,464},{32,96},{48,496},{64,128},{80,16},{96,160},{112,48... | collective-permute-start | bytes 589832 | tf_op jit(solution)/shard_map/ppermute | solution.py:37
  57.4 1.9 %collective-permute-start.9 = (bf16[1,64,1536]{2,1,0:T(8,128)(2,1)S(1)}, bf16[1,64,1536]{2,1,0:T(8,128)(2,1)S(1)}, u32[]{:S(2)}, u32[]{:S(2)}) collective-permute-start(bf16[1,64,1536]{2,1,0:T(8,128)(2,1)S(1)} %slice.41), channel_id=1, source_target_pairs={{0,64},{16,464},{32,96},{48,496},{64,128},{80,16},{96,160},{112,48... | collective-permute-start | bytes 589832 | tf_op jit(solution)/shard_map/ppermute | solution.py:37
  59.6 1.9 %collective-permute-done.8.refs_11_ = bf16[1,64,1536]{2,1,0:T(8,128)(2,1)S(1)} collective-permute-done((bf16[1,64,1536]{2,1,0:T(8,128)(2,1)S(1)}, bf16[1,64,1536]{2,1,0:T(8,128)(2,1)S(1)}, u32[]{:S(2)}, u32[]{:S(2)}) %collective-permute-start.8) | collective-permute-done | bytes 196640 | tf_op jit(solution)/shard_map/ppermute | solution.py:37
  61.5 2.4 %collective-permute-done.9.refs_12_ = bf16[1,64,1536]{2,1,0:T(8,128)(2,1)S(1)} collective-permute-done((bf16[1,64,1536]{2,1,0:T(8,128)(2,1)S(1)}, bf16[1,64,1536]{2,1,0:T(8,128)(2,1)S(1)}, u32[]{:S(2)}, u32[]{:S(2)}) %collective-permute-start.9) | collective-permute-done | bytes 196640 | tf_op jit(solution)/shard_map/ppermute | solution.py:37
  63.8 2.4 %shard_map.84 = (bf16[8,128,128]{2,1,0:T(8,128)(2,1)S(1)}, bf16[8,128,128]{2,1,0:T(8,128)(2,1)S(1)}) custom-call(s32[2,8]{1,0:T(2,128)S(1)} %get-tuple-element.17.refs_0_, bf16[1552,128]{1,0:T(8,128)(2,1)S(1)} %shard_map.83.refs_1_, bf16[1552,128]{1,0:T(8,128)(2,1)S(1)} %collective-permute-done.11.refs_2_, ...), custom_call_target="tpu_custom_call" | custom-call | flops 805306368 | bytes 3145728 | tf_op jit(solution)/shard_map/pallas_call | solution.py:75
  66.3 1.9 %collective-permute-start.13 = (bf16[8,128,128]{2,1,0:T(8,128)(2,1)S(1)}, bf16[8,128,128]{2,1,0:T(8,128)(2,1)S(1)}, u32[]{:S(2)}, u32[]{:S(2)}) collective-permute-start(bf16[8,128,128]{2,1,0:T(8,128)(2,1)S(1)} %get-tuple-element.13.refs_13_), channel_id=1, source_target_pairs={{0,32},{16,48},{32,0},{48,16},{64,96},{80,112},{96,64},{112,80},{1... | collective-permute-start | bytes 786440 | tf_op jit(solution)/shard_map/ppermute | solution.py:37
  68.2 2.4 %shard_map.85 = (bf16[8,128,128]{2,1,0:T(8,128)(2,1)S(1)}, bf16[8,128,128]{2,1,0:T(8,128)(2,1)S(1)}) custom-call(s32[2,8]{1,0:T(2,128)S(1)} %get-tuple-element.18.refs_0_, bf16[1552,128]{1,0:T(8,128)(2,1)S(1)} %pad_maximum_fusion.refs_1_, bf16[1552,128]{1,0:T(8,128)(2,1)S(1)} %collective-permute-done.refs_2_, ...), custom_call_target="tpu_custom_call" | custom-call | flops 805306368 | bytes 3145728 | tf_op jit(solution)/shard_map/pallas_call | solution.py:75
  70.6 6.6 %collective-permute-start.12 = (bf16[8,128,128]{2,1,0:T(8,128)(2,1)S(1)}, bf16[8,128,128]{2,1,0:T(8,128)(2,1)S(1)}, u32[]{:S(2)}, u32[]{:S(2)}) collective-permute-start(bf16[8,128,128]{2,1,0:T(8,128)(2,1)S(1)} %get-tuple-element.15), channel_id=1, source_target_pairs={{0,16},{16,0},{32,48},{48,32},{64,80},{80,64},{96,112},{112,96},{1... | collective-permute-start | bytes 786440 | tf_op jit(solution)/shard_map/ppermute | solution.py:37
  77.2 7.2 %collective-permute-start.14 = (bf16[8,128,128]{2,1,0:T(8,128)(2,1)S(1)}, bf16[8,128,128]{2,1,0:T(8,128)(2,1)S(1)}, u32[]{:S(2)}, u32[]{:S(2)}) collective-permute-start(bf16[8,128,128]{2,1,0:T(8,128)(2,1)S(1)} %get-tuple-element.16), channel_id=1, source_target_pairs={{0,48},{16,32},{32,16},{48,0},{64,112},{80,96},{96,80},{112,64},{1... | collective-permute-start | bytes 786440 | tf_op jit(solution)/shard_map/ppermute | solution.py:37
  84.5 7.1 %collective-permute-done.14.refs_3_ = bf16[8,128,128]{2,1,0:T(8,128)(2,1)S(1)} collective-permute-done((bf16[8,128,128]{2,1,0:T(8,128)(2,1)S(1)}, bf16[8,128,128]{2,1,0:T(8,128)(2,1)S(1)}, u32[]{:S(2)}, u32[]{:S(2)}) %collective-permute-start.14) | collective-permute-done | bytes 262176 | tf_op jit(solution)/shard_map/ppermute | solution.py:37
  92.3 58.6 %all_to_all.5 = bf16[16,4,128,128]{3,2,1,0:T(8,128)(2,1)S(1)} all-to-all(bf16[16,4,128,128]{3,2,1,0:T(8,128)(2,1)S(1)} %bitcast.39), channel_id=1, replica_groups=mesh['kring'=32,'kblk'=16] {'kblk'}, dimensions={0} | all-to-all | bytes 4194304 | tf_op jit(solution)/shard_map/all_to_all | solution.py:219
  151.0 1.3 copy.14
  (44 shorter events, 6.1 us)
Async XLA Ops:
  0.0 13.7 %copy-start = (s32[1,1,32]{2,1,0:T(1,128)S(1)}, s32[1,1,32]{2,1,0:T(1,128)}, u32[]{:S(2)}) copy-start(s32[1,1,32]{2,1,0:T(1,128)} %param.14) | copy-start | bytes 388
  1.1 28.3 %copy-start.1 = (s32[1,1,32,1]{2,3,1,0:T(1,128)S(1)}, s32[1,1,32,1]{2,3,1,0:T(1,128)}, u32[]{:S(2)}) copy-start(s32[1,1,32,1]{2,3,1,0:T(1,128)} %param.15) | copy-start | bytes 388
  1.1 12.8 %collective-permute-start.1 = (bf16[128,1536]{1,0:T(8,128)(2,1)S(1)}, bf16[128,1536]{1,0:T(8,128)(2,1)S(1)}, u32[]{:S(2)}, u32[]{:S(2)}) collective-permute-start(bf16[128,1536]{1,0:T(8,128)(2,1)S(1)} %pad_maximum_fusion.1.a_ref), channel_id=1, source_target_pairs={{0,16},{16,0},{32,48},{48,32},{64,80},{80,64},{96,112},{112,96},{1... | collective-permute-start | bytes 1179656 | tf_op jit(solution)/shard_map/ppermute | solution.py:37
  13.9 15.6 %collective-permute-start.2 = (bf16[2,64,1536]{2,1,0:T(8,128)(2,1)S(1)}, bf16[2,64,1536]{2,1,0:T(8,128)(2,1)S(1)}, u32[]{:S(2)}, u32[]{:S(2)}) collective-permute-start(bf16[2,64,1536]{2,1,0:T(8,128)(2,1)S(1)} %get-tuple-element.11.refs_3_), channel_id=1, source_target_pairs={{0,64},{16,464},{32,96},{48,496},{64,128},{80,16},{96,160},{112,48... | collective-permute-start | bytes 1179656 | tf_op jit(solution)/shard_map/ppermute | solution.py:37
  15.9 32.9 %collective-permute-start.10 = (bf16[1552,128]{1,0:T(8,128)(2,1)S(1)}, bf16[1552,128]{1,0:T(8,128)(2,1)S(1)}, u32[]{:S(2)}, u32[]{:S(2)}) collective-permute-start(bf16[1552,128]{1,0:T(8,128)(2,1)S(1)} %pad_maximum_fusion.refs_1_), channel_id=1, source_target_pairs={{0,32},{16,48},{32,0},{48,16},{64,96},{80,112},{96,64},{112,80},{1... | collective-permute-start | bytes 1191944 | tf_op jit(solution)/shard_map/ppermute | solution.py:37
  24.3 24.4 %collective-permute-start = (bf16[1552,128]{1,0:T(8,128)(2,1)S(1)}, bf16[1552,128]{1,0:T(8,128)(2,1)S(1)}, u32[]{:S(2)}, u32[]{:S(2)}) collective-permute-start(bf16[1552,128]{1,0:T(8,128)(2,1)S(1)} %pad_maximum_fusion.refs_1_), channel_id=1, source_target_pairs={{0,16},{16,0},{32,48},{48,32},{64,80},{80,64},{96,112},{112,96},{1... | collective-permute-start | bytes 1191944 | tf_op jit(solution)/shard_map/ppermute | solution.py:37
  26.3 8.8 %collective-permute-start.3 = (bf16[2,64,1536]{2,1,0:T(8,128)(2,1)S(1)}, bf16[2,64,1536]{2,1,0:T(8,128)(2,1)S(1)}, u32[]{:S(2)}, u32[]{:S(2)}) collective-permute-start(bf16[2,64,1536]{2,1,0:T(8,128)(2,1)S(1)} %get-tuple-element.12.refs_4_), channel_id=1, source_target_pairs={{0,64},{16,464},{32,96},{48,496},{64,128},{80,16},{96,160},{112,48... | collective-permute-start | bytes 1179656 | tf_op jit(solution)/shard_map/ppermute | solution.py:37
  29.5 9.8 %collective-permute-start.4 = (bf16[2,64,1536]{2,1,0:T(8,128)(2,1)S(1)}, bf16[2,64,1536]{2,1,0:T(8,128)(2,1)S(1)}, u32[]{:S(2)}, u32[]{:S(2)}) collective-permute-start(bf16[2,64,1536]{2,1,0:T(8,128)(2,1)S(1)} %collective-permute-done.2.refs_5_), channel_id=1, source_target_pairs={{0,64},{16,464},{32,96},{48,496},{64,128},{80,16},{96,160},{112,48... | collective-permute-start | bytes 1179656 | tf_op jit(solution)/shard_map/ppermute | solution.py:37
  35.1 8.6 %collective-permute-start.5 = (bf16[2,64,1536]{2,1,0:T(8,128)(2,1)S(1)}, bf16[2,64,1536]{2,1,0:T(8,128)(2,1)S(1)}, u32[]{:S(2)}, u32[]{:S(2)}) collective-permute-start(bf16[2,64,1536]{2,1,0:T(8,128)(2,1)S(1)} %collective-permute-done.3.refs_6_), channel_id=1, source_target_pairs={{0,64},{16,464},{32,96},{48,496},{64,128},{80,16},{96,160},{112,48... | collective-permute-start | bytes 1179656 | tf_op jit(solution)/shard_map/ppermute | solution.py:37
  39.3 9.4 %collective-permute-start.6 = (bf16[2,64,1536]{2,1,0:T(8,128)(2,1)S(1)}, bf16[2,64,1536]{2,1,0:T(8,128)(2,1)S(1)}, u32[]{:S(2)}, u32[]{:S(2)}) collective-permute-start(bf16[2,64,1536]{2,1,0:T(8,128)(2,1)S(1)} %collective-permute-done.4.refs_7_), channel_id=1, source_target_pairs={{0,64},{16,464},{32,96},{48,496},{64,128},{80,16},{96,160},{112,48... | collective-permute-start | bytes 1179656 | tf_op jit(solution)/shard_map/ppermute | solution.py:37
  43.7 13.7 %collective-permute-start.7 = (bf16[2,64,1536]{2,1,0:T(8,128)(2,1)S(1)}, bf16[2,64,1536]{2,1,0:T(8,128)(2,1)S(1)}, u32[]{:S(2)}, u32[]{:S(2)}) collective-permute-start(bf16[2,64,1536]{2,1,0:T(8,128)(2,1)S(1)} %collective-permute-done.5.refs_8_), channel_id=1, source_target_pairs={{0,64},{16,464},{32,96},{48,496},{64,128},{80,16},{96,160},{112,48... | collective-permute-start | bytes 1179656 | tf_op jit(solution)/shard_map/ppermute | solution.py:37
  48.8 10.5 %collective-permute-start.11 = (bf16[1552,128]{1,0:T(8,128)(2,1)S(1)}, bf16[1552,128]{1,0:T(8,128)(2,1)S(1)}, u32[]{:S(2)}, u32[]{:S(2)}) collective-permute-start(bf16[1552,128]{1,0:T(8,128)(2,1)S(1)} %shard_map.83.refs_1_), channel_id=1, source_target_pairs={{0,16},{16,0},{32,48},{48,32},{64,80},{80,64},{96,112},{112,96},{1... | collective-permute-start | bytes 1191944 | tf_op jit(solution)/shard_map/ppermute | solution.py:37
  54.8 6.7 %collective-permute-start.8 = (bf16[1,64,1536]{2,1,0:T(8,128)(2,1)S(1)}, bf16[1,64,1536]{2,1,0:T(8,128)(2,1)S(1)}, u32[]{:S(2)}, u32[]{:S(2)}) collective-permute-start(bf16[1,64,1536]{2,1,0:T(8,128)(2,1)S(1)} %slice.40), channel_id=1, source_target_pairs={{0,64},{16,464},{32,96},{48,496},{64,128},{80,16},{96,160},{112,48... | collective-permute-start | bytes 589832 | tf_op jit(solution)/shard_map/ppermute | solution.py:37
  57.4 6.4 %collective-permute-start.9 = (bf16[1,64,1536]{2,1,0:T(8,128)(2,1)S(1)}, bf16[1,64,1536]{2,1,0:T(8,128)(2,1)S(1)}, u32[]{:S(2)}, u32[]{:S(2)}) collective-permute-start(bf16[1,64,1536]{2,1,0:T(8,128)(2,1)S(1)} %slice.41), channel_id=1, source_target_pairs={{0,64},{16,464},{32,96},{48,496},{64,128},{80,16},{96,160},{112,48... | collective-permute-start | bytes 589832 | tf_op jit(solution)/shard_map/ppermute | solution.py:37
  66.3 25.3 %collective-permute-start.13 = (bf16[8,128,128]{2,1,0:T(8,128)(2,1)S(1)}, bf16[8,128,128]{2,1,0:T(8,128)(2,1)S(1)}, u32[]{:S(2)}, u32[]{:S(2)}) collective-permute-start(bf16[8,128,128]{2,1,0:T(8,128)(2,1)S(1)} %get-tuple-element.13.refs_13_), channel_id=1, source_target_pairs={{0,32},{16,48},{32,0},{48,16},{64,96},{80,112},{96,64},{112,80},{1... | collective-permute-start | bytes 786440 | tf_op jit(solution)/shard_map/ppermute | solution.py:37
  70.6 13.9 %collective-permute-start.12 = (bf16[8,128,128]{2,1,0:T(8,128)(2,1)S(1)}, bf16[8,128,128]{2,1,0:T(8,128)(2,1)S(1)}, u32[]{:S(2)}, u32[]{:S(2)}) collective-permute-start(bf16[8,128,128]{2,1,0:T(8,128)(2,1)S(1)} %get-tuple-element.15), channel_id=1, source_target_pairs={{0,16},{16,0},{32,48},{48,32},{64,80},{80,64},{96,112},{112,96},{1... | collective-permute-start | bytes 786440 | tf_op jit(solution)/shard_map/ppermute | solution.py:37
  77.2 14.3 %collective-permute-start.14 = (bf16[8,128,128]{2,1,0:T(8,128)(2,1)S(1)}, bf16[8,128,128]{2,1,0:T(8,128)(2,1)S(1)}, u32[]{:S(2)}, u32[]{:S(2)}) collective-permute-start(bf16[8,128,128]{2,1,0:T(8,128)(2,1)S(1)} %get-tuple-element.16), channel_id=1, source_target_pairs={{0,48},{16,32},{32,16},{48,0},{64,112},{80,96},{96,80},{112,64},{1... | collective-permute-start | bytes 786440 | tf_op jit(solution)/shard_map/ppermute | solution.py:37

commit v4 on v3

--- a/solution.py
+++ b/solution.py
@@ -12,7 +12,6 @@
 TILE = 128
 G_COUNT = 1024
 CHAINS = 2
-STEPS = ((0, 1, 2, 3, 4),)
 
 
 def place(i):
@@ -37,11 +36,12 @@
     return lax.ppermute(x, "kring", perm)
 
 
-def tiles_kernel(parts, cut_ref, elem_a, elem_b, *refs):
-    *block_refs, out_a, out_b, masked, total = refs
+def tiles_kernel(parts, count, cut_ref, *refs):
+    elem_refs, block_refs, out_refs = refs[:count], refs[count : -count - 2], refs[-count - 2 : -2]
+    masked, total = refs[-2:]
     depth = masked.shape[2]
     lane = lax.broadcasted_iota(jnp.int32, (16, G_COUNT), 1)
-    for e, (elem_ref, out_ref) in enumerate(((elem_a, out_a), (elem_b, out_b))):
+    for e, (elem_ref, out_ref) in enumerate(zip(elem_refs, out_refs)):
         for at, (spot, sources, k) in enumerate(parts):
             keep = (lane < cut_ref[e, spot]).astype(jnp.float32).astype(jnp.bfloat16)
             for n, source in enumerate(sources):
@@ -56,7 +56,7 @@
             out_ref[at] = total[e, pl.ds(at * TILE, TILE), :].T.astype(jnp.bfloat16)
 
 
-def make_tiles(cuts, elem_a, elem_b, chains, steps, after=()):
+def make_tiles(cuts, elems, chains, steps, after=()):
     depth = chains[0][0].shape[2]
     flat, parts = [], []
     for step in steps:
@@ -70,22 +70,23 @@
     shape = jax.ShapeDtypeStruct((count, TILE, TILE), jnp.bfloat16)
 
     def kernel(*refs):
-        tiles_kernel(parts, *refs[: 3 + len(flat)], *refs[3 + len(flat) + len(after) :])
+        read = 1 + len(elems) + len(flat)
+        tiles_kernel(parts, len(elems), *refs[:read], *refs[read + len(after) :])
 
     return pl.pallas_call(
         kernel,
-        out_shape=(shape, shape),
-        in_specs=[pl.BlockSpec(memory_space=pltpu.SMEM)] + [vmem] * (2 + len(flat)) + [free] * len(after),
-        out_specs=(vmem, vmem),
+        out_shape=(shape,) * len(elems),
+        in_specs=[pl.BlockSpec(memory_space=pltpu.SMEM)] + [vmem] * (len(elems) + len(flat)) + [free] * len(after),
+        out_specs=(vmem,) * len(elems),
         scratch_shapes=[
-            pltpu.VMEM((2, count * TILE, depth), jnp.bfloat16),
-            pltpu.VMEM((2, count * TILE, TILE), jnp.float32),
+            pltpu.VMEM((len(elems), count * TILE, depth), jnp.bfloat16),
+            pltpu.VMEM((len(elems), count * TILE, TILE), jnp.float32),
         ],
         compiler_params=pltpu.CompilerParams(vmem_limit_bytes=24 << 20),
         cost_estimate=pl.CostEstimate(
-            flops=4 * count * TILE * depth * TILE, bytes_accessed=2 * count * TILE * depth, transcendentals=0
+            flops=2 * len(elems) * count * TILE * depth * TILE, bytes_accessed=2 * count * TILE * depth, transcendentals=0
         ),
-    )(cuts, elem_a, elem_b, *flat, *after)
+    )(cuts, *elems, *flat, *after)
 
 
 def pair_kernel(pieces, a_ref, b_ref, *refs):
@@ -165,7 +166,8 @@
     rows = jnp.concatenate([rows_x[0, 0], rows_d[0, 0]], axis=1)
     tile_rows, depth = rows.shape
 
-    chains = [ring(held) for held in pair(rows, send(rows, OTHER_CORE), CHAINS)]
+    held = pair(rows, send(rows, OTHER_CORE), CHAINS)
+    chains = [ring(h) for h in held]
 
     scaled_x = (elem_x[0, 0].astype(jnp.float32) * coulomb).astype(jnp.bfloat16)
     scaled_d = (elem_d[0, 0].astype(jnp.float32) * screened).astype(jnp.bfloat16)
@@ -177,7 +179,6 @@
     far = send(elem_t, OTHER_HALF)
     far = copy_after(far, (chains[0][3],))
     far_near = send(far, OTHER_CORE)
-    near = send(elem_t, OTHER_CORE)
 
     partner = jnp.arange(4 * RING, dtype=jnp.int32)
     p_y, p_z, p_c = place(partner)
@@ -197,7 +198,7 @@
         row = parts[:, 0] * 32 + parts[:, 1]
         return jnp.sum(jnp.where(listed[None], row[:, None, :], 0), axis=2)
 
-    cuts_far, cuts_near = cuts_of(far, far_near), cuts_of(elem_t, near)
+    cuts_far, cuts_far_near = cuts_of(far), cuts_of(far_near)
 
     spot = jnp.where(has_mine, spot_mine, RING + spot_other) + 2 * RING * jnp.abs(p_z - my_z)
     dest = owners[0, 0, :, 0]
@@ -207,14 +208,15 @@
     hit = slots[:, None] == (dest * CAP + slot_of)[None, :]
     pos = 4 * RING + jnp.sum(jnp.where(hit, (spot - 4 * RING)[None, :], 0), axis=1)
 
-    from_far, from_far_near, after = [], [], ()
-    for steps in STEPS:
-        to_far, to_far_near = make_tiles(cuts_far, far, far_near, chains, steps, after)
-        from_far.append(send(to_far, OTHER_HALF))
-        from_far_near.append(send(to_far_near, OTHER_BOTH))
-        after = from_far[-1:]
-    mine, to_near = make_tiles(cuts_near, elem_t, near, chains, range(RING // 2 + 1), (to_far,))
-    parts = [mine, send(to_near, OTHER_CORE)] + from_far + from_far_near
+    steps = range(RING // 2 + 1)
+    (to_far_near,) = make_tiles(cuts_far_near, (far_near,), chains, steps)
+    from_far_near = send(to_far_near, OTHER_BOTH)
+    (to_far,) = make_tiles(cuts_far, (far,), chains, steps, (to_far_near,))
+    from_far = send(to_far, OTHER_HALF)
+    near = send(copy_after(elem_t, (chains[1][3],)), OTHER_CORE)
+    cuts_near = cuts_of(elem_t, near)
+    mine, to_near = make_tiles(cuts_near, (elem_t, near), chains, steps, (to_far,))
+    parts = [mine, send(to_near, OTHER_CORE), from_far, from_far_near]
     outbox = make_outbox(pos, parts).reshape(blk_len, CAP, tile_rows, tile_rows)
     received = lax.all_to_all(outbox, "kblk", split_axis=0, concat_axis=0, tiled=True)
     return received[None, None]

time: 154 us -> 151 us (0.981)
  starting transfers between devices: 65.9 us -> 60.1 us
  waiting for transfers between devices: 14.8 us -> 10.3 us
  blocking collectives: 58.6 us -> 62 us
  other arithmetic: 3.36 us -> 5.41 us
  Pallas kernels: 5.71 us -> 7.48 us
    ppermute x15, starting transfers between devices: 65.9 us -> 60.1 us  [send(): return lax.ppermute(x, 'kring', perm)]
    ppermute x15, waiting for transfers between devices: 14.8 us -> 10.3 us  [send(): return lax.ppermute(x, 'kring', perm)]
    all_to_all x1, blocking collectives: 58.6 us -> 62 us  [body(): lax.all_to_all(outbox, 'kblk', split_axis=0, concat_axis=0, tiled=True)]
    pallas_call x2 -> x3, Pallas kernels: 4.88 us -> 5.63 us  [make_tiles(): pl.pallas_call(kernel, out_shape=(shape,) * len(elems), in_specs=[pl.Bloc...]
    unnamed x7 -> x11, local copies, waits for them, and re-layouts: 3.47 us -> 3.48 us
  transfers between devices with their start and end apart: 15 -> 15, of which waited for: 6 -> 6; matrix products, arithmetic and copies ran while one was open for 3% -> 4% of each run, Pallas kernels for 2% -> 3%
where the time goes in v4:
time: 151 us; the launch traced here: 149 us
  blocking collectives  62 us (41%)
  starting transfers between devices  60.1 us (40%)
  waiting for transfers between devices  10.3 us (7%)
  Pallas kernels  7.48 us (5%)
  other arithmetic  5.41 us (4%)
  local copies, waits for them, and re-layouts  3.51 us (2%)
    all_to_all x1, blocking collectives, body(): lax.all_to_all(outbox, 'kblk', split_axis=0, concat_axis=0, tiled=True)  62 us
    ppermute x15, starting transfers between devices, send(): return lax.ppermute(x, 'kring', perm)  60.1 us
    ppermute x15, waiting for transfers between devices, send(): return lax.ppermute(x, 'kring', perm)  10.3 us
    pallas_call x3, Pallas kernels, make_tiles(): pl.pallas_call(kernel, out_shape=(shape,) * len(elems), in_specs=[pl.Bloc...  5.63 us
    unnamed x11, local copies, waits for them, and re-layouts  3.48 us
  transfers between devices with their start and end apart: 15, of which 6 were waited for; matrix products, arithmetic and copies ran while one was open for 4% of the time, Pallas kernels for 3%

profile of v4, /device:TPU:1, one launch (start us, length us, event | category | flops | bytes accessed | tf_op | source)
XLA Modules:
  0.0 149.3 jit_solution(9453436228126973463)
XLA Ops:
  1.1 8.8 %collective-permute-start = (bf16[128,1536]{1,0:T(8,128)(2,1)S(1)}, bf16[128,1536]{1,0:T(8,128)(2,1)S(1)}, u32[]{:S(2)}, u32[]{:S(2)}) collective-permute-start(bf16[128,1536]{1,0:T(8,128)(2,1)S(1)} %pad_maximum_fusion.1.a_ref), channel_id=1, source_target_pairs={{0,16},{16,0},{32,48},{48,32},{64,80},{80,64},{96,112},{112,96},{1... | collective-permute-start | bytes 1179656 | tf_op jit(solution)/shard_map/ppermute | solution.py:36
  13.2 1.9 %collective-permute-start.5 = (bf16[2,64,1536]{2,1,0:T(8,128)(2,1)S(1)}, bf16[2,64,1536]{2,1,0:T(8,128)(2,1)S(1)}, u32[]{:S(2)}, u32[]{:S(2)}) collective-permute-start(bf16[2,64,1536]{2,1,0:T(8,128)(2,1)S(1)} %get-tuple-element.10.refs_2_.refs_3_), channel_id=1, source_target_pairs={{0,64},{16,464},{32,96},{48,496},{64,128},{80,16},{96,160},{112,48... | collective-permute-start | bytes 1179656 | tf_op jit(solution)/shard_map/ppermute | solution.py:36
  15.1 1.9 %collective-permute-start.1 = (bf16[2,64,1536]{2,1,0:T(8,128)(2,1)S(1)}, bf16[2,64,1536]{2,1,0:T(8,128)(2,1)S(1)}, u32[]{:S(2)}, u32[]{:S(2)}) collective-permute-start(bf16[2,64,1536]{2,1,0:T(8,128)(2,1)S(1)} %get-tuple-element.9.refs_3_.refs_4_), channel_id=1, source_target_pairs={{0,64},{16,464},{32,96},{48,496},{64,128},{80,16},{96,160},{112,48... | collective-permute-start | bytes 1179656 | tf_op jit(solution)/shard_map/ppermute | solution.py:36
  17.1 9.5 %collective-permute-start.10 = (bf16[1552,128]{1,0:T(8,128)(2,1)S(1)}, bf16[1552,128]{1,0:T(8,128)(2,1)}, u32[]{:S(2)}, u32[]{:S(2)}) collective-permute-start(bf16[1552,128]{1,0:T(8,128)(2,1)S(1)} %pad_maximum_fusion.x_ref.refs_1_), channel_id=1, source_target_pairs={{0,32},{16,48},{32,0},{48,16},{64,96},{80,112},{96,64},{112,80},{1... | collective-permute-start | bytes 1191944 | tf_op jit(solution)/shard_map/ppermute | solution.py:36
  26.7 3.0 %collective-permute-start.6 = (bf16[2,64,1536]{2,1,0:T(8,128)(2,1)S(1)}, bf16[2,64,1536]{2,1,0:T(8,128)(2,1)S(1)}, u32[]{:S(2)}, u32[]{:S(2)}) collective-permute-start(bf16[2,64,1536]{2,1,0:T(8,128)(2,1)S(1)} %collective-permute-done.5.refs_4_.refs_5_), channel_id=1, source_target_pairs={{0,64},{16,464},{32,96},{48,496},{64,128},{80,16},{96,160},{112,48... | collective-permute-start | bytes 1179656 | tf_op jit(solution)/shard_map/ppermute | solution.py:36
  29.7 3.0 %collective-permute-start.2 = (bf16[2,64,1536]{2,1,0:T(8,128)(2,1)S(1)}, bf16[2,64,1536]{2,1,0:T(8,128)(2,1)S(1)}, u32[]{:S(2)}, u32[]{:S(2)}) collective-permute-start(bf16[2,64,1536]{2,1,0:T(8,128)(2,1)S(1)} %collective-permute-done.1.refs_5_.refs_6_), channel_id=1, source_target_pairs={{0,64},{16,464},{32,96},{48,496},{64,128},{80,16},{96,160},{112,48... | collective-permute-start | bytes 1179656 | tf_op jit(solution)/shard_map/ppermute | solution.py:36
  32.7 2.8 %collective-permute-done.6.refs_6_.refs_7_ = bf16[2,64,1536]{2,1,0:T(8,128)(2,1)S(1)} collective-permute-done((bf16[2,64,1536]{2,1,0:T(8,128)(2,1)S(1)}, bf16[2,64,1536]{2,1,0:T(8,128)(2,1)S(1)}, u32[]{:S(2)}, u32[]{:S(2)}) %collective-permute-start.6) | collective-permute-done | bytes 393248 | tf_op jit(solution)/shard_map/ppermute | solution.py:36
  35.5 4.1 %collective-permute-start.7 = (bf16[2,64,1536]{2,1,0:T(8,128)(2,1)S(1)}, bf16[2,64,1536]{2,1,0:T(8,128)(2,1)S(1)}, u32[]{:S(2)}, u32[]{:S(2)}) collective-permute-start(bf16[2,64,1536]{2,1,0:T(8,128)(2,1)S(1)} %collective-permute-done.6.refs_6_.refs_7_), channel_id=1, source_target_pairs={{0,64},{16,464},{32,96},{48,496},{64,128},{80,16},{96,160},{112,48... | collective-permute-start | bytes 1179656 | tf_op jit(solution)/shard_map/ppermute | solution.py:36
  39.7 3.9 %collective-permute-start.3 = (bf16[2,64,1536]{2,1,0:T(8,128)(2,1)S(1)}, bf16[2,64,1536]{2,1,0:T(8,128)(2,1)S(1)}, u32[]{:S(2)}, u32[]{:S(2)}) collective-permute-start(bf16[2,64,1536]{2,1,0:T(8,128)(2,1)S(1)} %collective-permute-done.2.refs_7_.refs_8_), channel_id=1, source_target_pairs={{0,64},{16,464},{32,96},{48,496},{64,128},{80,16},{96,160},{112,48... | collective-permute-start | bytes 1179656 | tf_op jit(solution)/shard_map/ppermute | solution.py:36
  43.6 1.2 fusion.22
  47.4 3.1 %collective-permute-start.11 = (bf16[1552,128]{1,0:T(8,128)(2,1)S(1)}, bf16[1552,128]{1,0:T(8,128)(2,1)S(1)}, u32[]{:S(2)}, u32[]{:S(2)}) collective-permute-start(bf16[1552,128]{1,0:T(8,128)(2,1)S(1)} %shard_map.84.refs_1_), channel_id=1, source_target_pairs={{0,16},{16,0},{32,48},{48,32},{64,80},{80,64},{96,112},{112,96},{1... | collective-permute-start | bytes 1191944 | tf_op jit(solution)/shard_map/ppermute | solution.py:36
  50.6 2.9 %collective-permute-start.8 = (bf16[1,64,1536]{2,1,0:T(8,128)(2,1)S(1)}, bf16[1,64,1536]{2,1,0:T(8,128)(2,1)S(1)}, u32[]{:S(2)}, u32[]{:S(2)}) collective-permute-start(bf16[1,64,1536]{2,1,0:T(8,128)(2,1)S(1)} %slice.48), channel_id=1, source_target_pairs={{0,64},{16,464},{32,96},{48,496},{64,128},{80,16},{96,160},{112,48... | collective-permute-start | bytes 589832 | tf_op jit(solution)/shard_map/ppermute | solution.py:36
  53.5 1.9 %collective-permute-start.9 = (bf16[1,64,1536]{2,1,0:T(8,128)(2,1)S(1)}, bf16[1,64,1536]{2,1,0:T(8,128)(2,1)S(1)}, u32[]{:S(2)}, u32[]{:S(2)}) collective-permute-start(bf16[1,64,1536]{2,1,0:T(8,128)(2,1)S(1)} %slice.49), channel_id=1, source_target_pairs={{0,64},{16,464},{32,96},{48,496},{64,128},{80,16},{96,160},{112,48... | collective-permute-start | bytes 589832 | tf_op jit(solution)/shard_map/ppermute | solution.py:36
  55.5 2.8 %collective-permute-start.4 = (bf16[1552,128]{1,0:T(8,128)(2,1)S(1)}, bf16[1552,128]{1,0:T(8,128)(2,1)S(1)}, u32[]{:S(2)}, u32[]{:S(2)}) collective-permute-start(bf16[1552,128]{1,0:T(8,128)(2,1)S(1)} %shard_map.83), channel_id=1, source_target_pairs={{0,16},{16,0},{32,48},{48,32},{64,80},{80,64},{96,112},{112,96},{1... | collective-permute-start | bytes 1191944 | tf_op jit(solution)/shard_map/ppermute | solution.py:36
  60.2 1.6 %shard_map.85.refs_12_ = bf16[8,128,128]{2,1,0:T(8,128)(2,1)S(1)} custom-call(s32[1,8]{1,0:T(1,128)S(1)} %bitcast.51, bf16[1552,128]{1,0:T(8,128)(2,1)S(1)} %collective-permute-done.11.refs_1_, bf16[2,64,1536]{2,1,0:T(8,128)(2,1)S(1)} %get-tuple-element.10.refs_2_.refs_3_, bf16[2,64,1536]{2,1,0:T(8,128)(2,1)S(1)} %get-tuple-element.9.refs_3_.refs_4_, ...), custom_call_target="tpu_custom_call" | custom-call | flops 402653184 | bytes 3145728 | tf_op jit(solution)/shard_map/pallas_call | solution.py:76
  61.8 6.7 %collective-permute-start.14 = (bf16[8,128,128]{2,1,0:T(8,128)(2,1)S(1)}, bf16[8,128,128]{2,1,0:T(8,128)(2,1)S(1)}, u32[]{:S(2)}, u32[]{:S(2)}) collective-permute-start(bf16[8,128,128]{2,1,0:T(8,128)(2,1)S(1)} %shard_map.85.refs_12_), channel_id=1, source_target_pairs={{0,48},{16,32},{32,16},{48,0},{64,112},{80,96},{96,80},{112,64},{1... | collective-permute-start | bytes 786440 | tf_op jit(solution)/shard_map/ppermute | solution.py:36
  68.5 1.6 %shard_map.86.refs_13_ = bf16[8,128,128]{2,1,0:T(8,128)(2,1)S(1)} custom-call(s32[1,8]{1,0:T(1,128)S(1)} %bitcast.52, bf16[1552,128]{1,0:T(8,128)(2,1)S(1)} %shard_map.84.refs_1_, bf16[2,64,1536]{2,1,0:T(8,128)(2,1)S(1)} %get-tuple-element.10.refs_2_.refs_3_, bf16[2,64,1536]{2,1,0:T(8,128)(2,1)S(1)} %get-tuple-element.9.refs_3_.refs_4_, ...), custom_call_target="tpu_custom_call" | custom-call | flops 402653184 | bytes 3145728 | tf_op jit(solution)/shard_map/pallas_call | solution.py:76
  70.1 4.7 %collective-permute-start.13 = (bf16[8,128,128]{2,1,0:T(8,128)(2,1)S(1)}, bf16[8,128,128]{2,1,0:T(8,128)(2,1)S(1)}, u32[]{:S(2)}, u32[]{:S(2)}) collective-permute-start(bf16[8,128,128]{2,1,0:T(8,128)(2,1)S(1)} %shard_map.86.refs_13_), channel_id=1, source_target_pairs={{0,32},{16,48},{32,0},{48,16},{64,96},{80,112},{96,64},{112,80},{1... | collective-permute-start | bytes 786440 | tf_op jit(solution)/shard_map/ppermute | solution.py:36
  74.9 2.4 %shard_map.87 = (bf16[8,128,128]{2,1,0:T(8,128)(2,1)S(1)}, bf16[8,128,128]{2,1,0:T(8,128)(2,1)S(1)}) custom-call(s32[2,8]{1,0:T(2,128)S(1)} %select_reduce_fusion.1.refs_0_, bf16[1552,128]{1,0:T(8,128)(2,1)S(1)} %pad_maximum_fusion.x_ref.refs_1_, bf16[1552,128]{1,0:T(8,128)(2,1)S(1)} %collective-permute-done.4.refs_2_, ...), custom_call_target="tpu_custom_call" | custom-call | flops 805306368 | bytes 3145728 | tf_op jit(solution)/shard_map/pallas_call | solution.py:76
  77.4 1.9 %collective-permute-start.12 = (bf16[8,128,128]{2,1,0:T(8,128)(2,1)S(1)}, bf16[8,128,128]{2,1,0:T(8,128)(2,1)S(1)}, u32[]{:S(2)}, u32[]{:S(2)}) collective-permute-start(bf16[8,128,128]{2,1,0:T(8,128)(2,1)S(1)} %get-tuple-element.12), channel_id=1, source_target_pairs={{0,16},{16,0},{32,48},{48,32},{64,80},{80,64},{96,112},{112,96},{1... | collective-permute-start | bytes 786440 | tf_op jit(solution)/shard_map/ppermute | solution.py:36
  79.4 1.4 collective-permute-done.12.refs_1_
  80.8 4.4 %collective-permute-done.13.refs_2_ = bf16[8,128,128]{2,1,0:T(8,128)(2,1)S(1)} collective-permute-done((bf16[8,128,128]{2,1,0:T(8,128)(2,1)S(1)}, bf16[8,128,128]{2,1,0:T(8,128)(2,1)S(1)}, u32[]{:S(2)}, u32[]{:S(2)}) %collective-permute-start.13) | collective-permute-done | bytes 262176 | tf_op jit(solution)/shard_map/ppermute | solution.py:36
  85.9 62.0 %all_to_all.5 = bf16[16,4,128,128]{3,2,1,0:T(8,128)(2,1)S(1)} all-to-all(bf16[16,4,128,128]{3,2,1,0:T(8,128)(2,1)S(1)} %bitcast.50), channel_id=1, replica_groups=mesh['kring'=32,'kblk'=16] {'kblk'}, dimensions={0} | all-to-all | bytes 4194304 | tf_op jit(solution)/shard_map/all_to_all | solution.py:221
  148.0 1.3 copy.14
  (51 shorter events, 10.1 us)
Async XLA Ops:
  0.0 12.9 %copy-start = (f32[512]{0:T(512)S(1)}, f32[512]{0:T(512)}, u32[]{:S(2)}) copy-start(f32[512]{0:T(512)} %param.13) | copy-start | bytes 6148
  0.0 17.0 %copy-start.3 = (s32[1,1,32]{2,1,0:T(1,128)S(1)}, s32[1,1,32]{2,1,0:T(1,128)}, u32[]{:S(2)}) copy-start(s32[1,1,32]{2,1,0:T(1,128)} %param.14) | copy-start | bytes 388
  1.1 12.0 %collective-permute-start = (bf16[128,1536]{1,0:T(8,128)(2,1)S(1)}, bf16[128,1536]{1,0:T(8,128)(2,1)S(1)}, u32[]{:S(2)}, u32[]{:S(2)}) collective-permute-start(bf16[128,1536]{1,0:T(8,128)(2,1)S(1)} %pad_maximum_fusion.1.a_ref), channel_id=1, source_target_pairs={{0,16},{16,0},{32,48},{48,32},{64,80},{80,64},{96,112},{112,96},{1... | collective-permute-start | bytes 1179656 | tf_op jit(solution)/shard_map/ppermute | solution.py:36
  13.2 13.5 %collective-permute-start.5 = (bf16[2,64,1536]{2,1,0:T(8,128)(2,1)S(1)}, bf16[2,64,1536]{2,1,0:T(8,128)(2,1)S(1)}, u32[]{:S(2)}, u32[]{:S(2)}) collective-permute-start(bf16[2,64,1536]{2,1,0:T(8,128)(2,1)S(1)} %get-tuple-element.10.refs_2_.refs_3_), channel_id=1, source_target_pairs={{0,64},{16,464},{32,96},{48,496},{64,128},{80,16},{96,160},{112,48... | collective-permute-start | bytes 1179656 | tf_op jit(solution)/shard_map/ppermute | solution.py:36
  15.1 14.6 %collective-permute-start.1 = (bf16[2,64,1536]{2,1,0:T(8,128)(2,1)S(1)}, bf16[2,64,1536]{2,1,0:T(8,128)(2,1)S(1)}, u32[]{:S(2)}, u32[]{:S(2)}) collective-permute-start(bf16[2,64,1536]{2,1,0:T(8,128)(2,1)S(1)} %get-tuple-element.9.refs_3_.refs_4_), channel_id=1, source_target_pairs={{0,64},{16,464},{32,96},{48,496},{64,128},{80,16},{96,160},{112,48... | collective-permute-start | bytes 1179656 | tf_op jit(solution)/shard_map/ppermute | solution.py:36
  17.1 29.3 %collective-permute-start.10 = (bf16[1552,128]{1,0:T(8,128)(2,1)S(1)}, bf16[1552,128]{1,0:T(8,128)(2,1)}, u32[]{:S(2)}, u32[]{:S(2)}) collective-permute-start(bf16[1552,128]{1,0:T(8,128)(2,1)S(1)} %pad_maximum_fusion.x_ref.refs_1_), channel_id=1, source_target_pairs={{0,32},{16,48},{32,0},{48,16},{64,96},{80,112},{96,64},{112,80},{1... | collective-permute-start | bytes 1191944 | tf_op jit(solution)/shard_map/ppermute | solution.py:36
  26.7 8.8 %collective-permute-start.6 = (bf16[2,64,1536]{2,1,0:T(8,128)(2,1)S(1)}, bf16[2,64,1536]{2,1,0:T(8,128)(2,1)S(1)}, u32[]{:S(2)}, u32[]{:S(2)}) collective-permute-start(bf16[2,64,1536]{2,1,0:T(8,128)(2,1)S(1)} %collective-permute-done.5.refs_4_.refs_5_), channel_id=1, source_target_pairs={{0,64},{16,464},{32,96},{48,496},{64,128},{80,16},{96,160},{112,48... | collective-permute-start | bytes 1179656 | tf_op jit(solution)/shard_map/ppermute | solution.py:36
  29.7 10.0 %collective-permute-start.2 = (bf16[2,64,1536]{2,1,0:T(8,128)(2,1)S(1)}, bf16[2,64,1536]{2,1,0:T(8,128)(2,1)S(1)}, u32[]{:S(2)}, u32[]{:S(2)}) collective-permute-start(bf16[2,64,1536]{2,1,0:T(8,128)(2,1)S(1)} %collective-permute-done.1.refs_5_.refs_6_), channel_id=1, source_target_pairs={{0,64},{16,464},{32,96},{48,496},{64,128},{80,16},{96,160},{112,48... | collective-permute-start | bytes 1179656 | tf_op jit(solution)/shard_map/ppermute | solution.py:36
  35.5 10.9 %collective-permute-start.7 = (bf16[2,64,1536]{2,1,0:T(8,128)(2,1)S(1)}, bf16[2,64,1536]{2,1,0:T(8,128)(2,1)S(1)}, u32[]{:S(2)}, u32[]{:S(2)}) collective-permute-start(bf16[2,64,1536]{2,1,0:T(8,128)(2,1)S(1)} %collective-permute-done.6.refs_6_.refs_7_), channel_id=1, source_target_pairs={{0,64},{16,464},{32,96},{48,496},{64,128},{80,16},{96,160},{112,48... | collective-permute-start | bytes 1179656 | tf_op jit(solution)/shard_map/ppermute | solution.py:36
  39.7 13.8 %collective-permute-start.3 = (bf16[2,64,1536]{2,1,0:T(8,128)(2,1)S(1)}, bf16[2,64,1536]{2,1,0:T(8,128)(2,1)S(1)}, u32[]{:S(2)}, u32[]{:S(2)}) collective-permute-start(bf16[2,64,1536]{2,1,0:T(8,128)(2,1)S(1)} %collective-permute-done.2.refs_7_.refs_8_), channel_id=1, source_target_pairs={{0,64},{16,464},{32,96},{48,496},{64,128},{80,16},{96,160},{112,48... | collective-permute-start | bytes 1179656 | tf_op jit(solution)/shard_map/ppermute | solution.py:36
  44.8 14.9 %copy-start.1 = (bf16[1,1,32]{2,1,0:T(2,128)(2,1)S(1)}, bf16[1,1,32]{2,1,0:T(2,128)(2,1)}, u32[]{:S(2)}) copy-start(bf16[1,1,32]{2,1,0:T(2,128)(2,1)} %get-tuple-element.15) | copy-start | bytes 196
  44.8 14.9 %copy-start.2 = (bf16[1,1,32]{2,1,0:T(2,128)(2,1)S(1)}, bf16[1,1,32]{2,1,0:T(2,128)(2,1)}, u32[]{:S(2)}) copy-start(bf16[1,1,32]{2,1,0:T(2,128)(2,1)} %get-tuple-element.16) | copy-start | bytes 196
  47.4 11.0 %collective-permute-start.11 = (bf16[1552,128]{1,0:T(8,128)(2,1)S(1)}, bf16[1552,128]{1,0:T(8,128)(2,1)S(1)}, u32[]{:S(2)}, u32[]{:S(2)}) collective-permute-start(bf16[1552,128]{1,0:T(8,128)(2,1)S(1)} %shard_map.84.refs_1_), channel_id=1, source_target_pairs={{0,16},{16,0},{32,48},{48,32},{64,80},{80,64},{96,112},{112,96},{1... | collective-permute-start | bytes 1191944 | tf_op jit(solution)/shard_map/ppermute | solution.py:36
  50.6 9.1 %collective-permute-start.8 = (bf16[1,64,1536]{2,1,0:T(8,128)(2,1)S(1)}, bf16[1,64,1536]{2,1,0:T(8,128)(2,1)S(1)}, u32[]{:S(2)}, u32[]{:S(2)}) collective-permute-start(bf16[1,64,1536]{2,1,0:T(8,128)(2,1)S(1)} %slice.48), channel_id=1, source_target_pairs={{0,64},{16,464},{32,96},{48,496},{64,128},{80,16},{96,160},{112,48... | collective-permute-start | bytes 589832 | tf_op jit(solution)/shard_map/ppermute | solution.py:36
  53.5 6.7 %collective-permute-start.9 = (bf16[1,64,1536]{2,1,0:T(8,128)(2,1)S(1)}, bf16[1,64,1536]{2,1,0:T(8,128)(2,1)S(1)}, u32[]{:S(2)}, u32[]{:S(2)}) collective-permute-start(bf16[1,64,1536]{2,1,0:T(8,128)(2,1)S(1)} %slice.49), channel_id=1, source_target_pairs={{0,64},{16,464},{32,96},{48,496},{64,128},{80,16},{96,160},{112,48... | collective-permute-start | bytes 589832 | tf_op jit(solution)/shard_map/ppermute | solution.py:36
  55.5 4.2 %collective-permute-start.4 = (bf16[1552,128]{1,0:T(8,128)(2,1)S(1)}, bf16[1552,128]{1,0:T(8,128)(2,1)S(1)}, u32[]{:S(2)}, u32[]{:S(2)}) collective-permute-start(bf16[1552,128]{1,0:T(8,128)(2,1)S(1)} %shard_map.83), channel_id=1, source_target_pairs={{0,16},{16,0},{32,48},{48,32},{64,80},{80,64},{96,112},{112,96},{1... | collective-permute-start | bytes 1191944 | tf_op jit(solution)/shard_map/ppermute | solution.py:36
  61.8 23.3 %collective-permute-start.14 = (bf16[8,128,128]{2,1,0:T(8,128)(2,1)S(1)}, bf16[8,128,128]{2,1,0:T(8,128)(2,1)S(1)}, u32[]{:S(2)}, u32[]{:S(2)}) collective-permute-start(bf16[8,128,128]{2,1,0:T(8,128)(2,1)S(1)} %shard_map.85.refs_12_), channel_id=1, source_target_pairs={{0,48},{16,32},{32,16},{48,0},{64,112},{80,96},{96,80},{112,64},{1... | collective-permute-start | bytes 786440 | tf_op jit(solution)/shard_map/ppermute | solution.py:36
  70.1 15.0 %collective-permute-start.13 = (bf16[8,128,128]{2,1,0:T(8,128)(2,1)S(1)}, bf16[8,128,128]{2,1,0:T(8,128)(2,1)S(1)}, u32[]{:S(2)}, u32[]{:S(2)}) collective-permute-start(bf16[8,128,128]{2,1,0:T(8,128)(2,1)S(1)} %shard_map.86.refs_13_), channel_id=1, source_target_pairs={{0,32},{16,48},{32,0},{48,16},{64,96},{80,112},{96,64},{112,80},{1... | collective-permute-start | bytes 786440 | tf_op jit(solution)/shard_map/ppermute | solution.py:36
  77.4 3.4 %collective-permute-start.12 = (bf16[8,128,128]{2,1,0:T(8,128)(2,1)S(1)}, bf16[8,128,128]{2,1,0:T(8,128)(2,1)S(1)}, u32[]{:S(2)}, u32[]{:S(2)}) collective-permute-start(bf16[8,128,128]{2,1,0:T(8,128)(2,1)S(1)} %get-tuple-element.12), channel_id=1, source_target_pairs={{0,16},{16,0},{32,48},{48,32},{64,80},{80,64},{96,112},{112,96},{1... | collective-permute-start | bytes 786440 | tf_op jit(solution)/shard_map/ppermute | solution.py:36

commit v5 on v4

--- a/solution.py
+++ b/solution.py
@@ -209,14 +209,16 @@
     pos = 4 * RING + jnp.sum(jnp.where(hit, (spot - 4 * RING)[None, :], 0), axis=1)
 
     steps = range(RING // 2 + 1)
+    (ahead,) = make_tiles(cuts_far, (far,), chains, (0, 1, 2, 3))
+    from_far = [send(ahead, OTHER_HALF)]
     (to_far_near,) = make_tiles(cuts_far_near, (far_near,), chains, steps)
     from_far_near = send(to_far_near, OTHER_BOTH)
-    (to_far,) = make_tiles(cuts_far, (far,), chains, steps, (to_far_near,))
-    from_far = send(to_far, OTHER_HALF)
+    (to_far,) = make_tiles(cuts_far, (far,), chains, (4,), (to_far_near,))
+    from_far.append(send(to_far, OTHER_HALF))
     near = send(copy_after(elem_t, (chains[1][3],)), OTHER_CORE)
     cuts_near = cuts_of(elem_t, near)
     mine, to_near = make_tiles(cuts_near, (elem_t, near), chains, steps, (to_far,))
-    parts = [mine, send(to_near, OTHER_CORE), from_far, from_far_near]
+    parts = [mine, send(to_near, OTHER_CORE)] + from_far + [from_far_near]
     outbox = make_outbox(pos, parts).reshape(blk_len, CAP, tile_rows, tile_rows)
     received = lax.all_to_all(outbox, "kblk", split_axis=0, concat_axis=0, tiled=True)
     return received[None, None]

time: 151 us -> 149 us (0.987)
  blocking collectives: 62 us -> 55.4 us
  starting transfers between devices: 60.1 us -> 63.1 us
    all_to_all x1, blocking collectives: 62 us -> 55.4 us  [body(): lax.all_to_all(outbox, 'kblk', split_axis=0, concat_axis=0, tiled=True)]
    ppermute x15 -> x16, starting transfers between devices: 60.1 us -> 63.1 us  [send(): return lax.ppermute(x, 'kring', perm)]
    pallas_call x3 -> x4, Pallas kernels: 5.63 us -> 6.4 us  [make_tiles(): pl.pallas_call(kernel, out_shape=(shape,) * len(elems), in_specs=[pl.Bloc...]
    ppermute x15 -> x16, waiting for transfers between devices: 10.3 us -> 10.2 us  [send(): return lax.ppermute(x, 'kring', perm)]
  transfers between devices with their start and end apart: 15 -> 16, of which waited for: 6 -> 3; matrix products, arithmetic and copies ran while one was open for 4% -> 4% of each run, Pallas kernels for 3% -> 5%
where the time goes in v5:
time: 149 us; the launch traced here: 146 us
  starting transfers between devices  63.1 us (42%)
  blocking collectives  55.4 us (37%)
  waiting for transfers between devices  10.2 us (7%)
  Pallas kernels  8.26 us (6%)
  other arithmetic  5.48 us (4%)
  local copies, waits for them, and re-layouts  3.51 us (2%)
    ppermute x16, starting transfers between devices, send(): return lax.ppermute(x, 'kring', perm)  63.1 us
    all_to_all x1, blocking collectives, body(): lax.all_to_all(outbox, 'kblk', split_axis=0, concat_axis=0, tiled=True)  55.4 us
    ppermute x16, waiting for transfers between devices, send(): return lax.ppermute(x, 'kring', perm)  10.2 us
    pallas_call x4, Pallas kernels, make_tiles(): pl.pallas_call(kernel, out_shape=(shape,) * len(elems), in_specs=[pl.Bloc...  6.4 us
    unnamed x11, local copies, waits for them, and re-layouts  3.48 us
  transfers between devices with their start and end apart: 16, of which 3 were waited for; matrix products, arithmetic and copies ran while one was open for 4% of the time, Pallas kernels for 5%

profile of v5, /device:TPU:1, one launch (start us, length us, event | category | flops | bytes accessed | tf_op | source)
XLA Modules:
  0.0 146.4 jit_solution(10579117863889291065)
XLA Ops:
  1.1 8.8 %collective-permute-start = (bf16[128,1536]{1,0:T(8,128)(2,1)S(1)}, bf16[128,1536]{1,0:T(8,128)(2,1)S(1)}, u32[]{:S(2)}, u32[]{:S(2)}) collective-permute-start(bf16[128,1536]{1,0:T(8,128)(2,1)S(1)} %pad_maximum_fusion.1.a_ref), channel_id=1, source_target_pairs={{0,16},{16,0},{32,48},{48,32},{64,80},{80,64},{96,112},{112,96},{1... | collective-permute-start | bytes 1179656 | tf_op jit(solution)/shard_map/ppermute | solution.py:36
  13.2 1.9 %collective-permute-start.5 = (bf16[2,64,1536]{2,1,0:T(8,128)(2,1)S(1)}, bf16[2,64,1536]{2,1,0:T(8,128)(2,1)S(1)}, u32[]{:S(2)}, u32[]{:S(2)}) collective-permute-start(bf16[2,64,1536]{2,1,0:T(8,128)(2,1)S(1)} %get-tuple-element.10.refs_2_.refs_3_), channel_id=1, source_target_pairs={{0,64},{16,464},{32,96},{48,496},{64,128},{80,16},{96,160},{112,48... | collective-permute-start | bytes 1179656 | tf_op jit(solution)/shard_map/ppermute | solution.py:36
  15.1 1.9 %collective-permute-start.1 = (bf16[2,64,1536]{2,1,0:T(8,128)(2,1)S(1)}, bf16[2,64,1536]{2,1,0:T(8,128)(2,1)S(1)}, u32[]{:S(2)}, u32[]{:S(2)}) collective-permute-start(bf16[2,64,1536]{2,1,0:T(8,128)(2,1)S(1)} %get-tuple-element.9.refs_3_.refs_4_), channel_id=1, source_target_pairs={{0,64},{16,464},{32,96},{48,496},{64,128},{80,16},{96,160},{112,48... | collective-permute-start | bytes 1179656 | tf_op jit(solution)/shard_map/ppermute | solution.py:36
  17.1 9.5 %collective-permute-start.10 = (bf16[1552,128]{1,0:T(8,128)(2,1)S(1)}, bf16[1552,128]{1,0:T(8,128)(2,1)}, u32[]{:S(2)}, u32[]{:S(2)}) collective-permute-start(bf16[1552,128]{1,0:T(8,128)(2,1)S(1)} %pad_maximum_fusion.x_ref.refs_1_), channel_id=1, source_target_pairs={{0,32},{16,48},{32,0},{48,16},{64,96},{80,112},{96,64},{112,80},{1... | collective-permute-start | bytes 1191944 | tf_op jit(solution)/shard_map/ppermute | solution.py:36
  26.7 3.0 %collective-permute-start.6 = (bf16[2,64,1536]{2,1,0:T(8,128)(2,1)S(1)}, bf16[2,64,1536]{2,1,0:T(8,128)(2,1)S(1)}, u32[]{:S(2)}, u32[]{:S(2)}) collective-permute-start(bf16[2,64,1536]{2,1,0:T(8,128)(2,1)S(1)} %collective-permute-done.5.refs_4_.refs_5_), channel_id=1, source_target_pairs={{0,64},{16,464},{32,96},{48,496},{64,128},{80,16},{96,160},{112,48... | collective-permute-start | bytes 1179656 | tf_op jit(solution)/shard_map/ppermute | solution.py:36
  29.7 3.0 %collective-permute-start.2 = (bf16[2,64,1536]{2,1,0:T(8,128)(2,1)S(1)}, bf16[2,64,1536]{2,1,0:T(8,128)(2,1)S(1)}, u32[]{:S(2)}, u32[]{:S(2)}) collective-permute-start(bf16[2,64,1536]{2,1,0:T(8,128)(2,1)S(1)} %collective-permute-done.1.refs_5_.refs_6_), channel_id=1, source_target_pairs={{0,64},{16,464},{32,96},{48,496},{64,128},{80,16},{96,160},{112,48... | collective-permute-start | bytes 1179656 | tf_op jit(solution)/shard_map/ppermute | solution.py:36
  32.7 2.8 %collective-permute-done.6.refs_6_.refs_7_ = bf16[2,64,1536]{2,1,0:T(8,128)(2,1)S(1)} collective-permute-done((bf16[2,64,1536]{2,1,0:T(8,128)(2,1)S(1)}, bf16[2,64,1536]{2,1,0:T(8,128)(2,1)S(1)}, u32[]{:S(2)}, u32[]{:S(2)}) %collective-permute-start.6) | collective-permute-done | bytes 393248 | tf_op jit(solution)/shard_map/ppermute | solution.py:36
  35.5 4.1 %collective-permute-start.7 = (bf16[2,64,1536]{2,1,0:T(8,128)(2,1)S(1)}, bf16[2,64,1536]{2,1,0:T(8,128)(2,1)S(1)}, u32[]{:S(2)}, u32[]{:S(2)}) collective-permute-start(bf16[2,64,1536]{2,1,0:T(8,128)(2,1)S(1)} %collective-permute-done.6.refs_6_.refs_7_), channel_id=1, source_target_pairs={{0,64},{16,464},{32,96},{48,496},{64,128},{80,16},{96,160},{112,48... | collective-permute-start | bytes 1179656 | tf_op jit(solution)/shard_map/ppermute | solution.py:36
  39.7 3.9 %collective-permute-start.3 = (bf16[2,64,1536]{2,1,0:T(8,128)(2,1)S(1)}, bf16[2,64,1536]{2,1,0:T(8,128)(2,1)S(1)}, u32[]{:S(2)}, u32[]{:S(2)}) collective-permute-start(bf16[2,64,1536]{2,1,0:T(8,128)(2,1)S(1)} %collective-permute-done.2.refs_7_.refs_8_), channel_id=1, source_target_pairs={{0,64},{16,464},{32,96},{48,496},{64,128},{80,16},{96,160},{112,48... | collective-permute-start | bytes 1179656 | tf_op jit(solution)/shard_map/ppermute | solution.py:36
  43.6 1.2 fusion.22
  47.5 3.1 %collective-permute-start.11 = (bf16[1552,128]{1,0:T(8,128)(2,1)S(1)}, bf16[1552,128]{1,0:T(8,128)(2,1)S(1)}, u32[]{:S(2)}, u32[]{:S(2)}) collective-permute-start(bf16[1552,128]{1,0:T(8,128)(2,1)S(1)} %shard_map.84.refs_1_), channel_id=1, source_target_pairs={{0,16},{16,0},{32,48},{48,32},{64,80},{80,64},{96,112},{112,96},{1... | collective-permute-start | bytes 1191944 | tf_op jit(solution)/shard_map/ppermute | solution.py:36
  50.6 3.0 %collective-permute-start.8 = (bf16[1,64,1536]{2,1,0:T(8,128)(2,1)S(1)}, bf16[1,64,1536]{2,1,0:T(8,128)(2,1)S(1)}, u32[]{:S(2)}, u32[]{:S(2)}) collective-permute-start(bf16[1,64,1536]{2,1,0:T(8,128)(2,1)S(1)} %slice.48), channel_id=1, source_target_pairs={{0,64},{16,464},{32,96},{48,496},{64,128},{80,16},{96,160},{112,48... | collective-permute-start | bytes 589832 | tf_op jit(solution)/shard_map/ppermute | solution.py:36
  53.6 1.9 %collective-permute-start.9 = (bf16[1,64,1536]{2,1,0:T(8,128)(2,1)S(1)}, bf16[1,64,1536]{2,1,0:T(8,128)(2,1)S(1)}, u32[]{:S(2)}, u32[]{:S(2)}) collective-permute-start(bf16[1,64,1536]{2,1,0:T(8,128)(2,1)S(1)} %slice.49), channel_id=1, source_target_pairs={{0,64},{16,464},{32,96},{48,496},{64,128},{80,16},{96,160},{112,48... | collective-permute-start | bytes 589832 | tf_op jit(solution)/shard_map/ppermute | solution.py:36
  55.6 2.8 %collective-permute-start.4 = (bf16[1552,128]{1,0:T(8,128)(2,1)S(1)}, bf16[1552,128]{1,0:T(8,128)(2,1)S(1)}, u32[]{:S(2)}, u32[]{:S(2)}) collective-permute-start(bf16[1552,128]{1,0:T(8,128)(2,1)S(1)} %shard_map.83), channel_id=1, source_target_pairs={{0,16},{16,0},{32,48},{48,32},{64,80},{80,64},{96,112},{112,96},{1... | collective-permute-start | bytes 1191944 | tf_op jit(solution)/shard_map/ppermute | solution.py:36
  58.6 1.5 %shard_map.88 = bf16[7,128,128]{2,1,0:T(8,128)(2,1)S(1)} custom-call(s32[1,8]{1,0:T(1,128)S(1)} %bitcast.51, bf16[1552,128]{1,0:T(8,128)(2,1)S(1)} %shard_map.84.refs_1_, bf16[2,64,1536]{2,1,0:T(8,128)(2,1)S(1)} %get-tuple-element.10.refs_2_.refs_3_, bf16[2,64,1536]{2,1,0:T(8,128)(2,1)S(1)} %get-tuple-element.9.refs_3_.refs_4_, ...), custom_call_target="tpu_custom_call" | custom-call | flops 352321536 | bytes 2752512 | tf_op jit(solution)/shard_map/pallas_call | solution.py:76
  60.1 4.9 %collective-permute-start.13 = (bf16[7,128,128]{2,1,0:T(8,128)(2,1)S(1)}, bf16[7,128,128]{2,1,0:T(8,128)(2,1)S(1)}, u32[]{:S(2)}, u32[]{:S(2)}) collective-permute-start(bf16[7,128,128]{2,1,0:T(8,128)(2,1)S(1)} %shard_map.88), channel_id=1, source_target_pairs={{0,32},{16,48},{32,0},{48,16},{64,96},{80,112},{96,64},{112,80},{1... | collective-permute-start | bytes 688136 | tf_op jit(solution)/shard_map/ppermute | solution.py:36
  65.0 1.6 %shard_map.85.refs_4_ = bf16[8,128,128]{2,1,0:T(8,128)(2,1)S(1)} custom-call(s32[1,8]{1,0:T(1,128)S(1)} %bitcast.53, bf16[1552,128]{1,0:T(8,128)(2,1)S(1)} %collective-permute-done.11.refs_1_, bf16[2,64,1536]{2,1,0:T(8,128)(2,1)S(1)} %get-tuple-element.10.refs_2_.refs_3_, bf16[2,64,1536]{2,1,0:T(8,128)(2,1)S(1)} %get-tuple-element.9.refs_3_.refs_4_, ...), custom_call_target="tpu_custom_call" | custom-call | flops 402653184 | bytes 3145728 | tf_op jit(solution)/shard_map/pallas_call | solution.py:76
  66.6 4.5 %collective-permute-start.15 = (bf16[8,128,128]{2,1,0:T(8,128)(2,1)S(1)}, bf16[8,128,128]{2,1,0:T(8,128)(2,1)S(1)}, u32[]{:S(2)}, u32[]{:S(2)}) collective-permute-start(bf16[8,128,128]{2,1,0:T(8,128)(2,1)S(1)} %shard_map.85.refs_4_), channel_id=1, source_target_pairs={{0,48},{16,32},{32,16},{48,0},{64,112},{80,96},{96,80},{112,64},{1... | collective-permute-start | bytes 786440 | tf_op jit(solution)/shard_map/ppermute | solution.py:36
  72.2 2.4 %shard_map.87 = (bf16[8,128,128]{2,1,0:T(8,128)(2,1)S(1)}, bf16[8,128,128]{2,1,0:T(8,128)(2,1)S(1)}) custom-call(s32[2,8]{1,0:T(2,128)S(1)} %select_reduce_fusion.1.refs_0_, bf16[1552,128]{1,0:T(8,128)(2,1)S(1)} %pad_maximum_fusion.x_ref.refs_1_, bf16[1552,128]{1,0:T(8,128)(2,1)S(1)} %collective-permute-done.4.refs_2_, ...), custom_call_target="tpu_custom_call" | custom-call | flops 805306368 | bytes 3145728 | tf_op jit(solution)/shard_map/pallas_call | solution.py:76
  74.6 2.1 %collective-permute-start.12 = (bf16[8,128,128]{2,1,0:T(8,128)(2,1)S(1)}, bf16[8,128,128]{2,1,0:T(8,128)(2,1)S(1)}, u32[]{:S(2)}, u32[]{:S(2)}) collective-permute-start(bf16[8,128,128]{2,1,0:T(8,128)(2,1)S(1)} %get-tuple-element.12), channel_id=1, source_target_pairs={{0,16},{16,0},{32,48},{48,32},{64,80},{80,64},{96,112},{112,96},{1... | collective-permute-start | bytes 786440 | tf_op jit(solution)/shard_map/ppermute | solution.py:36
  76.9 4.8 %collective-permute-start.14 = (bf16[1,128,128]{2,1,0:T(8,128)(2,1)S(1)}, bf16[1,128,128]{2,1,0:T(8,128)(2,1)S(1)}, u32[]{:S(2)}, u32[]{:S(2)}) collective-permute-start(bf16[1,128,128]{2,1,0:T(8,128)(2,1)S(1)} %shard_map.86.refs_13_), channel_id=1, source_target_pairs={{0,32},{16,48},{32,0},{48,16},{64,96},{80,112},{96,64},{112,80},{1... | collective-permute-start | bytes 98312 | tf_op jit(solution)/shard_map/ppermute | solution.py:36
  81.7 7.3 %collective-permute-done.14.refs_3_ = bf16[1,128,128]{2,1,0:T(8,128)(2,1)S(1)} collective-permute-done((bf16[1,128,128]{2,1,0:T(8,128)(2,1)S(1)}, bf16[1,128,128]{2,1,0:T(8,128)(2,1)S(1)}, u32[]{:S(2)}, u32[]{:S(2)}) %collective-permute-start.14) | collective-permute-done | bytes 32800 | tf_op jit(solution)/shard_map/ppermute | solution.py:36
  89.8 55.4 %all_to_all.5 = bf16[16,4,128,128]{3,2,1,0:T(8,128)(2,1)S(1)} all-to-all(bf16[16,4,128,128]{3,2,1,0:T(8,128)(2,1)S(1)} %bitcast.50), channel_id=1, replica_groups=mesh['kring'=32,'kblk'=16] {'kblk'}, dimensions={0} | all-to-all | bytes 4194304 | tf_op jit(solution)/shard_map/all_to_all | solution.py:223
  145.1 1.3 copy.14
  (54 shorter events, 9.3 us)
Async XLA Ops:
  0.0 12.9 %copy-start = (f32[512]{0:T(512)S(1)}, f32[512]{0:T(512)}, u32[]{:S(2)}) copy-start(f32[512]{0:T(512)} %param.13) | copy-start | bytes 6148
  0.0 17.0 %copy-start.3 = (s32[1,1,32]{2,1,0:T(1,128)S(1)}, s32[1,1,32]{2,1,0:T(1,128)}, u32[]{:S(2)}) copy-start(s32[1,1,32]{2,1,0:T(1,128)} %param.14) | copy-start | bytes 388
  1.1 12.0 %collective-permute-start = (bf16[128,1536]{1,0:T(8,128)(2,1)S(1)}, bf16[128,1536]{1,0:T(8,128)(2,1)S(1)}, u32[]{:S(2)}, u32[]{:S(2)}) collective-permute-start(bf16[128,1536]{1,0:T(8,128)(2,1)S(1)} %pad_maximum_fusion.1.a_ref), channel_id=1, source_target_pairs={{0,16},{16,0},{32,48},{48,32},{64,80},{80,64},{96,112},{112,96},{1... | collective-permute-start | bytes 1179656 | tf_op jit(solution)/shard_map/ppermute | solution.py:36
  13.2 13.5 %collective-permute-start.5 = (bf16[2,64,1536]{2,1,0:T(8,128)(2,1)S(1)}, bf16[2,64,1536]{2,1,0:T(8,128)(2,1)S(1)}, u32[]{:S(2)}, u32[]{:S(2)}) collective-permute-start(bf16[2,64,1536]{2,1,0:T(8,128)(2,1)S(1)} %get-tuple-element.10.refs_2_.refs_3_), channel_id=1, source_target_pairs={{0,64},{16,464},{32,96},{48,496},{64,128},{80,16},{96,160},{112,48... | collective-permute-start | bytes 1179656 | tf_op jit(solution)/shard_map/ppermute | solution.py:36
  15.1 14.6 %collective-permute-start.1 = (bf16[2,64,1536]{2,1,0:T(8,128)(2,1)S(1)}, bf16[2,64,1536]{2,1,0:T(8,128)(2,1)S(1)}, u32[]{:S(2)}, u32[]{:S(2)}) collective-permute-start(bf16[2,64,1536]{2,1,0:T(8,128)(2,1)S(1)} %get-tuple-element.9.refs_3_.refs_4_), channel_id=1, source_target_pairs={{0,64},{16,464},{32,96},{48,496},{64,128},{80,16},{96,160},{112,48... | collective-permute-start | bytes 1179656 | tf_op jit(solution)/shard_map/ppermute | solution.py:36
  17.1 29.3 %collective-permute-start.10 = (bf16[1552,128]{1,0:T(8,128)(2,1)S(1)}, bf16[1552,128]{1,0:T(8,128)(2,1)}, u32[]{:S(2)}, u32[]{:S(2)}) collective-permute-start(bf16[1552,128]{1,0:T(8,128)(2,1)S(1)} %pad_maximum_fusion.x_ref.refs_1_), channel_id=1, source_target_pairs={{0,32},{16,48},{32,0},{48,16},{64,96},{80,112},{96,64},{112,80},{1... | collective-permute-start | bytes 1191944 | tf_op jit(solution)/shard_map/ppermute | solution.py:36
  26.7 8.8 %collective-permute-start.6 = (bf16[2,64,1536]{2,1,0:T(8,128)(2,1)S(1)}, bf16[2,64,1536]{2,1,0:T(8,128)(2,1)S(1)}, u32[]{:S(2)}, u32[]{:S(2)}) collective-permute-start(bf16[2,64,1536]{2,1,0:T(8,128)(2,1)S(1)} %collective-permute-done.5.refs_4_.refs_5_), channel_id=1, source_target_pairs={{0,64},{16,464},{32,96},{48,496},{64,128},{80,16},{96,160},{112,48... | collective-permute-start | bytes 1179656 | tf_op jit(solution)/shard_map/ppermute | solution.py:36
  29.7 10.0 %collective-permute-start.2 = (bf16[2,64,1536]{2,1,0:T(8,128)(2,1)S(1)}, bf16[2,64,1536]{2,1,0:T(8,128)(2,1)S(1)}, u32[]{:S(2)}, u32[]{:S(2)}) collective-permute-start(bf16[2,64,1536]{2,1,0:T(8,128)(2,1)S(1)} %collective-permute-done.1.refs_5_.refs_6_), channel_id=1, source_target_pairs={{0,64},{16,464},{32,96},{48,496},{64,128},{80,16},{96,160},{112,48... | collective-permute-start | bytes 1179656 | tf_op jit(solution)/shard_map/ppermute | solution.py:36
  35.5 11.0 %collective-permute-start.7 = (bf16[2,64,1536]{2,1,0:T(8,128)(2,1)S(1)}, bf16[2,64,1536]{2,1,0:T(8,128)(2,1)S(1)}, u32[]{:S(2)}, u32[]{:S(2)}) collective-permute-start(bf16[2,64,1536]{2,1,0:T(8,128)(2,1)S(1)} %collective-permute-done.6.refs_6_.refs_7_), channel_id=1, source_target_pairs={{0,64},{16,464},{32,96},{48,496},{64,128},{80,16},{96,160},{112,48... | collective-permute-start | bytes 1179656 | tf_op jit(solution)/shard_map/ppermute | solution.py:36
  39.7 13.9 %collective-permute-start.3 = (bf16[2,64,1536]{2,1,0:T(8,128)(2,1)S(1)}, bf16[2,64,1536]{2,1,0:T(8,128)(2,1)S(1)}, u32[]{:S(2)}, u32[]{:S(2)}) collective-permute-start(bf16[2,64,1536]{2,1,0:T(8,128)(2,1)S(1)} %collective-permute-done.2.refs_7_.refs_8_), channel_id=1, source_target_pairs={{0,64},{16,464},{32,96},{48,496},{64,128},{80,16},{96,160},{112,48... | collective-permute-start | bytes 1179656 | tf_op jit(solution)/shard_map/ppermute | solution.py:36
  47.5 10.9 %collective-permute-start.11 = (bf16[1552,128]{1,0:T(8,128)(2,1)S(1)}, bf16[1552,128]{1,0:T(8,128)(2,1)S(1)}, u32[]{:S(2)}, u32[]{:S(2)}) collective-permute-start(bf16[1552,128]{1,0:T(8,128)(2,1)S(1)} %shard_map.84.refs_1_), channel_id=1, source_target_pairs={{0,16},{16,0},{32,48},{48,32},{64,80},{80,64},{96,112},{112,96},{1... | collective-permute-start | bytes 1191944 | tf_op jit(solution)/shard_map/ppermute | solution.py:36
  50.6 14.4 %collective-permute-start.8 = (bf16[1,64,1536]{2,1,0:T(8,128)(2,1)S(1)}, bf16[1,64,1536]{2,1,0:T(8,128)(2,1)S(1)}, u32[]{:S(2)}, u32[]{:S(2)}) collective-permute-start(bf16[1,64,1536]{2,1,0:T(8,128)(2,1)S(1)} %slice.48), channel_id=1, source_target_pairs={{0,64},{16,464},{32,96},{48,496},{64,128},{80,16},{96,160},{112,48... | collective-permute-start | bytes 589832 | tf_op jit(solution)/shard_map/ppermute | solution.py:36
  53.6 11.4 %collective-permute-start.9 = (bf16[1,64,1536]{2,1,0:T(8,128)(2,1)S(1)}, bf16[1,64,1536]{2,1,0:T(8,128)(2,1)S(1)}, u32[]{:S(2)}, u32[]{:S(2)}) collective-permute-start(bf16[1,64,1536]{2,1,0:T(8,128)(2,1)S(1)} %slice.49), channel_id=1, source_target_pairs={{0,64},{16,464},{32,96},{48,496},{64,128},{80,16},{96,160},{112,48... | collective-permute-start | bytes 589832 | tf_op jit(solution)/shard_map/ppermute | solution.py:36
  55.6 9.4 %copy-start.1 = (bf16[1,1,32]{2,1,0:T(2,128)(2,1)S(1)}, bf16[1,1,32]{2,1,0:T(2,128)(2,1)}, u32[]{:S(2)}) copy-start(bf16[1,1,32]{2,1,0:T(2,128)(2,1)} %get-tuple-element.15) | copy-start | bytes 196
  55.6 9.4 %copy-start.2 = (bf16[1,1,32]{2,1,0:T(2,128)(2,1)S(1)}, bf16[1,1,32]{2,1,0:T(2,128)(2,1)}, u32[]{:S(2)}) copy-start(bf16[1,1,32]{2,1,0:T(2,128)(2,1)} %get-tuple-element.16) | copy-start | bytes 196
  55.6 9.4 %collective-permute-start.4 = (bf16[1552,128]{1,0:T(8,128)(2,1)S(1)}, bf16[1552,128]{1,0:T(8,128)(2,1)S(1)}, u32[]{:S(2)}, u32[]{:S(2)}) collective-permute-start(bf16[1552,128]{1,0:T(8,128)(2,1)S(1)} %shard_map.83), channel_id=1, source_target_pairs={{0,16},{16,0},{32,48},{48,32},{64,80},{80,64},{96,112},{112,96},{1... | collective-permute-start | bytes 1191944 | tf_op jit(solution)/shard_map/ppermute | solution.py:36
  60.1 28.9 %collective-permute-start.13 = (bf16[7,128,128]{2,1,0:T(8,128)(2,1)S(1)}, bf16[7,128,128]{2,1,0:T(8,128)(2,1)S(1)}, u32[]{:S(2)}, u32[]{:S(2)}) collective-permute-start(bf16[7,128,128]{2,1,0:T(8,128)(2,1)S(1)} %shard_map.88), channel_id=1, source_target_pairs={{0,32},{16,48},{32,0},{48,16},{64,96},{80,112},{96,64},{112,80},{1... | collective-permute-start | bytes 688136 | tf_op jit(solution)/shard_map/ppermute | solution.py:36
  66.6 22.4 %collective-permute-start.15 = (bf16[8,128,128]{2,1,0:T(8,128)(2,1)S(1)}, bf16[8,128,128]{2,1,0:T(8,128)(2,1)S(1)}, u32[]{:S(2)}, u32[]{:S(2)}) collective-permute-start(bf16[8,128,128]{2,1,0:T(8,128)(2,1)S(1)} %shard_map.85.refs_4_), channel_id=1, source_target_pairs={{0,48},{16,32},{32,16},{48,0},{64,112},{80,96},{96,80},{112,64},{1... | collective-permute-start | bytes 786440 | tf_op jit(solution)/shard_map/ppermute | solution.py:36
  74.6 14.4 %collective-permute-start.12 = (bf16[8,128,128]{2,1,0:T(8,128)(2,1)S(1)}, bf16[8,128,128]{2,1,0:T(8,128)(2,1)S(1)}, u32[]{:S(2)}, u32[]{:S(2)}) collective-permute-start(bf16[8,128,128]{2,1,0:T(8,128)(2,1)S(1)} %get-tuple-element.12), channel_id=1, source_target_pairs={{0,16},{16,0},{32,48},{48,32},{64,80},{80,64},{96,112},{112,96},{1... | collective-permute-start | bytes 786440 | tf_op jit(solution)/shard_map/ppermute | solution.py:36
  76.9 12.1 %collective-permute-start.14 = (bf16[1,128,128]{2,1,0:T(8,128)(2,1)S(1)}, bf16[1,128,128]{2,1,0:T(8,128)(2,1)S(1)}, u32[]{:S(2)}, u32[]{:S(2)}) collective-permute-start(bf16[1,128,128]{2,1,0:T(8,128)(2,1)S(1)} %shard_map.86.refs_13_), channel_id=1, source_target_pairs={{0,32},{16,48},{32,0},{48,16},{64,96},{80,112},{96,64},{112,80},{1... | collective-permute-start | bytes 98312 | tf_op jit(solution)/shard_map/ppermute | solution.py:36

commit v6 on v5

--- a/solution.py
+++ b/solution.py
@@ -215,7 +215,7 @@
     from_far_near = send(to_far_near, OTHER_BOTH)
     (to_far,) = make_tiles(cuts_far, (far,), chains, (4,), (to_far_near,))
     from_far.append(send(to_far, OTHER_HALF))
-    near = send(copy_after(elem_t, (chains[1][3],)), OTHER_CORE)
+    near = send(copy_after(elem_t, (chains[1][2],)), OTHER_CORE)
     cuts_near = cuts_of(elem_t, near)
     mine, to_near = make_tiles(cuts_near, (elem_t, near), chains, steps, (to_far,))
     parts = [mine, send(to_near, OTHER_CORE)] + from_far + [from_far_near]

time: 149 us -> 148 us (level)
  transfers between devices with their start and end apart: 16 -> 16, of which waited for: 3 -> 3; matrix products, arithmetic and copies ran while one was open for 4% -> 5% of each run, Pallas kernels for 5% -> 5%
where the time goes in v6:
time: 148 us; the launch traced here: 146 us
  starting transfers between devices  63.4 us (43%)
  blocking collectives  55.6 us (38%)
  waiting for transfers between devices  9.32 us (6%)
  Pallas kernels  8.25 us (6%)
  other arithmetic  5.48 us (4%)
  local copies, waits for them, and re-layouts  3.51 us (2%)
    ppermute x16, starting transfers between devices, send(): return lax.ppermute(x, 'kring', perm)  63.4 us
    all_to_all x1, blocking collectives, body(): lax.all_to_all(outbox, 'kblk', split_axis=0, concat_axis=0, tiled=True)  55.6 us
    ppermute x16, waiting for transfers between devices, send(): return lax.ppermute(x, 'kring', perm)  9.32 us
    pallas_call x4, Pallas kernels, make_tiles(): pl.pallas_call(kernel, out_shape=(shape,) * len(elems), in_specs=[pl.Bloc...  6.4 us
    unnamed x11, local copies, waits for them, and re-layouts  3.48 us
  transfers between devices with their start and end apart: 16, of which 3 were waited for; matrix products, arithmetic and copies ran while one was open for 5% of the time, Pallas kernels for 5%

profile of v6, /device:TPU:1, one launch (start us, length us, event | category | flops | bytes accessed | tf_op | source)
XLA Modules:
  0.0 146.0 jit_solution(6264604386216499856)
XLA Ops:
  1.1 8.8 %collective-permute-start = (bf16[128,1536]{1,0:T(8,128)(2,1)S(1)}, bf16[128,1536]{1,0:T(8,128)(2,1)S(1)}, u32[]{:S(2)}, u32[]{:S(2)}) collective-permute-start(bf16[128,1536]{1,0:T(8,128)(2,1)S(1)} %pad_maximum_fusion.1.a_ref), channel_id=1, source_target_pairs={{0,16},{16,0},{32,48},{48,32},{64,80},{80,64},{96,112},{112,96},{1... | collective-permute-start | bytes 1179656 | tf_op jit(solution)/shard_map/ppermute | solution.py:36
  13.2 1.9 %collective-permute-start.4 = (bf16[2,64,1536]{2,1,0:T(8,128)(2,1)S(1)}, bf16[2,64,1536]{2,1,0:T(8,128)(2,1)S(1)}, u32[]{:S(2)}, u32[]{:S(2)}) collective-permute-start(bf16[2,64,1536]{2,1,0:T(8,128)(2,1)S(1)} %get-tuple-element.10.refs_2_.refs_3_), channel_id=1, source_target_pairs={{0,64},{16,464},{32,96},{48,496},{64,128},{80,16},{96,160},{112,48... | collective-permute-start | bytes 1179656 | tf_op jit(solution)/shard_map/ppermute | solution.py:36
  15.1 1.9 %collective-permute-start.1 = (bf16[2,64,1536]{2,1,0:T(8,128)(2,1)S(1)}, bf16[2,64,1536]{2,1,0:T(8,128)(2,1)S(1)}, u32[]{:S(2)}, u32[]{:S(2)}) collective-permute-start(bf16[2,64,1536]{2,1,0:T(8,128)(2,1)S(1)} %get-tuple-element.9.refs_3_.refs_4_), channel_id=1, source_target_pairs={{0,64},{16,464},{32,96},{48,496},{64,128},{80,16},{96,160},{112,48... | collective-permute-start | bytes 1179656 | tf_op jit(solution)/shard_map/ppermute | solution.py:36
  17.1 9.5 %collective-permute-start.10 = (bf16[1552,128]{1,0:T(8,128)(2,1)S(1)}, bf16[1552,128]{1,0:T(8,128)(2,1)}, u32[]{:S(2)}, u32[]{:S(2)}) collective-permute-start(bf16[1552,128]{1,0:T(8,128)(2,1)S(1)} %pad_maximum_fusion.x_ref.refs_1_), channel_id=1, source_target_pairs={{0,32},{16,48},{32,0},{48,16},{64,96},{80,112},{96,64},{112,80},{1... | collective-permute-start | bytes 1191944 | tf_op jit(solution)/shard_map/ppermute | solution.py:36
  26.7 3.0 %collective-permute-start.5 = (bf16[2,64,1536]{2,1,0:T(8,128)(2,1)S(1)}, bf16[2,64,1536]{2,1,0:T(8,128)(2,1)S(1)}, u32[]{:S(2)}, u32[]{:S(2)}) collective-permute-start(bf16[2,64,1536]{2,1,0:T(8,128)(2,1)S(1)} %collective-permute-done.4.refs_4_.refs_5_), channel_id=1, source_target_pairs={{0,64},{16,464},{32,96},{48,496},{64,128},{80,16},{96,160},{112,48... | collective-permute-start | bytes 1179656 | tf_op jit(solution)/shard_map/ppermute | solution.py:36
  29.7 3.0 %collective-permute-start.2 = (bf16[2,64,1536]{2,1,0:T(8,128)(2,1)S(1)}, bf16[2,64,1536]{2,1,0:T(8,128)(2,1)S(1)}, u32[]{:S(2)}, u32[]{:S(2)}) collective-permute-start(bf16[2,64,1536]{2,1,0:T(8,128)(2,1)S(1)} %collective-permute-done.1.refs_5_.refs_6_), channel_id=1, source_target_pairs={{0,64},{16,464},{32,96},{48,496},{64,128},{80,16},{96,160},{112,48... | collective-permute-start | bytes 1179656 | tf_op jit(solution)/shard_map/ppermute | solution.py:36
  32.7 2.8 %collective-permute-done.5.refs_6_.refs_7_ = bf16[2,64,1536]{2,1,0:T(8,128)(2,1)S(1)} collective-permute-done((bf16[2,64,1536]{2,1,0:T(8,128)(2,1)S(1)}, bf16[2,64,1536]{2,1,0:T(8,128)(2,1)S(1)}, u32[]{:S(2)}, u32[]{:S(2)}) %collective-permute-start.5) | collective-permute-done | bytes 393248 | tf_op jit(solution)/shard_map/ppermute | solution.py:36
  35.5 4.1 %collective-permute-start.6 = (bf16[2,64,1536]{2,1,0:T(8,128)(2,1)S(1)}, bf16[2,64,1536]{2,1,0:T(8,128)(2,1)S(1)}, u32[]{:S(2)}, u32[]{:S(2)}) collective-permute-start(bf16[2,64,1536]{2,1,0:T(8,128)(2,1)S(1)} %collective-permute-done.5.refs_6_.refs_7_), channel_id=1, source_target_pairs={{0,64},{16,464},{32,96},{48,496},{64,128},{80,16},{96,160},{112,48... | collective-permute-start | bytes 1179656 | tf_op jit(solution)/shard_map/ppermute | solution.py:36
  39.7 3.9 %collective-permute-start.7 = (bf16[2,64,1536]{2,1,0:T(8,128)(2,1)S(1)}, bf16[2,64,1536]{2,1,0:T(8,128)(2,1)S(1)}, u32[]{:S(2)}, u32[]{:S(2)}) collective-permute-start(bf16[2,64,1536]{2,1,0:T(8,128)(2,1)S(1)} %collective-permute-done.2.refs_0_.refs_7_.refs_8_), channel_id=1, source_target_pairs={{0,64},{16,464},{32,96},{48,496},{64,128},{80,16},{96,160},{112,48... | collective-permute-start | bytes 1179656 | tf_op jit(solution)/shard_map/ppermute | solution.py:36
  43.6 1.2 fusion.22
  46.5 2.0 %collective-permute-start.3 = (bf16[1552,128]{1,0:T(8,128)(2,1)S(1)}, bf16[1552,128]{1,0:T(8,128)(2,1)S(1)}, u32[]{:S(2)}, u32[]{:S(2)}) collective-permute-start(bf16[1552,128]{1,0:T(8,128)(2,1)S(1)} %shard_map.83), channel_id=1, source_target_pairs={{0,16},{16,0},{32,48},{48,32},{64,80},{80,64},{96,112},{112,96},{1... | collective-permute-start | bytes 1191944 | tf_op jit(solution)/shard_map/ppermute | solution.py:36
  49.6 2.3 %collective-permute-start.11 = (bf16[1552,128]{1,0:T(8,128)(2,1)S(1)}, bf16[1552,128]{1,0:T(8,128)(2,1)S(1)}, u32[]{:S(2)}, u32[]{:S(2)}) collective-permute-start(bf16[1552,128]{1,0:T(8,128)(2,1)S(1)} %shard_map.84.refs_1_), channel_id=1, source_target_pairs={{0,16},{16,0},{32,48},{48,32},{64,80},{80,64},{96,112},{112,96},{1... | collective-permute-start | bytes 1191944 | tf_op jit(solution)/shard_map/ppermute | solution.py:36
  51.9 3.6 %collective-permute-start.8 = (bf16[1,64,1536]{2,1,0:T(8,128)(2,1)S(1)}, bf16[1,64,1536]{2,1,0:T(8,128)(2,1)S(1)}, u32[]{:S(2)}, u32[]{:S(2)}) collective-permute-start(bf16[1,64,1536]{2,1,0:T(8,128)(2,1)S(1)} %slice.48), channel_id=1, source_target_pairs={{0,64},{16,464},{32,96},{48,496},{64,128},{80,16},{96,160},{112,48... | collective-permute-start | bytes 589832 | tf_op jit(solution)/shard_map/ppermute | solution.py:36
  55.6 1.9 %collective-permute-start.9 = (bf16[1,64,1536]{2,1,0:T(8,128)(2,1)S(1)}, bf16[1,64,1536]{2,1,0:T(8,128)(2,1)S(1)}, u32[]{:S(2)}, u32[]{:S(2)}) collective-permute-start(bf16[1,64,1536]{2,1,0:T(8,128)(2,1)S(1)} %slice.49), channel_id=1, source_target_pairs={{0,64},{16,464},{32,96},{48,496},{64,128},{80,16},{96,160},{112,48... | collective-permute-start | bytes 589832 | tf_op jit(solution)/shard_map/ppermute | solution.py:36
  57.9 1.5 %shard_map.88 = bf16[7,128,128]{2,1,0:T(8,128)(2,1)S(1)} custom-call(s32[1,8]{1,0:T(1,128)S(1)} %bitcast.51, bf16[1552,128]{1,0:T(8,128)(2,1)S(1)} %shard_map.84.refs_1_, bf16[2,64,1536]{2,1,0:T(8,128)(2,1)S(1)} %get-tuple-element.10.refs_2_.refs_3_, bf16[2,64,1536]{2,1,0:T(8,128)(2,1)S(1)} %get-tuple-element.9.refs_3_.refs_4_, ...), custom_call_target="tpu_custom_call" | custom-call | flops 352321536 | bytes 2752512 | tf_op jit(solution)/shard_map/pallas_call | solution.py:76
  59.4 3.7 %collective-permute-start.13 = (bf16[7,128,128]{2,1,0:T(8,128)(2,1)S(1)}, bf16[7,128,128]{2,1,0:T(8,128)(2,1)S(1)}, u32[]{:S(2)}, u32[]{:S(2)}) collective-permute-start(bf16[7,128,128]{2,1,0:T(8,128)(2,1)S(1)} %shard_map.88), channel_id=1, source_target_pairs={{0,32},{16,48},{32,0},{48,16},{64,96},{80,112},{96,64},{112,80},{1... | collective-permute-start | bytes 688136 | tf_op jit(solution)/shard_map/ppermute | solution.py:36
  63.1 1.6 %shard_map.85.refs_4_ = bf16[8,128,128]{2,1,0:T(8,128)(2,1)S(1)} custom-call(s32[1,8]{1,0:T(1,128)S(1)} %bitcast.53, bf16[1552,128]{1,0:T(8,128)(2,1)S(1)} %collective-permute-done.11.refs_1_, bf16[2,64,1536]{2,1,0:T(8,128)(2,1)S(1)} %get-tuple-element.10.refs_2_.refs_3_, bf16[2,64,1536]{2,1,0:T(8,128)(2,1)S(1)} %get-tuple-element.9.refs_3_.refs_4_, ...), custom_call_target="tpu_custom_call" | custom-call | flops 402653184 | bytes 3145728 | tf_op jit(solution)/shard_map/pallas_call | solution.py:76
  64.7 7.0 %collective-permute-start.15 = (bf16[8,128,128]{2,1,0:T(8,128)(2,1)S(1)}, bf16[8,128,128]{2,1,0:T(8,128)(2,1)S(1)}, u32[]{:S(2)}, u32[]{:S(2)}) collective-permute-start(bf16[8,128,128]{2,1,0:T(8,128)(2,1)S(1)} %shard_map.85.refs_4_), channel_id=1, source_target_pairs={{0,48},{16,32},{32,16},{48,0},{64,112},{80,96},{96,80},{112,64},{1... | collective-permute-start | bytes 786440 | tf_op jit(solution)/shard_map/ppermute | solution.py:36
  72.6 2.4 %shard_map.87 = (bf16[8,128,128]{2,1,0:T(8,128)(2,1)S(1)}, bf16[8,128,128]{2,1,0:T(8,128)(2,1)S(1)}) custom-call(s32[2,8]{1,0:T(2,128)S(1)} %select_reduce_fusion.1.refs_0_, bf16[1552,128]{1,0:T(8,128)(2,1)S(1)} %pad_maximum_fusion.x_ref.refs_1_, bf16[1552,128]{1,0:T(8,128)(2,1)S(1)} %collective-permute-done.3.refs_2_, ...), custom_call_target="tpu_custom_call" | custom-call | flops 805306368 | bytes 3145728 | tf_op jit(solution)/shard_map/pallas_call | solution.py:76
  75.1 1.9 %collective-permute-start.12 = (bf16[8,128,128]{2,1,0:T(8,128)(2,1)S(1)}, bf16[8,128,128]{2,1,0:T(8,128)(2,1)S(1)}, u32[]{:S(2)}, u32[]{:S(2)}) collective-permute-start(bf16[8,128,128]{2,1,0:T(8,128)(2,1)S(1)} %get-tuple-element.12), channel_id=1, source_target_pairs={{0,16},{16,0},{32,48},{48,32},{64,80},{80,64},{96,112},{112,96},{1... | collective-permute-start | bytes 786440 | tf_op jit(solution)/shard_map/ppermute | solution.py:36
  77.1 4.9 %collective-permute-start.14 = (bf16[1,128,128]{2,1,0:T(8,128)(2,1)S(1)}, bf16[1,128,128]{2,1,0:T(8,128)(2,1)S(1)}, u32[]{:S(2)}, u32[]{:S(2)}) collective-permute-start(bf16[1,128,128]{2,1,0:T(8,128)(2,1)S(1)} %shard_map.86.refs_13_), channel_id=1, source_target_pairs={{0,32},{16,48},{32,0},{48,16},{64,96},{80,112},{96,64},{112,80},{1... | collective-permute-start | bytes 98312 | tf_op jit(solution)/shard_map/ppermute | solution.py:36
  82.0 6.4 %collective-permute-done.14.refs_3_ = bf16[1,128,128]{2,1,0:T(8,128)(2,1)S(1)} collective-permute-done((bf16[1,128,128]{2,1,0:T(8,128)(2,1)S(1)}, bf16[1,128,128]{2,1,0:T(8,128)(2,1)S(1)}, u32[]{:S(2)}, u32[]{:S(2)}) %collective-permute-start.14) | collective-permute-done | bytes 32800 | tf_op jit(solution)/shard_map/ppermute | solution.py:36
  89.1 55.6 %all_to_all.5 = bf16[16,4,128,128]{3,2,1,0:T(8,128)(2,1)S(1)} all-to-all(bf16[16,4,128,128]{3,2,1,0:T(8,128)(2,1)S(1)} %bitcast.50), channel_id=1, replica_groups=mesh['kring'=32,'kblk'=16] {'kblk'}, dimensions={0} | all-to-all | bytes 4194304 | tf_op jit(solution)/shard_map/all_to_all | solution.py:223
  144.7 1.3 copy.14
  (54 shorter events, 9.3 us)
Async XLA Ops:
  0.0 12.9 %copy-start = (f32[512]{0:T(512)S(1)}, f32[512]{0:T(512)}, u32[]{:S(2)}) copy-start(f32[512]{0:T(512)} %param.13) | copy-start | bytes 6148
  0.0 17.0 %copy-start.3 = (s32[1,1,32]{2,1,0:T(1,128)S(1)}, s32[1,1,32]{2,1,0:T(1,128)}, u32[]{:S(2)}) copy-start(s32[1,1,32]{2,1,0:T(1,128)} %param.14) | copy-start | bytes 388
  1.1 12.0 %collective-permute-start = (bf16[128,1536]{1,0:T(8,128)(2,1)S(1)}, bf16[128,1536]{1,0:T(8,128)(2,1)S(1)}, u32[]{:S(2)}, u32[]{:S(2)}) collective-permute-start(bf16[128,1536]{1,0:T(8,128)(2,1)S(1)} %pad_maximum_fusion.1.a_ref), channel_id=1, source_target_pairs={{0,16},{16,0},{32,48},{48,32},{64,80},{80,64},{96,112},{112,96},{1... | collective-permute-start | bytes 1179656 | tf_op jit(solution)/shard_map/ppermute | solution.py:36
  13.2 13.5 %collective-permute-start.4 = (bf16[2,64,1536]{2,1,0:T(8,128)(2,1)S(1)}, bf16[2,64,1536]{2,1,0:T(8,128)(2,1)S(1)}, u32[]{:S(2)}, u32[]{:S(2)}) collective-permute-start(bf16[2,64,1536]{2,1,0:T(8,128)(2,1)S(1)} %get-tuple-element.10.refs_2_.refs_3_), channel_id=1, source_target_pairs={{0,64},{16,464},{32,96},{48,496},{64,128},{80,16},{96,160},{112,48... | collective-permute-start | bytes 1179656 | tf_op jit(solution)/shard_map/ppermute | solution.py:36
  15.1 14.6 %collective-permute-start.1 = (bf16[2,64,1536]{2,1,0:T(8,128)(2,1)S(1)}, bf16[2,64,1536]{2,1,0:T(8,128)(2,1)S(1)}, u32[]{:S(2)}, u32[]{:S(2)}) collective-permute-start(bf16[2,64,1536]{2,1,0:T(8,128)(2,1)S(1)} %get-tuple-element.9.refs_3_.refs_4_), channel_id=1, source_target_pairs={{0,64},{16,464},{32,96},{48,496},{64,128},{80,16},{96,160},{112,48... | collective-permute-start | bytes 1179656 | tf_op jit(solution)/shard_map/ppermute | solution.py:36
  17.1 31.4 %collective-permute-start.10 = (bf16[1552,128]{1,0:T(8,128)(2,1)S(1)}, bf16[1552,128]{1,0:T(8,128)(2,1)}, u32[]{:S(2)}, u32[]{:S(2)}) collective-permute-start(bf16[1552,128]{1,0:T(8,128)(2,1)S(1)} %pad_maximum_fusion.x_ref.refs_1_), channel_id=1, source_target_pairs={{0,32},{16,48},{32,0},{48,16},{64,96},{80,112},{96,64},{112,80},{1... | collective-permute-start | bytes 1191944 | tf_op jit(solution)/shard_map/ppermute | solution.py:36
  26.7 8.8 %collective-permute-start.5 = (bf16[2,64,1536]{2,1,0:T(8,128)(2,1)S(1)}, bf16[2,64,1536]{2,1,0:T(8,128)(2,1)S(1)}, u32[]{:S(2)}, u32[]{:S(2)}) collective-permute-start(bf16[2,64,1536]{2,1,0:T(8,128)(2,1)S(1)} %collective-permute-done.4.refs_4_.refs_5_), channel_id=1, source_target_pairs={{0,64},{16,464},{32,96},{48,496},{64,128},{80,16},{96,160},{112,48... | collective-permute-start | bytes 1179656 | tf_op jit(solution)/shard_map/ppermute | solution.py:36
  29.7 10.0 %collective-permute-start.2 = (bf16[2,64,1536]{2,1,0:T(8,128)(2,1)S(1)}, bf16[2,64,1536]{2,1,0:T(8,128)(2,1)S(1)}, u32[]{:S(2)}, u32[]{:S(2)}) collective-permute-start(bf16[2,64,1536]{2,1,0:T(8,128)(2,1)S(1)} %collective-permute-done.1.refs_5_.refs_6_), channel_id=1, source_target_pairs={{0,64},{16,464},{32,96},{48,496},{64,128},{80,16},{96,160},{112,48... | collective-permute-start | bytes 1179656 | tf_op jit(solution)/shard_map/ppermute | solution.py:36
  35.5 13.0 %collective-permute-start.6 = (bf16[2,64,1536]{2,1,0:T(8,128)(2,1)S(1)}, bf16[2,64,1536]{2,1,0:T(8,128)(2,1)S(1)}, u32[]{:S(2)}, u32[]{:S(2)}) collective-permute-start(bf16[2,64,1536]{2,1,0:T(8,128)(2,1)S(1)} %collective-permute-done.5.refs_6_.refs_7_), channel_id=1, source_target_pairs={{0,64},{16,464},{32,96},{48,496},{64,128},{80,16},{96,160},{112,48... | collective-permute-start | bytes 1179656 | tf_op jit(solution)/shard_map/ppermute | solution.py:36
  39.7 15.8 %collective-permute-start.7 = (bf16[2,64,1536]{2,1,0:T(8,128)(2,1)S(1)}, bf16[2,64,1536]{2,1,0:T(8,128)(2,1)S(1)}, u32[]{:S(2)}, u32[]{:S(2)}) collective-permute-start(bf16[2,64,1536]{2,1,0:T(8,128)(2,1)S(1)} %collective-permute-done.2.refs_0_.refs_7_.refs_8_), channel_id=1, source_target_pairs={{0,64},{16,464},{32,96},{48,496},{64,128},{80,16},{96,160},{112,48... | collective-permute-start | bytes 1179656 | tf_op jit(solution)/shard_map/ppermute | solution.py:36
  44.8 12.7 %copy-start.1 = (bf16[1,1,32]{2,1,0:T(2,128)(2,1)S(1)}, bf16[1,1,32]{2,1,0:T(2,128)(2,1)}, u32[]{:S(2)}) copy-start(bf16[1,1,32]{2,1,0:T(2,128)(2,1)} %get-tuple-element.15) | copy-start | bytes 196
  44.9 12.7 %copy-start.2 = (bf16[1,1,32]{2,1,0:T(2,128)(2,1)S(1)}, bf16[1,1,32]{2,1,0:T(2,128)(2,1)}, u32[]{:S(2)}) copy-start(bf16[1,1,32]{2,1,0:T(2,128)(2,1)} %get-tuple-element.16) | copy-start | bytes 196
  46.5 11.0 %collective-permute-start.3 = (bf16[1552,128]{1,0:T(8,128)(2,1)S(1)}, bf16[1552,128]{1,0:T(8,128)(2,1)S(1)}, u32[]{:S(2)}, u32[]{:S(2)}) collective-permute-start(bf16[1552,128]{1,0:T(8,128)(2,1)S(1)} %shard_map.83), channel_id=1, source_target_pairs={{0,16},{16,0},{32,48},{48,32},{64,80},{80,64},{96,112},{112,96},{1... | collective-permute-start | bytes 1191944 | tf_op jit(solution)/shard_map/ppermute | solution.py:36
  49.6 8.2 %collective-permute-start.11 = (bf16[1552,128]{1,0:T(8,128)(2,1)S(1)}, bf16[1552,128]{1,0:T(8,128)(2,1)S(1)}, u32[]{:S(2)}, u32[]{:S(2)}) collective-permute-start(bf16[1552,128]{1,0:T(8,128)(2,1)S(1)} %shard_map.84.refs_1_), channel_id=1, source_target_pairs={{0,16},{16,0},{32,48},{48,32},{64,80},{80,64},{96,112},{112,96},{1... | collective-permute-start | bytes 1191944 | tf_op jit(solution)/shard_map/ppermute | solution.py:36
  51.9 11.2 %collective-permute-start.8 = (bf16[1,64,1536]{2,1,0:T(8,128)(2,1)S(1)}, bf16[1,64,1536]{2,1,0:T(8,128)(2,1)S(1)}, u32[]{:S(2)}, u32[]{:S(2)}) collective-permute-start(bf16[1,64,1536]{2,1,0:T(8,128)(2,1)S(1)} %slice.48), channel_id=1, source_target_pairs={{0,64},{16,464},{32,96},{48,496},{64,128},{80,16},{96,160},{112,48... | collective-permute-start | bytes 589832 | tf_op jit(solution)/shard_map/ppermute | solution.py:36
  55.6 7.6 %collective-permute-start.9 = (bf16[1,64,1536]{2,1,0:T(8,128)(2,1)S(1)}, bf16[1,64,1536]{2,1,0:T(8,128)(2,1)S(1)}, u32[]{:S(2)}, u32[]{:S(2)}) collective-permute-start(bf16[1,64,1536]{2,1,0:T(8,128)(2,1)S(1)} %slice.49), channel_id=1, source_target_pairs={{0,64},{16,464},{32,96},{48,496},{64,128},{80,16},{96,160},{112,48... | collective-permute-start | bytes 589832 | tf_op jit(solution)/shard_map/ppermute | solution.py:36
  59.4 28.9 %collective-permute-start.13 = (bf16[7,128,128]{2,1,0:T(8,128)(2,1)S(1)}, bf16[7,128,128]{2,1,0:T(8,128)(2,1)S(1)}, u32[]{:S(2)}, u32[]{:S(2)}) collective-permute-start(bf16[7,128,128]{2,1,0:T(8,128)(2,1)S(1)} %shard_map.88), channel_id=1, source_target_pairs={{0,32},{16,48},{32,0},{48,16},{64,96},{80,112},{96,64},{112,80},{1... | collective-permute-start | bytes 688136 | tf_op jit(solution)/shard_map/ppermute | solution.py:36
  64.7 23.6 %collective-permute-start.15 = (bf16[8,128,128]{2,1,0:T(8,128)(2,1)S(1)}, bf16[8,128,128]{2,1,0:T(8,128)(2,1)S(1)}, u32[]{:S(2)}, u32[]{:S(2)}) collective-permute-start(bf16[8,128,128]{2,1,0:T(8,128)(2,1)S(1)} %shard_map.85.refs_4_), channel_id=1, source_target_pairs={{0,48},{16,32},{32,16},{48,0},{64,112},{80,96},{96,80},{112,64},{1... | collective-permute-start | bytes 786440 | tf_op jit(solution)/shard_map/ppermute | solution.py:36
  75.1 13.3 %collective-permute-start.12 = (bf16[8,128,128]{2,1,0:T(8,128)(2,1)S(1)}, bf16[8,128,128]{2,1,0:T(8,128)(2,1)S(1)}, u32[]{:S(2)}, u32[]{:S(2)}) collective-permute-start(bf16[8,128,128]{2,1,0:T(8,128)(2,1)S(1)} %get-tuple-element.12), channel_id=1, source_target_pairs={{0,16},{16,0},{32,48},{48,32},{64,80},{80,64},{96,112},{112,96},{1... | collective-permute-start | bytes 786440 | tf_op jit(solution)/shard_map/ppermute | solution.py:36
  77.1 11.3 %collective-permute-start.14 = (bf16[1,128,128]{2,1,0:T(8,128)(2,1)S(1)}, bf16[1,128,128]{2,1,0:T(8,128)(2,1)S(1)}, u32[]{:S(2)}, u32[]{:S(2)}) collective-permute-start(bf16[1,128,128]{2,1,0:T(8,128)(2,1)S(1)} %shard_map.86.refs_13_), channel_id=1, source_target_pairs={{0,32},{16,48},{32,0},{48,16},{64,96},{80,112},{96,64},{112,80},{1... | collective-permute-start | bytes 98312 | tf_op jit(solution)/shard_map/ppermute | solution.py:36

commit v7 on v6

--- a/solution.py
+++ b/solution.py
@@ -84,7 +84,7 @@
         ],
         compiler_params=pltpu.CompilerParams(vmem_limit_bytes=24 << 20),
         cost_estimate=pl.CostEstimate(
-            flops=2 * len(elems) * count * TILE * depth * TILE, bytes_accessed=2 * count * TILE * depth, transcendentals=0
+            flops=16 * len(elems) * count * TILE * depth * TILE, bytes_accessed=2 * count * TILE * depth, transcendentals=0
         ),
     )(cuts, *elems, *flat, *after)
 

time: 148 us -> 148 us (level)
  blocking collectives: 55.6 us -> 53.5 us
    all_to_all x1, blocking collectives: 55.6 us -> 53.5 us  [body(): lax.all_to_all(outbox, 'kblk', split_axis=0, concat_axis=0, tiled=True)]
    unnamed x11 -> x13, local copies, waits for them, and re-layouts: 3.48 us -> 3.48 us
where the time goes in v7:
time: 148 us; the launch traced here: 146 us
  starting transfers between devices  63.3 us (43%)
  blocking collectives  53.5 us (36%)
  waiting for transfers between devices  10.2 us (7%)
  Pallas kernels  8.64 us (6%)
  other arithmetic  6.04 us (4%)
  local copies, waits for them, and re-layouts  3.51 us (2%)
    ppermute x16, starting transfers between devices, send(): return lax.ppermute(x, 'kring', perm)  63.3 us
    all_to_all x1, blocking collectives, body(): lax.all_to_all(outbox, 'kblk', split_axis=0, concat_axis=0, tiled=True)  53.5 us
    ppermute x16, waiting for transfers between devices, send(): return lax.ppermute(x, 'kring', perm)  10.2 us
    pallas_call x4, Pallas kernels, make_tiles(): pl.pallas_call(kernel, out_shape=(shape,) * len(elems), in_specs=[pl.Bloc...  7.78 us
    unnamed x13, local copies, waits for them, and re-layouts  3.48 us
  transfers between devices with their start and end apart: 16, of which 3 were waited for; matrix products, arithmetic and copies ran while one was open for 5% of the time, Pallas kernels for 5%

profile of v7, /device:TPU:1, one launch (start us, length us, event | category | flops | bytes accessed | tf_op | source)
XLA Modules:
  0.0 145.6 jit_solution(1939468598685255084)
XLA Ops:
  1.1 8.8 %collective-permute-start = (bf16[128,1536]{1,0:T(8,128)(2,1)S(1)}, bf16[128,1536]{1,0:T(8,128)(2,1)S(1)}, u32[]{:S(2)}, u32[]{:S(2)}) collective-permute-start(bf16[128,1536]{1,0:T(8,128)(2,1)S(1)} %pad_maximum_fusion.1.a_ref), channel_id=1, source_target_pairs={{0,16},{16,0},{32,48},{48,32},{64,80},{80,64},{96,112},{112,96},{1... | collective-permute-start | bytes 1179656 | tf_op jit(solution)/shard_map/ppermute | solution.py:36
  13.2 1.9 %collective-permute-start.4 = (bf16[2,64,1536]{2,1,0:T(8,128)(2,1)S(1)}, bf16[2,64,1536]{2,1,0:T(8,128)(2,1)S(1)}, u32[]{:S(2)}, u32[]{:S(2)}) collective-permute-start(bf16[2,64,1536]{2,1,0:T(8,128)(2,1)S(1)} %get-tuple-element.10.refs_2_.refs_3_), channel_id=1, source_target_pairs={{0,64},{16,464},{32,96},{48,496},{64,128},{80,16},{96,160},{112,48... | collective-permute-start | bytes 1179656 | tf_op jit(solution)/shard_map/ppermute | solution.py:36
  15.1 1.9 %collective-permute-start.1 = (bf16[2,64,1536]{2,1,0:T(8,128)(2,1)S(1)}, bf16[2,64,1536]{2,1,0:T(8,128)(2,1)S(1)}, u32[]{:S(2)}, u32[]{:S(2)}) collective-permute-start(bf16[2,64,1536]{2,1,0:T(8,128)(2,1)S(1)} %get-tuple-element.9.refs_3_.refs_4_), channel_id=1, source_target_pairs={{0,64},{16,464},{32,96},{48,496},{64,128},{80,16},{96,160},{112,48... | collective-permute-start | bytes 1179656 | tf_op jit(solution)/shard_map/ppermute | solution.py:36
  17.1 9.5 %collective-permute-start.10 = (bf16[1552,128]{1,0:T(8,128)(2,1)S(1)}, bf16[1552,128]{1,0:T(8,128)(2,1)S(1)}, u32[]{:S(2)}, u32[]{:S(2)}) collective-permute-start(bf16[1552,128]{1,0:T(8,128)(2,1)S(1)} %pad_maximum_fusion.x_ref.refs_1_), channel_id=1, source_target_pairs={{0,32},{16,48},{32,0},{48,16},{64,96},{80,112},{96,64},{112,80},{1... | collective-permute-start | bytes 1191944 | tf_op jit(solution)/shard_map/ppermute | solution.py:36
  26.7 3.0 %collective-permute-start.5 = (bf16[2,64,1536]{2,1,0:T(8,128)(2,1)S(1)}, bf16[2,64,1536]{2,1,0:T(8,128)(2,1)}, u32[]{:S(2)}, u32[]{:S(2)}) collective-permute-start(bf16[2,64,1536]{2,1,0:T(8,128)(2,1)S(1)} %collective-permute-done.4.refs_4_.refs_5_), channel_id=1, source_target_pairs={{0,64},{16,464},{32,96},{48,496},{64,128},{80,16},{96,160},{112,48... | collective-permute-start | bytes 1179656 | tf_op jit(solution)/shard_map/ppermute | solution.py:36
  29.7 3.0 %collective-permute-start.2 = (bf16[2,64,1536]{2,1,0:T(8,128)(2,1)S(1)}, bf16[2,64,1536]{2,1,0:T(8,128)(2,1)S(1)}, u32[]{:S(2)}, u32[]{:S(2)}) collective-permute-start(bf16[2,64,1536]{2,1,0:T(8,128)(2,1)S(1)} %collective-permute-done.1.refs_5_.refs_6_), channel_id=1, source_target_pairs={{0,64},{16,464},{32,96},{48,496},{64,128},{80,16},{96,160},{112,48... | collective-permute-start | bytes 1179656 | tf_op jit(solution)/shard_map/ppermute | solution.py:36
  33.3 2.3 %collective-permute-done.5.refs_6_.refs_7_ = bf16[2,64,1536]{2,1,0:T(8,128)(2,1)} collective-permute-done((bf16[2,64,1536]{2,1,0:T(8,128)(2,1)S(1)}, bf16[2,64,1536]{2,1,0:T(8,128)(2,1)}, u32[]{:S(2)}, u32[]{:S(2)}) %collective-permute-start.5) | collective-permute-done | bytes 393248 | tf_op jit(solution)/shard_map/ppermute | solution.py:36
  35.6 3.9 %collective-permute-start.6 = (bf16[2,64,1536]{2,1,0:T(8,128)(2,1)}, bf16[2,64,1536]{2,1,0:T(8,128)(2,1)S(1)}, u32[]{:S(2)}, u32[]{:S(2)}) collective-permute-start(bf16[2,64,1536]{2,1,0:T(8,128)(2,1)} %collective-permute-done.5.refs_6_.refs_7_), channel_id=1, source_target_pairs={{0,64},{16,464},{32,96},{48,496},{64,128},{80,16},{96,160},{112,48... | collective-permute-start | bytes 1179656 | tf_op jit(solution)/shard_map/ppermute | solution.py:36
  39.7 3.9 %collective-permute-start.7 = (bf16[2,64,1536]{2,1,0:T(8,128)(2,1)S(1)}, bf16[2,64,1536]{2,1,0:T(8,128)(2,1)S(1)}, u32[]{:S(2)}, u32[]{:S(2)}) collective-permute-start(bf16[2,64,1536]{2,1,0:T(8,128)(2,1)S(1)} %collective-permute-done.2.refs_0_.refs_7_.refs_8_), channel_id=1, source_target_pairs={{0,64},{16,464},{32,96},{48,496},{64,128},{80,16},{96,160},{112,48... | collective-permute-start | bytes 1179656 | tf_op jit(solution)/shard_map/ppermute | solution.py:36
  43.6 1.2 fusion.22
  46.5 2.1 %collective-permute-start.3 = (bf16[1552,128]{1,0:T(8,128)(2,1)S(1)}, bf16[1552,128]{1,0:T(8,128)(2,1)S(1)}, u32[]{:S(2)}, u32[]{:S(2)}) collective-permute-start(bf16[1552,128]{1,0:T(8,128)(2,1)S(1)} %shard_map.83), channel_id=1, source_target_pairs={{0,16},{16,0},{32,48},{48,32},{64,80},{80,64},{96,112},{112,96},{1... | collective-permute-start | bytes 1191944 | tf_op jit(solution)/shard_map/ppermute | solution.py:36
  48.7 2.2 %collective-permute-start.11 = (bf16[1552,128]{1,0:T(8,128)(2,1)S(1)}, bf16[1552,128]{1,0:T(8,128)(2,1)S(1)}, u32[]{:S(2)}, u32[]{:S(2)}) collective-permute-start(bf16[1552,128]{1,0:T(8,128)(2,1)S(1)} %shard_map.84.refs_1_), channel_id=1, source_target_pairs={{0,16},{16,0},{32,48},{48,32},{64,80},{80,64},{96,112},{112,96},{1... | collective-permute-start | bytes 1191944 | tf_op jit(solution)/shard_map/ppermute | solution.py:36
  50.9 3.6 %collective-permute-start.8 = (bf16[1,64,1536]{2,1,0:T(8,128)(2,1)S(1)}, bf16[1,64,1536]{2,1,0:T(8,128)(2,1)S(1)}, u32[]{:S(2)}, u32[]{:S(2)}) collective-permute-start(bf16[1,64,1536]{2,1,0:T(8,128)(2,1)S(1)} %slice.48), channel_id=1, source_target_pairs={{0,64},{16,464},{32,96},{48,496},{64,128},{80,16},{96,160},{112,48... | collective-permute-start | bytes 589832 | tf_op jit(solution)/shard_map/ppermute | solution.py:36
  54.6 1.9 %collective-permute-start.9 = (bf16[1,64,1536]{2,1,0:T(8,128)(2,1)S(1)}, bf16[1,64,1536]{2,1,0:T(8,128)(2,1)S(1)}, u32[]{:S(2)}, u32[]{:S(2)}) collective-permute-start(bf16[1,64,1536]{2,1,0:T(8,128)(2,1)S(1)} %slice.49), channel_id=1, source_target_pairs={{0,64},{16,464},{32,96},{48,496},{64,128},{80,16},{96,160},{112,48... | collective-permute-start | bytes 589832 | tf_op jit(solution)/shard_map/ppermute | solution.py:36
  56.9 2.0 %shard_map.88 = bf16[7,128,128]{2,1,0:T(8,128)(2,1)S(1)} custom-call(s32[1,8]{1,0:T(1,128)S(1)} %bitcast.51, bf16[1552,128]{1,0:T(8,128)(2,1)S(1)} %shard_map.84.refs_1_, bf16[2,64,1536]{2,1,0:T(8,128)(2,1)S(1)} %get-tuple-element.10.refs_2_.refs_3_, bf16[2,64,1536]{2,1,0:T(8,128)(2,1)S(1)} %get-tuple-element.9.refs_3_.refs_4_, ...), custom_call_target="tpu_custom_call" | custom-call | flops 2818572288 | bytes 2752512 | tf_op jit(solution)/shard_map/pallas_call | solution.py:76
  58.9 3.7 %collective-permute-start.13 = (bf16[7,128,128]{2,1,0:T(8,128)(2,1)S(1)}, bf16[7,128,128]{2,1,0:T(8,128)(2,1)S(1)}, u32[]{:S(2)}, u32[]{:S(2)}) collective-permute-start(bf16[7,128,128]{2,1,0:T(8,128)(2,1)S(1)} %shard_map.88), channel_id=1, source_target_pairs={{0,32},{16,48},{32,0},{48,16},{64,96},{80,112},{96,64},{112,80},{1... | collective-permute-start | bytes 688136 | tf_op jit(solution)/shard_map/ppermute | solution.py:36
  62.6 2.1 %shard_map.85.refs_4_ = bf16[8,128,128]{2,1,0:T(8,128)(2,1)S(1)} custom-call(s32[1,8]{1,0:T(1,128)S(1)} %bitcast.53, bf16[1552,128]{1,0:T(8,128)(2,1)S(1)} %collective-permute-done.11.refs_1_, bf16[2,64,1536]{2,1,0:T(8,128)(2,1)S(1)} %get-tuple-element.10.refs_2_.refs_3_, bf16[2,64,1536]{2,1,0:T(8,128)(2,1)S(1)} %get-tuple-element.9.refs_3_.refs_4_, ...), custom_call_target="tpu_custom_call" | custom-call | flops 3221225472 | bytes 3145728 | tf_op jit(solution)/shard_map/pallas_call | solution.py:76
  64.7 7.0 %collective-permute-start.15 = (bf16[8,128,128]{2,1,0:T(8,128)(2,1)S(1)}, bf16[8,128,128]{2,1,0:T(8,128)(2,1)S(1)}, u32[]{:S(2)}, u32[]{:S(2)}) collective-permute-start(bf16[8,128,128]{2,1,0:T(8,128)(2,1)S(1)} %shard_map.85.refs_4_), channel_id=1, source_target_pairs={{0,48},{16,32},{32,16},{48,0},{64,112},{80,96},{96,80},{112,64},{1... | collective-permute-start | bytes 786440 | tf_op jit(solution)/shard_map/ppermute | solution.py:36
  72.6 2.9 %shard_map.87 = (bf16[8,128,128]{2,1,0:T(8,128)(2,1)S(1)}, bf16[8,128,128]{2,1,0:T(8,128)(2,1)S(1)}) custom-call(s32[2,8]{1,0:T(2,128)S(1)} %select_reduce_fusion.1.refs_0_, bf16[1552,128]{1,0:T(8,128)(2,1)S(1)} %pad_maximum_fusion.x_ref.refs_1_, bf16[1552,128]{1,0:T(8,128)(2,1)S(1)} %collective-permute-done.3.refs_2_, ...), custom_call_target="tpu_custom_call" | custom-call | flops 6442450944 | bytes 3145728 | tf_op jit(solution)/shard_map/pallas_call | solution.py:76
  75.5 1.9 %collective-permute-start.12 = (bf16[8,128,128]{2,1,0:T(8,128)(2,1)S(1)}, bf16[8,128,128]{2,1,0:T(8,128)(2,1)S(1)}, u32[]{:S(2)}, u32[]{:S(2)}) collective-permute-start(bf16[8,128,128]{2,1,0:T(8,128)(2,1)S(1)} %get-tuple-element.12), channel_id=1, source_target_pairs={{0,16},{16,0},{32,48},{48,32},{64,80},{80,64},{96,112},{112,96},{1... | collective-permute-start | bytes 786440 | tf_op jit(solution)/shard_map/ppermute | solution.py:36
  77.5 5.0 %collective-permute-start.14 = (bf16[1,128,128]{2,1,0:T(8,128)(2,1)S(1)}, bf16[1,128,128]{2,1,0:T(8,128)(2,1)S(1)}, u32[]{:S(2)}, u32[]{:S(2)}) collective-permute-start(bf16[1,128,128]{2,1,0:T(8,128)(2,1)S(1)} %shard_map.86.refs_13_), channel_id=1, source_target_pairs={{0,32},{16,48},{32,0},{48,16},{64,96},{80,112},{96,64},{112,80},{1... | collective-permute-start | bytes 98312 | tf_op jit(solution)/shard_map/ppermute | solution.py:36
  82.5 7.6 %collective-permute-done.14.refs_3_ = bf16[1,128,128]{2,1,0:T(8,128)(2,1)S(1)} collective-permute-done((bf16[1,128,128]{2,1,0:T(8,128)(2,1)S(1)}, bf16[1,128,128]{2,1,0:T(8,128)(2,1)S(1)}, u32[]{:S(2)}, u32[]{:S(2)}) %collective-permute-start.14) | collective-permute-done | bytes 32800 | tf_op jit(solution)/shard_map/ppermute | solution.py:36
  90.9 53.5 %all_to_all.5 = bf16[16,4,128,128]{3,2,1,0:T(8,128)(2,1)S(1)} all-to-all(bf16[16,4,128,128]{3,2,1,0:T(8,128)(2,1)S(1)} %bitcast.50), channel_id=1, replica_groups=mesh['kring'=32,'kblk'=16] {'kblk'}, dimensions={0} | all-to-all | bytes 4194304 | tf_op jit(solution)/shard_map/all_to_all | solution.py:223
  144.3 1.3 copy.14
  (56 shorter events, 9.0 us)
Async XLA Ops:
  0.0 12.9 %copy-start.1 = (f32[512]{0:T(512)S(1)}, f32[512]{0:T(512)}, u32[]{:S(2)}) copy-start(f32[512]{0:T(512)} %param.13) | copy-start | bytes 6148
  0.0 17.0 %copy-start.4 = (s32[1,1,32]{2,1,0:T(1,128)S(1)}, s32[1,1,32]{2,1,0:T(1,128)}, u32[]{:S(2)}) copy-start(s32[1,1,32]{2,1,0:T(1,128)} %param.14) | copy-start | bytes 388
  1.1 12.0 %collective-permute-start = (bf16[128,1536]{1,0:T(8,128)(2,1)S(1)}, bf16[128,1536]{1,0:T(8,128)(2,1)S(1)}, u32[]{:S(2)}, u32[]{:S(2)}) collective-permute-start(bf16[128,1536]{1,0:T(8,128)(2,1)S(1)} %pad_maximum_fusion.1.a_ref), channel_id=1, source_target_pairs={{0,16},{16,0},{32,48},{48,32},{64,80},{80,64},{96,112},{112,96},{1... | collective-permute-start | bytes 1179656 | tf_op jit(solution)/shard_map/ppermute | solution.py:36
  13.2 13.5 %collective-permute-start.4 = (bf16[2,64,1536]{2,1,0:T(8,128)(2,1)S(1)}, bf16[2,64,1536]{2,1,0:T(8,128)(2,1)S(1)}, u32[]{:S(2)}, u32[]{:S(2)}) collective-permute-start(bf16[2,64,1536]{2,1,0:T(8,128)(2,1)S(1)} %get-tuple-element.10.refs_2_.refs_3_), channel_id=1, source_target_pairs={{0,64},{16,464},{32,96},{48,496},{64,128},{80,16},{96,160},{112,48... | collective-permute-start | bytes 1179656 | tf_op jit(solution)/shard_map/ppermute | solution.py:36
  15.1 14.6 %collective-permute-start.1 = (bf16[2,64,1536]{2,1,0:T(8,128)(2,1)S(1)}, bf16[2,64,1536]{2,1,0:T(8,128)(2,1)S(1)}, u32[]{:S(2)}, u32[]{:S(2)}) collective-permute-start(bf16[2,64,1536]{2,1,0:T(8,128)(2,1)S(1)} %get-tuple-element.9.refs_3_.refs_4_), channel_id=1, source_target_pairs={{0,64},{16,464},{32,96},{48,496},{64,128},{80,16},{96,160},{112,48... | collective-permute-start | bytes 1179656 | tf_op jit(solution)/shard_map/ppermute | solution.py:36
  17.1 31.5 %collective-permute-start.10 = (bf16[1552,128]{1,0:T(8,128)(2,1)S(1)}, bf16[1552,128]{1,0:T(8,128)(2,1)S(1)}, u32[]{:S(2)}, u32[]{:S(2)}) collective-permute-start(bf16[1552,128]{1,0:T(8,128)(2,1)S(1)} %pad_maximum_fusion.x_ref.refs_1_), channel_id=1, source_target_pairs={{0,32},{16,48},{32,0},{48,16},{64,96},{80,112},{96,64},{112,80},{1... | collective-permute-start | bytes 1191944 | tf_op jit(solution)/shard_map/ppermute | solution.py:36
  26.7 8.9 %collective-permute-start.5 = (bf16[2,64,1536]{2,1,0:T(8,128)(2,1)S(1)}, bf16[2,64,1536]{2,1,0:T(8,128)(2,1)}, u32[]{:S(2)}, u32[]{:S(2)}) collective-permute-start(bf16[2,64,1536]{2,1,0:T(8,128)(2,1)S(1)} %collective-permute-done.4.refs_4_.refs_5_), channel_id=1, source_target_pairs={{0,64},{16,464},{32,96},{48,496},{64,128},{80,16},{96,160},{112,48... | collective-permute-start | bytes 1179656 | tf_op jit(solution)/shard_map/ppermute | solution.py:36
  29.7 10.0 %collective-permute-start.2 = (bf16[2,64,1536]{2,1,0:T(8,128)(2,1)S(1)}, bf16[2,64,1536]{2,1,0:T(8,128)(2,1)S(1)}, u32[]{:S(2)}, u32[]{:S(2)}) collective-permute-start(bf16[2,64,1536]{2,1,0:T(8,128)(2,1)S(1)} %collective-permute-done.1.refs_5_.refs_6_), channel_id=1, source_target_pairs={{0,64},{16,464},{32,96},{48,496},{64,128},{80,16},{96,160},{112,48... | collective-permute-start | bytes 1179656 | tf_op jit(solution)/shard_map/ppermute | solution.py:36
  35.6 13.0 %collective-permute-start.6 = (bf16[2,64,1536]{2,1,0:T(8,128)(2,1)}, bf16[2,64,1536]{2,1,0:T(8,128)(2,1)S(1)}, u32[]{:S(2)}, u32[]{:S(2)}) collective-permute-start(bf16[2,64,1536]{2,1,0:T(8,128)(2,1)} %collective-permute-done.5.refs_6_.refs_7_), channel_id=1, source_target_pairs={{0,64},{16,464},{32,96},{48,496},{64,128},{80,16},{96,160},{112,48... | collective-permute-start | bytes 1179656 | tf_op jit(solution)/shard_map/ppermute | solution.py:36
  39.7 14.8 %collective-permute-start.7 = (bf16[2,64,1536]{2,1,0:T(8,128)(2,1)S(1)}, bf16[2,64,1536]{2,1,0:T(8,128)(2,1)S(1)}, u32[]{:S(2)}, u32[]{:S(2)}) collective-permute-start(bf16[2,64,1536]{2,1,0:T(8,128)(2,1)S(1)} %collective-permute-done.2.refs_0_.refs_7_.refs_8_), channel_id=1, source_target_pairs={{0,64},{16,464},{32,96},{48,496},{64,128},{80,16},{96,160},{112,48... | collective-permute-start | bytes 1179656 | tf_op jit(solution)/shard_map/ppermute | solution.py:36
  44.9 11.7 %copy-start.2 = (bf16[1,1,32]{2,1,0:T(2,128)(2,1)S(1)}, bf16[1,1,32]{2,1,0:T(2,128)(2,1)}, u32[]{:S(2)}) copy-start(bf16[1,1,32]{2,1,0:T(2,128)(2,1)} %get-tuple-element.15) | copy-start | bytes 196
  44.9 11.7 %copy-start.3 = (bf16[1,1,32]{2,1,0:T(2,128)(2,1)S(1)}, bf16[1,1,32]{2,1,0:T(2,128)(2,1)}, u32[]{:S(2)}) copy-start(bf16[1,1,32]{2,1,0:T(2,128)(2,1)} %get-tuple-element.16) | copy-start | bytes 196
  44.9 11.8 %copy-start = (pred[8,32]{1,0:T(8,128)(4,1)S(1)}, pred[8,32]{1,0:T(8,128)(4,1)}, u32[]{:S(2)}) copy-start(pred[8,32]{1,0:T(8,128)(4,1)} %fusion.11) | copy-start | bytes 772
  46.5 10.1 %collective-permute-start.3 = (bf16[1552,128]{1,0:T(8,128)(2,1)S(1)}, bf16[1552,128]{1,0:T(8,128)(2,1)S(1)}, u32[]{:S(2)}, u32[]{:S(2)}) collective-permute-start(bf16[1552,128]{1,0:T(8,128)(2,1)S(1)} %shard_map.83), channel_id=1, source_target_pairs={{0,16},{16,0},{32,48},{48,32},{64,80},{80,64},{96,112},{112,96},{1... | collective-permute-start | bytes 1191944 | tf_op jit(solution)/shard_map/ppermute | solution.py:36
  48.7 8.1 %collective-permute-start.11 = (bf16[1552,128]{1,0:T(8,128)(2,1)S(1)}, bf16[1552,128]{1,0:T(8,128)(2,1)S(1)}, u32[]{:S(2)}, u32[]{:S(2)}) collective-permute-start(bf16[1552,128]{1,0:T(8,128)(2,1)S(1)} %shard_map.84.refs_1_), channel_id=1, source_target_pairs={{0,16},{16,0},{32,48},{48,32},{64,80},{80,64},{96,112},{112,96},{1... | collective-permute-start | bytes 1191944 | tf_op jit(solution)/shard_map/ppermute | solution.py:36
  50.9 11.7 %collective-permute-start.8 = (bf16[1,64,1536]{2,1,0:T(8,128)(2,1)S(1)}, bf16[1,64,1536]{2,1,0:T(8,128)(2,1)S(1)}, u32[]{:S(2)}, u32[]{:S(2)}) collective-permute-start(bf16[1,64,1536]{2,1,0:T(8,128)(2,1)S(1)} %slice.48), channel_id=1, source_target_pairs={{0,64},{16,464},{32,96},{48,496},{64,128},{80,16},{96,160},{112,48... | collective-permute-start | bytes 589832 | tf_op jit(solution)/shard_map/ppermute | solution.py:36
  54.6 8.0 %collective-permute-start.9 = (bf16[1,64,1536]{2,1,0:T(8,128)(2,1)S(1)}, bf16[1,64,1536]{2,1,0:T(8,128)(2,1)S(1)}, u32[]{:S(2)}, u32[]{:S(2)}) collective-permute-start(bf16[1,64,1536]{2,1,0:T(8,128)(2,1)S(1)} %slice.49), channel_id=1, source_target_pairs={{0,64},{16,464},{32,96},{48,496},{64,128},{80,16},{96,160},{112,48... | collective-permute-start | bytes 589832 | tf_op jit(solution)/shard_map/ppermute | solution.py:36
  58.9 31.2 %collective-permute-start.13 = (bf16[7,128,128]{2,1,0:T(8,128)(2,1)S(1)}, bf16[7,128,128]{2,1,0:T(8,128)(2,1)S(1)}, u32[]{:S(2)}, u32[]{:S(2)}) collective-permute-start(bf16[7,128,128]{2,1,0:T(8,128)(2,1)S(1)} %shard_map.88), channel_id=1, source_target_pairs={{0,32},{16,48},{32,0},{48,16},{64,96},{80,112},{96,64},{112,80},{1... | collective-permute-start | bytes 688136 | tf_op jit(solution)/shard_map/ppermute | solution.py:36
  64.7 25.4 %collective-permute-start.15 = (bf16[8,128,128]{2,1,0:T(8,128)(2,1)S(1)}, bf16[8,128,128]{2,1,0:T(8,128)(2,1)S(1)}, u32[]{:S(2)}, u32[]{:S(2)}) collective-permute-start(bf16[8,128,128]{2,1,0:T(8,128)(2,1)S(1)} %shard_map.85.refs_4_), channel_id=1, source_target_pairs={{0,48},{16,32},{32,16},{48,0},{64,112},{80,96},{96,80},{112,64},{1... | collective-permute-start | bytes 786440 | tf_op jit(solution)/shard_map/ppermute | solution.py:36
  75.5 14.6 %collective-permute-start.12 = (bf16[8,128,128]{2,1,0:T(8,128)(2,1)S(1)}, bf16[8,128,128]{2,1,0:T(8,128)(2,1)S(1)}, u32[]{:S(2)}, u32[]{:S(2)}) collective-permute-start(bf16[8,128,128]{2,1,0:T(8,128)(2,1)S(1)} %get-tuple-element.12), channel_id=1, source_target_pairs={{0,16},{16,0},{32,48},{48,32},{64,80},{80,64},{96,112},{112,96},{1... | collective-permute-start | bytes 786440 | tf_op jit(solution)/shard_map/ppermute | solution.py:36
  77.5 12.6 %collective-permute-start.14 = (bf16[1,128,128]{2,1,0:T(8,128)(2,1)S(1)}, bf16[1,128,128]{2,1,0:T(8,128)(2,1)S(1)}, u32[]{:S(2)}, u32[]{:S(2)}) collective-permute-start(bf16[1,128,128]{2,1,0:T(8,128)(2,1)S(1)} %shard_map.86.refs_13_), channel_id=1, source_target_pairs={{0,32},{16,48},{32,0},{48,16},{64,96},{80,112},{96,64},{112,80},{1... | collective-permute-start | bytes 98312 | tf_op jit(solution)/shard_map/ppermute | solution.py:36
